TPU v7x, 32 devices: a whole 2x2x4 slice. The times are simulated.
32 devices in a mesh: parts: 2 (over y), lat: 8 (over z, x), sub: 2 (over core).
Axes of the slice: x: 2, y: 2, z: 4, core: 2. Of those that a mesh axis runs over, the one named last changes fastest.
Arguments:
- residuals: bfloat16 [64, 5120], P(('parts', 'lat', 'sub')), parts along dimension 0, may hold values from -6 to 6
- enc_weight: bfloat16 [5120, 8192], P(None, ('parts', 'lat', 'sub')), parts along dimension 1, may hold values from -0.078125 to 0.078125
- enc_bias: float32 [8192], P(('parts', 'lat', 'sub')), parts along dimension 0, may hold values from -0.5 to 0.5
- dec_weight: bfloat16 [8192, 5120], P(('parts', 'lat', 'sub')), parts along dimension 0, may hold values from -0.1875 to 0.1875
- dec_bias: float32 [10240], P('parts'), parts along dimension 0, may hold values from -3 to 3
Outputs:
- reconstruction: bfloat16 [64, 5120], P(('parts', 'lat', 'sub')), parts along dimension 0
- loss_value: float32 [2], P('parts'), parts along dimension 0
- grad_enc: bfloat16 [5120, 8192], P(None, ('parts', 'lat', 'sub')), parts along dimension 1
- grad_enc_bias: float32 [8192], P(('parts', 'lat', 'sub')), parts along dimension 0
- grad_dec: bfloat16 [8192, 5120], P(('parts', 'lat', 'sub')), parts along dimension 0
- grad_dec_bias: float32 [10240], P('parts'), parts along dimension 0
There are 2 independent parts, one for each index of `parts`. A program takes and returns all parts, laid end to end along the dimension named above; each array names one. Nothing has to cross between parts.
All inputs are finite; a program needn't handle non-finite values.
Results may differ from a plain program's by a relative error of at most 0.00155.
The roundings to bfloat16 on the way count: a program that leaves them out, or rounds other values in their place, can miss the bound.
Values may be sent and summed in bfloat16 or wider, within the bound.
No kernel may reach another device: no remote copies, remote signals or barrier semaphores. Data moves between devices by JAX's collectives and lax.ppermute only.
A program may use at most 128 MiB of HBM per device.

v0:
```python
import jax
import jax.numpy as jnp
from jax import lax
from jax.sharding import PartitionSpec as P

PENALTY = 0.2


def local(residuals, enc_weight, enc_bias, dec_weight, dec_bias):
    own_rows = residuals.shape[0]
    width = residuals.shape[1]
    row_count = own_rows * lax.axis_size("lat") * lax.axis_size("sub")
    gathered = lax.all_gather(residuals, ("lat", "sub"), axis=0, tiled=True)
    centered = (gathered.astype(jnp.float32) - dec_bias).astype(jnp.bfloat16)
    preact = jnp.dot(centered, enc_weight, preferred_element_type=jnp.float32) + enc_bias
    active = jnp.maximum(preact, 0.0)
    codes = active * active
    codes_bf = codes.astype(jnp.bfloat16)
    summed = lax.psum_scatter(
        jnp.dot(codes_bf, dec_weight, preferred_element_type=jnp.float32),
        ("lat", "sub"),
        scatter_dimension=0,
        tiled=True,
    )
    recon_f = summed + dec_bias
    error_rows = recon_f - residuals.astype(jnp.float32)
    sq_total = jnp.sum(error_rows * error_rows)
    code_total = jnp.sum(codes)
    resid_grad = 2.0 / row_count * error_rows
    resid_bf = resid_grad.astype(jnp.bfloat16)
    own_bias = jnp.sum(resid_grad, axis=0)
    sq_all, code_all = lax.psum((sq_total, code_total), ("lat", "sub"))
    piece = lax.all_gather(resid_bf, ("lat", "sub"), axis=0, tiled=True)
    dec_total = lax.dot_general(
        codes_bf, piece, (((0,), (0,)), ((), ())), preferred_element_type=jnp.float32
    )
    back_piece = lax.dot_general(
        piece, dec_weight, (((1,), (1,)), ((), ())), preferred_element_type=jnp.float32
    )
    back_codes = back_piece
    dec_total, back_codes = (dec_total, back_codes)
    code_grad = 2.0 * active * (back_codes + PENALTY / row_count)
    grad_enc = lax.dot_general(
        centered,
        code_grad.astype(jnp.bfloat16),
        (((0,), (0,)), ((), ())),
        preferred_element_type=jnp.float32,
    ).astype(jnp.bfloat16)
    grad_enc_bias = jnp.sum(code_grad, axis=0)
    bias_terms = own_bias - jnp.dot(
        enc_weight.astype(jnp.float32), grad_enc_bias, precision=lax.Precision.HIGHEST
    )
    grad_dec_bias = lax.psum(bias_terms, ("lat", "sub"))
    total = (sq_all + PENALTY * code_all) / row_count
    loss_value = jnp.reshape(total / width, (1,))
    return (
        recon_f.astype(jnp.bfloat16),
        loss_value,
        grad_enc,
        grad_enc_bias,
        dec_total.astype(jnp.bfloat16),
        grad_dec_bias,
    )


def solution(mesh):
    placed = (
        P(("parts", "lat", "sub"), None),
        P(None, ("parts", "lat", "sub")),
        P(("parts", "lat", "sub")),
        P(("parts", "lat", "sub"), None),
        P("parts"),
    )
    return jax.shard_map(
        local,
        mesh=mesh,
        in_specs=placed,
        out_specs=(
            P(("parts", "lat", "sub"), None),
            P("parts"),
            P(None, ("parts", "lat", "sub")),
            P(("parts", "lat", "sub")),
            P(("parts", "lat", "sub"), None),
            P("parts"),
        ),
        check_vma=False,
    )
```

profile of v0, /device:TPU:0, one launch (start us, length us, event | category | flops | bytes accessed | tf_op | source)
XLA Modules:
  0.0 229.5 jit_solution(3729031945419980067)
XLA Ops:
  7.2 0.0 copy-start
  7.2 0.0 all-reduce.4.cloned.1.call-start
  7.2 25.8 %all-gather = bf16[16,2,5120]{2,1,0:T(2,128)(2,1)} all-gather(bf16[1,2,5120]{2,1,0:T(2,128)(2,1)} %bitcast.16), channel_id=1, replica_groups=mesh['parts'=2,'lat'=8,'sub'=2] {'lat','sub'}, dimensions={0}, use_global_device_ids=true | all-gather | bytes 348160 | tf_op jit(solution)/shard_map/all_gather | solution.py:13
  33.1 1.1 reshape.22
  34.1 2.9 %multiply_reduce_fusion.2 = (f32[]{:T(128)}, f32[32,256]{1,0:T(8,128)S(1)}) fusion(f32[256]{0:T(256)} %param.7, bf16[5120,256]{1,0:T(8,128)(2,1)} %param.6, f32[32,5120]{1,0:T(8,128)S(1)} %reshape.22, f32[5120]{0:T(1024)} %param.9), kind=kOutput, calls=%fused_computation.12 | convolution fusion | flops 84246528 | bytes 3331076 | tf_op jit(solution)/shard_map/dot_general | solution.py:15
  37.0 0.0 copy-start.6
  37.0 0.0 copy-start.3
  37.0 0.0 copy-start.4
  37.0 0.0 copy-done
  37.0 1.4 fusion.5
  38.4 0.0 all-reduce.4.cloned.1.call-update
  38.4 0.0 copy-done.6
  38.4 0.6 dynamic-slice
  39.7 87.2 %all-reduce.4.cloned.1.call-done = f32[32,5120]{1,0:T(8,128)} async-done(((f32[32,5120]{1,0:T(8,128)}), f32[32,5120]{1,0:T(8,128)}) %all-reduce.4.cloned.1.call-update) | async-done | bytes 655376
  126.9 0.0 copy-done.3
  126.9 0.0 copy-done.4
  126.9 1.6 fusion.3
  128.5 22.5 %all-gather.1 = bf16[16,2,5120]{2,1,0:T(2,128)(2,1)} all-gather(bf16[1,2,5120]{2,1,0:T(2,128)(2,1)S(1)} %get-tuple-element.11), channel_id=1, replica_groups=mesh['parts'=2,'lat'=8,'sub'=2] {'lat','sub'}, dimensions={0}, use_global_device_ids=true | all-gather | bytes 348160 | tf_op jit(solution)/shard_map/all_gather | solution.py:33
  151.0 1.8 reshape.21
  152.8 0.0 copy-start.2
  152.8 0.0 copy-start.1
  152.8 2.0 fusion.6
  154.8 0.0 copy-done.2
  154.8 0.0 copy-start.5
  154.8 2.4 %convolution_convert_fusion = bf16[256,5120]{1,0:T(8,128)(2,1)} fusion(bf16[32,5120]{1,0:T(8,128)(2,1)S(1)} %copy-done.2, f32[32,256]{1,0:T(8,128)S(1)} %get-tuple-element.15), kind=kOutput, calls=%fused_computation | convolution fusion | flops 85213184 | bytes 2981888 | tf_op jit(solution)/shard_map/dot_general | solution.py:34
  157.2 0.7 multiply_reduce_fusion.1
  157.9 0.0 copy-done.1
  157.9 2.1 fusion.7
  160.1 0.0 copy-done.5
  160.1 2.4 %convolution_convert_fusion.1 = bf16[5120,256]{1,0:T(8,128)(2,1)} fusion(f32[32,5120]{1,0:T(8,128)S(1)} %reshape.22, f32[5120]{0:T(1024)S(1)} %copy-done.3, bf16[32,256]{1,0:T(8,128)(2,1)S(1)} %get-tuple-element.17), kind=kOutput, calls=%fused_computation.1 | convolution fusion | flops 85524480 | bytes 3313664 | tf_op jit(solution)/shard_map/dot_general | solution.py:43
  162.5 57.8 %all-reduce.1 = (f32[]{:T(128)}, f32[]{:T(128)}, f32[5120]{0:T(1024)}) all-reduce(f32[]{:T(128)} %get-tuple-element.7, f32[]{:T(128)} %get-tuple-element.14, f32[5120]{0:T(1024)S(1)} %sub.17), channel_id=1, replica_groups=mesh['parts'=2,'lat'=8,'sub'=2] {'lat','sub'}, use_global_device_ids=true, to_apply=%region_2.0 | all-reduce | flops 5122 | bytes 40976 | tf_op jit(solution)/shard_map/psum | solution.py:32
  (1 shorter events, 0.0 us)
Async XLA Ops:
  7.2 29.8 %copy-start = (bf16[256,5120]{1,0:T(8,128)(2,1)S(1)}, bf16[256,5120]{1,0:T(8,128)(2,1)}, u32[]{:S(2)}) copy-start(bf16[256,5120]{1,0:T(8,128)(2,1)} %param.8) | copy-start | bytes 7864324
  7.2 119.7 %all-reduce.4.cloned.1.call-start = ((), (), s32[]{:S(2)}) async-start(), calls=%async_computation | async-start | bytes 1310720
  37.0 1.4 copy-start.6
  37.0 89.9 %copy-start.3 = (f32[5120]{0:T(1024)S(1)}, f32[5120]{0:T(1024)}, u32[]{:S(2)}) copy-start(f32[5120]{0:T(1024)} %param.9) | copy-start | bytes 61444
  37.0 89.9 %copy-start.4 = (bf16[2,5120]{1,0:T(2,128)(2,1)S(1)}, bf16[2,5120]{1,0:T(2,128)(2,1)}, u32[]{:S(2)}) copy-start(bf16[2,5120]{1,0:T(2,128)(2,1)} %param.5) | copy-start | bytes 61444
  152.8 2.0 copy-start.2
  152.8 5.2 %copy-start.1 = (bf16[5120,256]{1,0:T(8,128)(2,1)S(1)}, bf16[5120,256]{1,0:T(8,128)(2,1)}, u32[]{:S(2)}) copy-start(bf16[5120,256]{1,0:T(8,128)(2,1)} %param.6) | copy-start | bytes 7864324
  154.8 5.2 %copy-start.5 = (f32[256]{0:T(256)}, f32[256]{0:T(256)S(1)}, u32[]{:S(2)}) copy-start(f32[256]{0:T(256)S(1)} %get-tuple-element.16) | copy-start | bytes 3076
Sparse Core Ops, SparseCore 0:
  38.5 88.2 all-reduce.3
where the time goes:
time: 230 us; the launch traced here: 229 us
  blocking collectives  106 us (46%)
  waiting for transfers between devices  87.2 us (38%)
  between operations  17.1 us (7%)
  matrix products  13.2 us (6%)
  local copies, waits for them, and re-layouts  3.5 us (2%)
  other arithmetic  2.31 us (1%)
    unnamed x2, waiting for transfers between devices  87.2 us
    psum x1, blocking collectives, local(): sq_all, code_all = lax.psum((sq_total, code_total), ('lat', 'sub'))  57.8 us
    all_gather x1, blocking collectives, local(): gathered = lax.all_gather(residuals, ('lat', 'sub'), axis=0, tiled=True)  25.8 us
    all_gather x1, blocking collectives, local(): piece = lax.all_gather(resid_bf, ('lat', 'sub'), axis=0, tiled=True)  22.5 us
  transfers between devices with their start and end apart: 1, of which 1 were waited for; matrix products, arithmetic and copies ran while one was open for 0% of the time, Pallas kernels for 0%

commit v1 on v0

v1 whole, which is shorter than its diff:
```python
import jax
import jax.numpy as jnp
from jax import lax
from jax.sharding import PartitionSpec as P

PENALTY = 0.2
CORES = 0


def swap(values, mask):
    if mask == CORES:
        return lax.ppermute(values, "sub", [(i, i ^ 1) for i in range(2)])
    return lax.ppermute(values, "lat", [(i, i ^ mask) for i in range(lax.axis_size("lat"))])


def gather(rows, masks):
    for mask in masks:
        rows = jnp.concatenate([rows, swap(rows, mask)], axis=0)
    return rows


def halve(rows, masks):
    for mask in masks:
        half = rows.shape[0] // 2
        rows = rows[:half] + swap(rows[half:], mask)
    return rows


def local(residuals, enc_weight, enc_bias, dec_weight, dec_bias):
    own_rows, width = residuals.shape
    lat = lax.axis_size("lat")
    row_count = own_rows * lat * lax.axis_size("sub")
    bits = [1 << b for b in range(lat.bit_length() - 1)]
    far, near = bits[-1], bits[:-1]

    paired = gather(residuals, [far])
    gathered = gather(paired, near[::-1] + [CORES])
    centered = (gathered.astype(jnp.float32) - dec_bias).astype(jnp.bfloat16)
    preact = jnp.dot(centered, enc_weight, preferred_element_type=jnp.float32) + enc_bias
    active = jnp.maximum(preact, 0.0)
    codes = active * active
    codes_bf = codes.astype(jnp.bfloat16)
    code_total = jnp.sum(codes)

    partial = jnp.dot(codes_bf, dec_weight, preferred_element_type=jnp.float32)
    summed = halve(partial, [CORES] + near)
    other = swap(summed, far)
    summed = summed + jnp.concatenate([other[own_rows:], other[:own_rows]], axis=0)
    recon_f = summed + dec_bias
    error_rows = recon_f - paired.astype(jnp.float32)
    resid_grad = 2.0 / row_count * error_rows
    resid_bf = resid_grad.astype(jnp.bfloat16)
    own_error = error_rows[:own_rows]
    sq_total = jnp.sum(own_error * own_error)
    own_bias = jnp.sum(resid_grad[:own_rows], axis=0)

    resid_all = gather(resid_bf, near[::-1] + [CORES])
    back_codes = lax.dot_general(
        resid_all, dec_weight, (((1,), (1,)), ((), ())), preferred_element_type=jnp.float32
    )
    code_grad = 2.0 * active * (back_codes + PENALTY / row_count)
    grad_enc_bias = jnp.sum(code_grad, axis=0)
    bias_terms = own_bias - jnp.dot(
        enc_weight.astype(jnp.float32), grad_enc_bias, precision=lax.Precision.HIGHEST
    )
    scalars = (sq_total + PENALTY * code_total) / row_count
    terms = jnp.concatenate([bias_terms, jnp.broadcast_to(scalars, (128,))])
    for mask in [CORES] + bits:
        terms = terms + swap(terms, mask)
    grad_dec = lax.dot_general(
        codes_bf, resid_all, (((0,), (0,)), ((), ())), preferred_element_type=jnp.float32
    ).astype(jnp.bfloat16)
    grad_enc = lax.dot_general(
        centered,
        code_grad.astype(jnp.bfloat16),
        (((0,), (0,)), ((), ())),
        preferred_element_type=jnp.float32,
    ).astype(jnp.bfloat16)
    return (
        recon_f[:own_rows].astype(jnp.bfloat16),
        terms[width : width + 1] / width,
        grad_enc,
        grad_enc_bias,
        grad_dec,
        terms[:width],
    )


def solution(mesh):
    placed = (
        P(("parts", "lat", "sub"), None),
        P(None, ("parts", "lat", "sub")),
        P(("parts", "lat", "sub")),
        P(("parts", "lat", "sub"), None),
        P("parts"),
    )
    return jax.shard_map(
        local,
        mesh=mesh,
        in_specs=placed,
        out_specs=(
            P(("parts", "lat", "sub"), None),
            P("parts"),
            P(None, ("parts", "lat", "sub")),
            P(("parts", "lat", "sub")),
            P(("parts", "lat", "sub"), None),
            P("parts"),
        ),
        check_vma=False,
    )
```

time: 230 us -> 75 us (0.33)
  blocking collectives: 106 us -> 0 us
  waiting for transfers between devices: 87.2 us -> 26.1 us
  starting transfers between devices: 0.04 us -> 26 us
  between operations: 17.1 us -> 3.87 us
    unnamed x2 -> x0, waiting for transfers between devices: 87.2 us -> none
    psum x1 -> x0, blocking collectives: 57.8 us -> none  [local(): sq_all, code_all = lax.psum((sq_total, code_total), ('lat', 'sub'))]
    all_gather x2 -> x0, blocking collectives: 48.3 us -> none  [the longest x1 25.8 us: local(): gathered = lax.all_gather(residuals, ('lat', 'sub'), axis=0, tiled=True)]
    ppermute x0 -> x15, waiting for transfers between devices: none -> 26.1 us  [the longest x11 22.2 us: swap(): lax.ppermute(values, 'lat', [(i, i ^ mask) for i in range(lax.axis_size('...]
    ppermute x0 -> x15, starting transfers between devices: none -> 26 us  [the longest x11 25.1 us: swap(): lax.ppermute(values, 'lat', [(i, i ^ mask) for i in range(lax.axis_size('...]
    concatenate x0 -> x5, other arithmetic: none -> 3.19 us  [gather(): rows = jnp.concatenate([rows, swap(rows, mask)], axis=0)]
  transfers between devices with their start and end apart: 1 -> 15, of which waited for: 1 -> 13; matrix products, arithmetic and copies ran while one was open for 0% -> 8% of each run, Pallas kernels for 0% -> 0%
where the time goes in v1:
time: 75 us; the launch traced here: 74.6 us
  waiting for transfers between devices  26.1 us (35%)
  starting transfers between devices  26 us (35%)
  matrix products  11.1 us (15%)
  other arithmetic  4.13 us (6%)
  between operations  3.87 us (5%)
  local copies, waits for them, and re-layouts  3.31 us (4%)
    ppermute x11, starting transfers between devices, swap(): lax.ppermute(values, 'lat', [(i, i ^ mask) for i in range(lax.axis_size('...  25.1 us
    ppermute x11, waiting for transfers between devices, swap(): lax.ppermute(values, 'lat', [(i, i ^ mask) for i in range(lax.axis_size('...  22.2 us
    ppermute x4, waiting for transfers between devices, swap(): return lax.ppermute(values, 'sub', [(i, i ^ 1) for i in range(2)])  3.96 us
    concatenate x5, other arithmetic, gather(): rows = jnp.concatenate([rows, swap(rows, mask)], axis=0)  3.19 us
    dot_general x1, matrix products, local(): jnp.dot(centered, enc_weight, preferred_element_type=jnp.float32) + enc_bias  2.85 us
    dot_general x1, matrix products, local(): lax.dot_general(centered, code_grad.astype(jnp.bfloat16), (((0,), (0,)),...  2.38 us
    dot_general x1, matrix products, local(): lax.dot_general(codes_bf, resid_all, (((0,), (0,)), ((), ())), preferred_...  2.36 us
    dot_general x1, matrix products, local(): jnp.dot(enc_weight.astype(jnp.float32), grad_enc_bias, precision=lax.Prec...  2.12 us
  transfers between devices with their start and end apart: 15, of which 13 were waited for; matrix products, arithmetic and copies ran while one was open for 8% of the time, Pallas kernels for 0%

profile of v1, /device:TPU:0, one launch (start us, length us, event | category | flops | bytes accessed | tf_op | source)
XLA Modules:
  0.0 74.6 jit_solution(15165478831414739744)
XLA Ops:
  0.6 4.1 %collective-permute-start = (bf16[2,5120]{1,0:T(2,128)(2,1)}, bf16[2,5120]{1,0:T(2,128)(2,1)S(1)}, u32[]{:S(2)}, u32[]{:S(2)}) collective-permute-start(bf16[2,5120]{1,0:T(2,128)(2,1)} %param.5), channel_id=1, source_target_pairs={{0,8},{2,10},{4,12},{6,14},{8,0},{10,2},{12,4},{14,6},{1,9},{3,11}... | collective-permute-start | bytes 61448 | tf_op jit(solution)/shard_map/ppermute | solution.py:13
  4.7 2.0 %collective-permute-done = bf16[2,5120]{1,0:T(2,128)(2,1)S(1)} collective-permute-done((bf16[2,5120]{1,0:T(2,128)(2,1)}, bf16[2,5120]{1,0:T(2,128)(2,1)S(1)}, u32[]{:S(2)}, u32[]{:S(2)}) %collective-permute-start) | collective-permute-done | bytes 20512 | tf_op jit(solution)/shard_map/ppermute | solution.py:13
  6.7 0.8 %pad_maximum_fusion.7 = bf16[4,5120]{1,0:T(4,128)(2,1)S(1)} fusion(bf16[2,5120]{1,0:T(2,128)(2,1)S(1)} %collective-permute-done, bf16[2,5120]{1,0:T(2,128)(2,1)} %param.5), kind=kLoop, calls=%fused_computation.22 | loop fusion | flops 81920 | bytes 81920 | tf_op jit(solution)/shard_map/concatenate | solution.py:18
  7.5 2.0 %collective-permute-start.1 = (bf16[4,5120]{1,0:T(4,128)(2,1)S(1)}, bf16[4,5120]{1,0:T(4,128)(2,1)S(1)}, u32[]{:S(2)}, u32[]{:S(2)}) collective-permute-start(bf16[4,5120]{1,0:T(4,128)(2,1)S(1)} %pad_maximum_fusion.7), channel_id=1, source_target_pairs={{0,4},{2,6},{4,0},{6,2},{8,12},{10,14},{12,8},{14,10},{1,5},{3,7},... | collective-permute-start | bytes 122888 | tf_op jit(solution)/shard_map/ppermute | solution.py:13
  9.5 2.1 %collective-permute-done.1 = bf16[4,5120]{1,0:T(4,128)(2,1)S(1)} collective-permute-done((bf16[4,5120]{1,0:T(4,128)(2,1)S(1)}, bf16[4,5120]{1,0:T(4,128)(2,1)S(1)}, u32[]{:S(2)}, u32[]{:S(2)}) %collective-permute-start.1) | collective-permute-done | bytes 40992 | tf_op jit(solution)/shard_map/ppermute | solution.py:13
  11.6 0.8 %pad_maximum_fusion.3 = bf16[8,5120]{1,0:T(8,128)(2,1)S(1)} fusion(bf16[4,5120]{1,0:T(4,128)(2,1)S(1)} %collective-permute-done.1, bf16[2,5120]{1,0:T(2,128)(2,1)S(1)} %collective-permute-done, bf16[2,5120]{1,0:T(2,128)(2,1)} %param.5), kind=kLoop, calls=%fused_computation.13 | loop fusion | flops 245760 | bytes 163840 | tf_op jit(solution)/shard_map/concatenate | solution.py:18
  12.4 2.0 %collective-permute-start.2 = (bf16[8,5120]{1,0:T(8,128)(2,1)S(1)}, bf16[8,5120]{1,0:T(8,128)(2,1)S(1)}, u32[]{:S(2)}, u32[]{:S(2)}) collective-permute-start(bf16[8,5120]{1,0:T(8,128)(2,1)S(1)} %pad_maximum_fusion.3), channel_id=1, source_target_pairs={{0,2},{2,0},{4,6},{6,4},{8,10},{10,8},{12,14},{14,12},{1,3},{3,1},... | collective-permute-start | bytes 245768 | tf_op jit(solution)/shard_map/ppermute | solution.py:13
  14.4 2.5 %collective-permute-done.2 = bf16[8,5120]{1,0:T(8,128)(2,1)S(1)} collective-permute-done((bf16[8,5120]{1,0:T(8,128)(2,1)S(1)}, bf16[8,5120]{1,0:T(8,128)(2,1)S(1)}, u32[]{:S(2)}, u32[]{:S(2)}) %collective-permute-start.2) | collective-permute-done | bytes 81952 | tf_op jit(solution)/shard_map/ppermute | solution.py:13
  16.9 0.8 %pad_maximum_fusion.1 = bf16[16,5120]{1,0:T(8,128)(2,1)S(1)} fusion(bf16[8,5120]{1,0:T(8,128)(2,1)S(1)} %collective-permute-done.2, bf16[4,5120]{1,0:T(4,128)(2,1)S(1)} %collective-permute-done.1, bf16[2,5120]{1,0:T(2,128)(2,1)S(1)} %collective-permute-done, bf16[2,5120]{1,0:T(2,128)(2,1)} %param.5), kind=kLoop, calls=%fused_computation.10 | loop fusion | flops 655360 | bytes 327680 | tf_op jit(solution)/shard_map/concatenate | solution.py:18
  17.8 1.4 %collective-permute-done.3 = bf16[16,5120]{1,0:T(8,128)(2,1)S(1)} collective-permute-done((bf16[16,5120]{1,0:T(8,128)(2,1)S(1)}, bf16[16,5120]{1,0:T(8,128)(2,1)S(1)}, u32[]{:S(2)}, u32[]{:S(2)}) %collective-permute-start.3) | collective-permute-done | bytes 163872 | tf_op jit(solution)/shard_map/ppermute | solution.py:12
  19.2 0.9 %concatenate.35 = bf16[32,5120]{1,0:T(8,128)(2,1)S(1)} concatenate(bf16[2,5120]{1,0:T(2,128)(2,1)} %param.5, bf16[2,5120]{1,0:T(2,128)(2,1)S(1)} %collective-permute-done, bf16[4,5120]{1,0:T(4,128)(2,1)S(1)} %collective-permute-done.1, bf16[8,5120]{1,0:T(8,128)(2,1)S(1)} %collective-permute-done.2, bf16[16,5120]{1,0:T(8,128)(2,1)S(1)} %collective-permute-done.3), dimensions={0} | concatenate | bytes 655360 | tf_op jit(solution)/shard_map/concatenate | solution.py:18
  20.1 2.8 %multiply_reduce_fusion = (f32[]{:T(128)}, f32[32,256]{1,0:T(8,128)S(1)}) fusion(f32[256]{0:T(256)} %param.7, bf16[5120,256]{1,0:T(8,128)(2,1)} %param.6, bf16[32,5120]{1,0:T(8,128)(2,1)S(1)} %concatenate.35, f32[5120]{0:T(1024)} %param.9), kind=kOutput, calls=%fused_computation.24 | convolution fusion | flops 84410368 | bytes 3003396 | tf_op jit(solution)/shard_map/dot_general | solution.py:39
  23.7 1.5 %collective-permute-done.4 = f32[16,5120]{1,0:T(8,128)S(1)} collective-permute-done((f32[16,5120]{1,0:T(8,128)S(1)}, f32[16,5120]{1,0:T(8,128)S(1)}, u32[]{:S(2)}, u32[]{:S(2)}) %collective-permute-start.4) | collective-permute-done | bytes 327712 | tf_op jit(solution)/shard_map/ppermute | solution.py:12
  25.3 2.0 %collective-permute-start.5 = (f32[8,5120]{1,0:T(8,128)S(1)}, f32[8,5120]{1,0:T(8,128)S(1)}, u32[]{:S(2)}, u32[]{:S(2)}) collective-permute-start(f32[8,5120]{1,0:T(8,128)S(1)} %slice.56), channel_id=1, source_target_pairs={{0,2},{2,0},{4,6},{6,4},{8,10},{10,8},{12,14},{14,12},{1,3},{3,1},... | collective-permute-start | bytes 491528 | tf_op jit(solution)/shard_map/ppermute | solution.py:13
  27.3 4.5 %collective-permute-done.5 = f32[8,5120]{1,0:T(8,128)S(1)} collective-permute-done((f32[8,5120]{1,0:T(8,128)S(1)}, f32[8,5120]{1,0:T(8,128)S(1)}, u32[]{:S(2)}, u32[]{:S(2)}) %collective-permute-start.5) | collective-permute-done | bytes 163872 | tf_op jit(solution)/shard_map/ppermute | solution.py:13
  31.8 1.8 %collective-permute-start.6 = (f32[4,5120]{1,0:T(4,128)S(1)}, f32[4,5120]{1,0:T(4,128)S(1)}, u32[]{:S(2)}, u32[]{:S(2)}) collective-permute-start(f32[4,5120]{1,0:T(4,128)S(1)} %slice.58), channel_id=1, source_target_pairs={{0,4},{2,6},{4,0},{6,2},{8,12},{10,14},{12,8},{14,10},{1,5},{3,7},... | collective-permute-start | bytes 245768 | tf_op jit(solution)/shard_map/ppermute | solution.py:13
  33.6 2.7 %collective-permute-done.6 = f32[4,5120]{1,0:T(4,128)S(1)} collective-permute-done((f32[4,5120]{1,0:T(4,128)S(1)}, f32[4,5120]{1,0:T(4,128)S(1)}, u32[]{:S(2)}, u32[]{:S(2)}) %collective-permute-start.6) | collective-permute-done | bytes 81952 | tf_op jit(solution)/shard_map/ppermute | solution.py:13
  36.4 2.8 %collective-permute-start.7 = (f32[4,5120]{1,0:T(4,128)S(1)}, f32[4,5120]{1,0:T(4,128)S(1)}, u32[]{:S(2)}, u32[]{:S(2)}) collective-permute-start(f32[4,5120]{1,0:T(4,128)S(1)} %slice_add_fusion.2), channel_id=1, source_target_pairs={{0,8},{2,10},{4,12},{6,14},{8,0},{10,2},{12,4},{14,6},{1,9},{3,11}... | collective-permute-start | bytes 245768 | tf_op jit(solution)/shard_map/ppermute | solution.py:13
  39.2 2.6 %collective-permute-done.7 = f32[4,5120]{1,0:T(4,128)S(1)} collective-permute-done((f32[4,5120]{1,0:T(4,128)S(1)}, f32[4,5120]{1,0:T(4,128)S(1)}, u32[]{:S(2)}, u32[]{:S(2)}) %collective-permute-start.7) | collective-permute-done | bytes 81952 | tf_op jit(solution)/shard_map/ppermute | solution.py:13
  41.9 1.8 %collective-permute-start.8 = (bf16[4,5120]{1,0:T(4,128)(2,1)S(1)}, bf16[4,5120]{1,0:T(4,128)(2,1)S(1)}, u32[]{:S(2)}, u32[]{:S(2)}) collective-permute-start(bf16[4,5120]{1,0:T(4,128)(2,1)S(1)} %get-tuple-element.6), channel_id=1, source_target_pairs={{0,4},{2,6},{4,0},{6,2},{8,12},{10,14},{12,8},{14,10},{1,5},{3,7},... | collective-permute-start | bytes 122888 | tf_op jit(solution)/shard_map/ppermute | solution.py:13
  44.4 1.6 %collective-permute-done.8 = bf16[4,5120]{1,0:T(4,128)(2,1)S(1)} collective-permute-done((bf16[4,5120]{1,0:T(4,128)(2,1)S(1)}, bf16[4,5120]{1,0:T(4,128)(2,1)S(1)}, u32[]{:S(2)}, u32[]{:S(2)}) %collective-permute-start.8) | collective-permute-done | bytes 40992 | tf_op jit(solution)/shard_map/ppermute | solution.py:13
  46.1 1.8 %collective-permute-start.9 = (bf16[8,5120]{1,0:T(8,128)(2,1)S(1)}, bf16[8,5120]{1,0:T(8,128)(2,1)S(1)}, u32[]{:S(2)}, u32[]{:S(2)}) collective-permute-start(bf16[8,5120]{1,0:T(8,128)(2,1)S(1)} %pad_maximum_fusion.4), channel_id=1, source_target_pairs={{0,2},{2,0},{4,6},{6,4},{8,10},{10,8},{12,14},{14,12},{1,3},{3,1},... | collective-permute-start | bytes 245768 | tf_op jit(solution)/shard_map/ppermute | solution.py:13
  47.9 2.7 %collective-permute-done.9 = bf16[8,5120]{1,0:T(8,128)(2,1)S(1)} collective-permute-done((bf16[8,5120]{1,0:T(8,128)(2,1)S(1)}, bf16[8,5120]{1,0:T(8,128)(2,1)S(1)}, u32[]{:S(2)}, u32[]{:S(2)}) %collective-permute-start.9) | collective-permute-done | bytes 81952 | tf_op jit(solution)/shard_map/ppermute | solution.py:13
  52.9 0.9 %fusion.11 = (f32[256]{0:T(256)S(1)}, bf16[32,256]{1,0:T(8,128)(2,1)S(1)}) fusion(bf16[256,5120]{1,0:T(8,128)(2,1)S(1)} %copy-done, bf16[16,5120]{1,0:T(8,128)(2,1)S(1)} %collective-permute-done.10, bf16[8,5120]{1,0:T(8,128)(2,1)S(1)} %collective-permute-done.9, bf16[4,5120]{1,0:T(4,128)(2,1)S(1)} %collective-permute-done.8, ...), kind=kOutput, calls=%fused_computation.33 | convolution fusion | flops 85237504 | bytes 2999296 | tf_op jit(solution)/shard_map/dot_general | solution.py:58
  54.3 2.1 %fusion.12 = f32[1,5120]{1,0:T(1,128)S(1)} fusion(f32[256,1]{0,1:T(1,128)S(1)} %bitcast.9, bf16[5120,256]{1,0:T(8,128)(2,1)S(1)} %copy-done.1), kind=kOutput, calls=%fused_computation.34 | convolution fusion | flops 15728640 | bytes 2642944 | tf_op jit(solution)/shard_map/dot_general | solution.py:63
  57.1 0.8 %collective-permute-done.11 = f32[5248]{0:T(1024)S(1)} collective-permute-done((f32[5248]{0:T(1024)S(1)}, f32[5248]{0:T(1024)S(1)}, u32[]{:S(2)}, u32[]{:S(2)}) %collective-permute-start.11) | collective-permute-done | bytes 21024 | tf_op jit(solution)/shard_map/ppermute | solution.py:12
  57.9 1.8 %collective-permute-start.12 = (f32[5248]{0:T(1024)S(1)}, f32[5248]{0:T(1024)S(1)}, u32[]{:S(2)}, u32[]{:S(2)}) collective-permute-start(f32[5248]{0:T(1024)S(1)} %pad_add_fusion), channel_id=1, source_target_pairs={{0,2},{2,0},{4,6},{6,4},{8,10},{10,8},{12,14},{14,12},{1,3},{3,1},... | collective-permute-start | bytes 62984 | tf_op jit(solution)/shard_map/ppermute | solution.py:13
  60.3 1.5 %collective-permute-done.12 = f32[5248]{0:T(1024)S(1)} collective-permute-done((f32[5248]{0:T(1024)S(1)}, f32[5248]{0:T(1024)S(1)}, u32[]{:S(2)}, u32[]{:S(2)}) %collective-permute-start.12) | collective-permute-done | bytes 21024 | tf_op jit(solution)/shard_map/ppermute | solution.py:13
  61.7 1.7 %collective-permute-start.13 = (f32[5248]{0:T(1024)S(1)}, f32[5248]{0:T(1024)S(1)}, u32[]{:S(2)}, u32[]{:S(2)}) collective-permute-start(f32[5248]{0:T(1024)S(1)} %add.63), channel_id=1, source_target_pairs={{0,4},{2,6},{4,0},{6,2},{8,12},{10,14},{12,8},{14,10},{1,5},{3,7},... | collective-permute-start | bytes 62984 | tf_op jit(solution)/shard_map/ppermute | solution.py:13
  63.5 2.4 %convolution_convert_fusion.1 = bf16[5120,256]{1,0:T(8,128)(2,1)} fusion(bf16[32,5120]{1,0:T(8,128)(2,1)S(1)} %concatenate.35, f32[5120]{0:T(1024)S(1)} %copy-done.3, bf16[32,256]{1,0:T(8,128)(2,1)S(1)} %get-tuple-element.12), kind=kOutput, calls=%fused_computation.1 | convolution fusion | flops 85688320 | bytes 2985984 | tf_op jit(solution)/shard_map/dot_general | solution.py:73
  65.9 3.4 %collective-permute-start.14 = (f32[5248]{0:T(1024)S(1)}, f32[5248]{0:T(1024)S(1)}, u32[]{:S(2)}, u32[]{:S(2)}) collective-permute-start(f32[5248]{0:T(1024)S(1)} %add.64), channel_id=1, source_target_pairs={{0,8},{2,10},{4,12},{6,14},{8,0},{10,2},{12,4},{14,6},{1,9},{3,11}... | collective-permute-start | bytes 62984 | tf_op jit(solution)/shard_map/ppermute | solution.py:13
  69.3 2.4 %convolution_convert_fusion = bf16[256,5120]{1,0:T(8,128)(2,1)} fusion(bf16[16,5120]{1,0:T(8,128)(2,1)S(1)} %collective-permute-done.10, bf16[8,5120]{1,0:T(8,128)(2,1)S(1)} %collective-permute-done.9, bf16[4,5120]{1,0:T(4,128)(2,1)S(1)} %collective-permute-done.8, bf16[4,5120]{1,0:T(4,128)(2,1)S(1)} %get-tuple-element.6, f32[32,256]{1,0:T(8,128)S(1)} %get-tuple-element.14), kind=kOutput, calls=%fused_computation | convolution fusion | flops 86523904 | bytes 2981888 | tf_op jit(solution)/shard_map/dot_general | solution.py:70
  (40 shorter events, 5.8 us)
Async XLA Ops:
  0.6 22.3 %copy-start = (bf16[256,5120]{1,0:T(8,128)(2,1)S(1)}, bf16[256,5120]{1,0:T(8,128)(2,1)}, u32[]{:S(2)}) copy-start(bf16[256,5120]{1,0:T(8,128)(2,1)} %param.8) | copy-start | bytes 7864324
  0.6 6.1 %collective-permute-start = (bf16[2,5120]{1,0:T(2,128)(2,1)}, bf16[2,5120]{1,0:T(2,128)(2,1)S(1)}, u32[]{:S(2)}, u32[]{:S(2)}) collective-permute-start(bf16[2,5120]{1,0:T(2,128)(2,1)} %param.5), channel_id=1, source_target_pairs={{0,8},{2,10},{4,12},{6,14},{8,0},{10,2},{12,4},{14,6},{1,9},{3,11}... | collective-permute-start | bytes 61448 | tf_op jit(solution)/shard_map/ppermute | solution.py:13
  7.5 4.1 %collective-permute-start.1 = (bf16[4,5120]{1,0:T(4,128)(2,1)S(1)}, bf16[4,5120]{1,0:T(4,128)(2,1)S(1)}, u32[]{:S(2)}, u32[]{:S(2)}) collective-permute-start(bf16[4,5120]{1,0:T(4,128)(2,1)S(1)} %pad_maximum_fusion.7), channel_id=1, source_target_pairs={{0,4},{2,6},{4,0},{6,2},{8,12},{10,14},{12,8},{14,10},{1,5},{3,7},... | collective-permute-start | bytes 122888 | tf_op jit(solution)/shard_map/ppermute | solution.py:13
  12.4 4.5 %collective-permute-start.2 = (bf16[8,5120]{1,0:T(8,128)(2,1)S(1)}, bf16[8,5120]{1,0:T(8,128)(2,1)S(1)}, u32[]{:S(2)}, u32[]{:S(2)}) collective-permute-start(bf16[8,5120]{1,0:T(8,128)(2,1)S(1)} %pad_maximum_fusion.3), channel_id=1, source_target_pairs={{0,2},{2,0},{4,6},{6,4},{8,10},{10,8},{12,14},{14,12},{1,3},{3,1},... | collective-permute-start | bytes 245768 | tf_op jit(solution)/shard_map/ppermute | solution.py:13
  17.7 1.5 %collective-permute-start.3 = (bf16[16,5120]{1,0:T(8,128)(2,1)S(1)}, bf16[16,5120]{1,0:T(8,128)(2,1)S(1)}, u32[]{:S(2)}, u32[]{:S(2)}) collective-permute-start(bf16[16,5120]{1,0:T(8,128)(2,1)S(1)} %pad_maximum_fusion.1), channel_id=1, source_target_pairs={{0,1},{1,0},{2,3},{3,2},{4,5},{5,4},{6,7},{7,6},{8,9},{9,8},{10,11... | collective-permute-start | bytes 491528 | tf_op jit(solution)/shard_map/ppermute | solution.py:12
  22.9 18.9 %copy-start.2 = (bf16[2,5120]{1,0:T(2,128)(2,1)S(1)}, bf16[2,5120]{1,0:T(2,128)(2,1)}, u32[]{:S(2)}) copy-start(bf16[2,5120]{1,0:T(2,128)(2,1)} %param.5) | copy-start | bytes 61444
  22.9 18.9 %copy-start.3 = (f32[5120]{0:T(1024)S(1)}, f32[5120]{0:T(1024)}, u32[]{:S(2)}) copy-start(f32[5120]{0:T(1024)} %param.9) | copy-start | bytes 61444
  23.5 1.7 %collective-permute-start.4 = (f32[16,5120]{1,0:T(8,128)S(1)}, f32[16,5120]{1,0:T(8,128)S(1)}, u32[]{:S(2)}, u32[]{:S(2)}) collective-permute-start(f32[16,5120]{1,0:T(8,128)S(1)} %slice.54), channel_id=1, source_target_pairs={{0,1},{1,0},{2,3},{3,2},{4,5},{5,4},{6,7},{7,6},{8,9},{9,8},{10,11... | collective-permute-start | bytes 983048 | tf_op jit(solution)/shard_map/ppermute | solution.py:12
  25.3 6.5 %collective-permute-start.5 = (f32[8,5120]{1,0:T(8,128)S(1)}, f32[8,5120]{1,0:T(8,128)S(1)}, u32[]{:S(2)}, u32[]{:S(2)}) collective-permute-start(f32[8,5120]{1,0:T(8,128)S(1)} %slice.56), channel_id=1, source_target_pairs={{0,2},{2,0},{4,6},{6,4},{8,10},{10,8},{12,14},{14,12},{1,3},{3,1},... | collective-permute-start | bytes 491528 | tf_op jit(solution)/shard_map/ppermute | solution.py:13
  31.8 4.5 %collective-permute-start.6 = (f32[4,5120]{1,0:T(4,128)S(1)}, f32[4,5120]{1,0:T(4,128)S(1)}, u32[]{:S(2)}, u32[]{:S(2)}) collective-permute-start(f32[4,5120]{1,0:T(4,128)S(1)} %slice.58), channel_id=1, source_target_pairs={{0,4},{2,6},{4,0},{6,2},{8,12},{10,14},{12,8},{14,10},{1,5},{3,7},... | collective-permute-start | bytes 245768 | tf_op jit(solution)/shard_map/ppermute | solution.py:13
  36.4 5.4 %collective-permute-start.7 = (f32[4,5120]{1,0:T(4,128)S(1)}, f32[4,5120]{1,0:T(4,128)S(1)}, u32[]{:S(2)}, u32[]{:S(2)}) collective-permute-start(f32[4,5120]{1,0:T(4,128)S(1)} %slice_add_fusion.2), channel_id=1, source_target_pairs={{0,8},{2,10},{4,12},{6,14},{8,0},{10,2},{12,4},{14,6},{1,9},{3,11}... | collective-permute-start | bytes 245768 | tf_op jit(solution)/shard_map/ppermute | solution.py:13
  41.9 4.1 %collective-permute-start.8 = (bf16[4,5120]{1,0:T(4,128)(2,1)S(1)}, bf16[4,5120]{1,0:T(4,128)(2,1)S(1)}, u32[]{:S(2)}, u32[]{:S(2)}) collective-permute-start(bf16[4,5120]{1,0:T(4,128)(2,1)S(1)} %get-tuple-element.6), channel_id=1, source_target_pairs={{0,4},{2,6},{4,0},{6,2},{8,12},{10,14},{12,8},{14,10},{1,5},{3,7},... | collective-permute-start | bytes 122888 | tf_op jit(solution)/shard_map/ppermute | solution.py:13
  46.1 4.5 %collective-permute-start.9 = (bf16[8,5120]{1,0:T(8,128)(2,1)S(1)}, bf16[8,5120]{1,0:T(8,128)(2,1)S(1)}, u32[]{:S(2)}, u32[]{:S(2)}) collective-permute-start(bf16[8,5120]{1,0:T(8,128)(2,1)S(1)} %pad_maximum_fusion.4), channel_id=1, source_target_pairs={{0,2},{2,0},{4,6},{6,4},{8,10},{10,8},{12,14},{14,12},{1,3},{3,1},... | collective-permute-start | bytes 245768 | tf_op jit(solution)/shard_map/ppermute | solution.py:13
  51.3 1.6 %collective-permute-start.10 = (bf16[16,5120]{1,0:T(8,128)(2,1)}, bf16[16,5120]{1,0:T(8,128)(2,1)S(1)}, u32[]{:S(2)}, u32[]{:S(2)}) collective-permute-start(bf16[16,5120]{1,0:T(8,128)(2,1)} %pad_maximum_fusion.2), channel_id=1, source_target_pairs={{0,1},{1,0},{2,3},{3,2},{4,5},{5,4},{6,7},{7,6},{8,9},{9,8},{10,11... | collective-permute-start | bytes 491528 | tf_op jit(solution)/shard_map/ppermute | solution.py:12
  52.6 1.7 %copy-start.1 = (bf16[5120,256]{1,0:T(8,128)(2,1)S(1)}, bf16[5120,256]{1,0:T(8,128)(2,1)}, u32[]{:S(2)}) copy-start(bf16[5120,256]{1,0:T(8,128)(2,1)} %param.6) | copy-start | bytes 7864324
  53.8 12.1 %copy-start.4 = (f32[256]{0:T(256)}, f32[256]{0:T(256)S(1)}, u32[]{:S(2)}) copy-start(f32[256]{0:T(256)S(1)} %get-tuple-element.11) | copy-start | bytes 3076
  56.5 1.4 %collective-permute-start.11 = (f32[5248]{0:T(1024)S(1)}, f32[5248]{0:T(1024)S(1)}, u32[]{:S(2)}, u32[]{:S(2)}) collective-permute-start(f32[5248]{0:T(1024)S(1)} %concatenate.40), channel_id=1, source_target_pairs={{0,1},{1,0},{2,3},{3,2},{4,5},{5,4},{6,7},{7,6},{8,9},{9,8},{10,11... | collective-permute-start | bytes 62984 | tf_op jit(solution)/shard_map/ppermute | solution.py:12
  57.9 3.8 %collective-permute-start.12 = (f32[5248]{0:T(1024)S(1)}, f32[5248]{0:T(1024)S(1)}, u32[]{:S(2)}, u32[]{:S(2)}) collective-permute-start(f32[5248]{0:T(1024)S(1)} %pad_add_fusion), channel_id=1, source_target_pairs={{0,2},{2,0},{4,6},{6,4},{8,10},{10,8},{12,14},{14,12},{1,3},{3,1},... | collective-permute-start | bytes 62984 | tf_op jit(solution)/shard_map/ppermute | solution.py:13
  61.7 4.1 %collective-permute-start.13 = (f32[5248]{0:T(1024)S(1)}, f32[5248]{0:T(1024)S(1)}, u32[]{:S(2)}, u32[]{:S(2)}) collective-permute-start(f32[5248]{0:T(1024)S(1)} %add.63), channel_id=1, source_target_pairs={{0,4},{2,6},{4,0},{6,2},{8,12},{10,14},{12,8},{14,10},{1,5},{3,7},... | collective-permute-start | bytes 62984 | tf_op jit(solution)/shard_map/ppermute | solution.py:13
  65.9 5.8 %collective-permute-start.14 = (f32[5248]{0:T(1024)S(1)}, f32[5248]{0:T(1024)S(1)}, u32[]{:S(2)}, u32[]{:S(2)}) collective-permute-start(f32[5248]{0:T(1024)S(1)} %add.64), channel_id=1, source_target_pairs={{0,8},{2,10},{4,12},{6,14},{8,0},{10,2},{12,4},{14,6},{1,9},{3,11}... | collective-permute-start | bytes 62984 | tf_op jit(solution)/shard_map/ppermute | solution.py:13

commit v2 on v1

v2 whole, which is shorter than its diff:
```python
import jax
import jax.numpy as jnp
from jax import lax
from jax.experimental import pallas as pl
from jax.experimental.pallas import tpu as pltpu
from jax.sharding import PartitionSpec as P

PENALTY = 0.2
CORES = 0
LANES = 128
VMEM = pl.BlockSpec(memory_space=pltpu.VMEM)


def swap(values, mask):
    if mask == CORES:
        return lax.ppermute(values, "sub", [(i, i ^ 1) for i in range(2)])
    return lax.ppermute(values, "lat", [(i, i ^ mask) for i in range(lax.axis_size("lat"))])


def plan(lat):
    bits = [1 << b for b in range(lat.bit_length() - 1)]
    near = bits[:-1]
    steps = [[1, 2, 3]] + [[b] for b in near[2:]] if len(near) > 1 else [[b] for b in near]
    return bits[-1], steps


def gather(rows, steps):
    for masks in steps:
        rows = jnp.concatenate([rows] + [swap(rows, mask) for mask in masks], axis=0)
        rows = lax.optimization_barrier(rows)
    return rows


def halve(rows, steps):
    for masks in steps:
        size = rows.shape[0] // (len(masks) + 1)
        parts = [rows[j * size : (j + 1) * size] for j in range(len(masks) + 1)]
        rows = parts[0] + sum(swap(part, mask) for part, mask in zip(parts[1:], masks))
    return rows


def encode_decode(half_a, half_b, enc_weight, enc_bias, dec_weight, dec_bias):
    half, width = half_a.shape
    latents = enc_weight.shape[1]

    def kernel(a_ref, b_ref, enc_ref, enc_bias_ref, dec_ref, dec_bias_ref, centered_ref, active_ref, codes_ref, keep_ref, send_ref):
        bias = dec_bias_ref[...]
        centered_ref[:half] = (a_ref[...].astype(jnp.float32) - bias).astype(jnp.bfloat16)
        centered_ref[half:] = (b_ref[...].astype(jnp.float32) - bias).astype(jnp.bfloat16)
        preact = jnp.dot(centered_ref[...], enc_ref[...], preferred_element_type=jnp.float32) + enc_bias_ref[...]
        active = jnp.maximum(preact, 0.0)
        active_ref[...] = active
        codes = (active * active).astype(jnp.bfloat16)
        codes_ref[...] = codes
        partial = jnp.dot(codes, dec_ref[...], preferred_element_type=jnp.float32)
        keep_ref[...] = partial[:half]
        send_ref[...] = partial[half:]

    return pl.pallas_call(
        kernel,
        out_shape=[
            jax.ShapeDtypeStruct((2 * half, width), jnp.bfloat16),
            jax.ShapeDtypeStruct((2 * half, latents), jnp.float32),
            jax.ShapeDtypeStruct((2 * half, latents), jnp.bfloat16),
            jax.ShapeDtypeStruct((half, width), jnp.float32),
            jax.ShapeDtypeStruct((half, width), jnp.float32),
        ],
        in_specs=[VMEM] * 6,
        out_specs=[VMEM] * 5,
        compiler_params=pltpu.CompilerParams(vmem_limit_bytes=40 << 20),
        name="encode_decode",
    )(half_a, half_b, enc_weight, enc_bias, dec_weight, dec_bias)


def backward(half_a, half_b, dec_weight, enc_weight, active, own_bias, row_count):
    half, width = half_a.shape
    latents = dec_weight.shape[0]
    contract_last = (((1,), (1,)), ((), ()))

    def kernel(a_ref, b_ref, dec_ref, enc_ref, active_ref, own_ref, code_grad_ref, enc_bias_ref, terms_ref):
        resid = jnp.concatenate([a_ref[...], b_ref[...]], axis=0)
        back = lax.dot_general(resid, dec_ref[...], contract_last, preferred_element_type=jnp.float32)
        code_grad = 2.0 * active_ref[...] * (back + PENALTY / row_count)
        code_grad_ref[...] = code_grad.astype(jnp.bfloat16)
        total = jnp.sum(code_grad, axis=0, keepdims=True)
        enc_bias_ref[...] = total
        high = total.astype(jnp.bfloat16)
        rest = total - high.astype(jnp.float32)
        middle = rest.astype(jnp.bfloat16)
        low = (rest - middle.astype(jnp.float32)).astype(jnp.bfloat16)
        pieces = jnp.concatenate([high, middle, low], axis=0)
        product = lax.dot_general(pieces, enc_ref[...], contract_last, preferred_element_type=jnp.float32)
        terms_ref[...] = own_ref[...] - (product[0:1] + (product[1:2] + product[2:3]))

    return pl.pallas_call(
        kernel,
        out_shape=[
            jax.ShapeDtypeStruct((2 * half, latents), jnp.bfloat16),
            jax.ShapeDtypeStruct((1, latents), jnp.float32),
            jax.ShapeDtypeStruct((1, width), jnp.float32),
        ],
        in_specs=[VMEM] * 6,
        out_specs=[VMEM] * 3,
        compiler_params=pltpu.CompilerParams(vmem_limit_bytes=40 << 20),
        name="backward",
    )(half_a, half_b, dec_weight, enc_weight, active, own_bias)


def local(residuals, enc_weight, enc_bias, dec_weight, dec_bias):
    own_rows, width = residuals.shape
    lat = lax.axis_size("lat")
    row_count = own_rows * lat * lax.axis_size("sub")
    far, steps = plan(lat)
    bias_row = dec_bias.reshape(1, width)

    paired = gather(residuals, [[far]])
    rows_a = gather(paired, steps)
    rows_b = swap(rows_a, CORES)
    centered, active, codes_bf, keep, send = encode_decode(
        rows_a, rows_b, enc_weight, enc_bias.reshape(1, -1), dec_weight, bias_row
    )

    summed = halve(keep + swap(send, CORES), steps[::-1])
    other = swap(summed, far)
    summed = summed + jnp.concatenate([other[own_rows:], other[:own_rows]], axis=0)
    recon_f = summed + dec_bias
    error_rows = recon_f - paired.astype(jnp.float32)
    resid_grad = 2.0 / row_count * error_rows
    resid_bf = resid_grad.astype(jnp.bfloat16)
    own_error = error_rows[:own_rows]
    sq_total = jnp.sum(own_error * own_error)
    own_bias = jnp.sum(resid_grad[:own_rows], axis=0, keepdims=True)
    code_total = jnp.sum(active * active)

    resid_a = gather(resid_bf, steps)
    resid_b = swap(resid_a, CORES)
    code_grad_bf, grad_enc_bias, bias_terms = backward(
        resid_a, resid_b, dec_weight, enc_weight, active, own_bias, row_count
    )
    scalars = (sq_total + PENALTY * code_total) / row_count
    terms = jnp.concatenate([bias_terms[0], jnp.broadcast_to(scalars, (LANES,))])
    for mask in [CORES] + [1 << b for b in range(lat.bit_length() - 1)]:
        terms = terms + swap(terms, mask)
    resid_all = jnp.concatenate([resid_a, resid_b], axis=0)
    grad_dec = lax.dot_general(
        codes_bf, resid_all, (((0,), (0,)), ((), ())), preferred_element_type=jnp.float32
    ).astype(jnp.bfloat16)
    grad_enc = lax.dot_general(
        centered, code_grad_bf, (((0,), (0,)), ((), ())), preferred_element_type=jnp.float32
    ).astype(jnp.bfloat16)
    return (
        recon_f[:own_rows].astype(jnp.bfloat16),
        terms[width : width + 1] / width,
        grad_enc,
        grad_enc_bias[0],
        grad_dec,
        terms[:width],
    )


def solution(mesh):
    placed = (
        P(("parts", "lat", "sub"), None),
        P(None, ("parts", "lat", "sub")),
        P(("parts", "lat", "sub")),
        P(("parts", "lat", "sub"), None),
        P("parts"),
    )
    return jax.shard_map(
        local,
        mesh=mesh,
        in_specs=placed,
        out_specs=(
            P(("parts", "lat", "sub"), None),
            P("parts"),
            P(None, ("parts", "lat", "sub")),
            P(("parts", "lat", "sub")),
            P(("parts", "lat", "sub"), None),
            P("parts"),
        ),
        check_vma=False,
    )
```

time: 75 us -> 69.7 us (0.929)
  matrix products: 11.1 us -> 4.74 us
  local copies, waits for them, and re-layouts: 3.31 us -> 8.46 us
  Pallas kernels: 0 us -> 4.45 us
  starting transfers between devices: 26 us -> 22.2 us
  waiting for transfers between devices: 26.1 us -> 23.2 us
  other arithmetic: 4.13 us -> 2.49 us
    dot_general x5 -> x1, matrix products: 8.79 us -> 2.38 us  [local(): lax.dot_general(centered, code_grad_bf, (((0,), (0,)), ((), ())), preferr...]
    unnamed x10 -> x12, local copies, waits for them, and re-layouts: 0.56 us -> 6.63 us
    pallas_call x0 -> x2, Pallas kernels: none -> 4.45 us  [the longest x1 2.9 us: backward(): pl.pallas_call(kernel, out_shape=[jax.ShapeDtypeStruct((2 * half, latents...]
    ppermute x11 -> x14, starting transfers between devices: 25.1 us -> 21.3 us  [swap(): lax.ppermute(values, 'lat', [(i, i ^ mask) for i in range(lax.axis_size('...]
    ppermute x11 -> x14, waiting for transfers between devices: 22.2 us -> 19.4 us  [swap(): lax.ppermute(values, 'lat', [(i, i ^ mask) for i in range(lax.axis_size('...]
    concatenate x5 -> x3, other arithmetic: 3.19 us -> 0.98 us  [gather(): jnp.concatenate([rows] + [swap(rows, mask) for mask in masks], axis=0)]
    concatenate x2 -> x1, local copies, waits for them, and re-layouts: 0.91 us -> 0.01 us  [local(): jnp.concatenate([bias_terms[0], jnp.broadcast_to(scalars, (LANES,))])]
  transfers between devices with their start and end apart: 15 -> 18, of which waited for: 13 -> 16; matrix products, arithmetic and copies ran while one was open for 8% -> 10% of each run, Pallas kernels for 0% -> 0%
where the time goes in v2:
time: 69.7 us; the launch traced here: 69.3 us
  waiting for transfers between devices  23.2 us (33%)
  starting transfers between devices  22.2 us (32%)
  local copies, waits for them, and re-layouts  8.46 us (12%)
  matrix products  4.74 us (7%)
  Pallas kernels  4.45 us (6%)
  between operations  3.81 us (5%)
  other arithmetic  2.49 us (4%)
    ppermute x14, starting transfers between devices, swap(): lax.ppermute(values, 'lat', [(i, i ^ mask) for i in range(lax.axis_size('...  21.3 us
    ppermute x14, waiting for transfers between devices, swap(): lax.ppermute(values, 'lat', [(i, i ^ mask) for i in range(lax.axis_size('...  19.4 us
    unnamed x12, local copies, waits for them, and re-layouts  6.63 us
    ppermute x4, waiting for transfers between devices, swap(): return lax.ppermute(values, 'sub', [(i, i ^ 1) for i in range(2)])  3.75 us
    pallas_call x1, Pallas kernels, backward(): pl.pallas_call(kernel, out_shape=[jax.ShapeDtypeStruct((2 * half, latents...  2.9 us
    dot_general x1, matrix products, local(): lax.dot_general(centered, code_grad_bf, (((0,), (0,)), ((), ())), preferr...  2.38 us
    dot_general x1, matrix products, local(): lax.dot_general(codes_bf, resid_all, (((0,), (0,)), ((), ())), preferred_...  2.36 us
    pallas_call x1, Pallas kernels, encode_decode(): pl.pallas_call(kernel, out_shape=[jax.ShapeDtypeStruct((2 * half, width),...  1.55 us
  transfers between devices with their start and end apart: 18, of which 16 were waited for; matrix products, arithmetic and copies ran while one was open for 10% of the time, Pallas kernels for 0%

profile of v2, /device:TPU:0, one launch (start us, length us, event | category | flops | bytes accessed | tf_op | source)
XLA Modules:
  0.0 69.3 jit_solution(8122437500070063911)
XLA Ops:
  0.6 4.1 %collective-permute-start = (bf16[2,5120]{1,0:T(2,128)(2,1)}, bf16[2,5120]{1,0:T(2,128)(2,1)S(1)}, u32[]{:S(2)}, u32[]{:S(2)}) collective-permute-start(bf16[2,5120]{1,0:T(2,128)(2,1)} %param.5), channel_id=1, source_target_pairs={{0,8},{2,10},{4,12},{6,14},{8,0},{10,2},{12,4},{14,6},{1,9},{3,11}... | collective-permute-start | bytes 61448 | tf_op jit(solution)/shard_map/ppermute | solution.py:17
  4.7 2.0 %collective-permute-done = bf16[2,5120]{1,0:T(2,128)(2,1)S(1)} collective-permute-done((bf16[2,5120]{1,0:T(2,128)(2,1)}, bf16[2,5120]{1,0:T(2,128)(2,1)S(1)}, u32[]{:S(2)}, u32[]{:S(2)}) %collective-permute-start) | collective-permute-done | bytes 20512 | tf_op jit(solution)/shard_map/ppermute | solution.py:17
  6.7 0.8 %pad_maximum_fusion.2 = bf16[4,5120]{1,0:T(4,128)(2,1)S(1)} fusion(bf16[2,5120]{1,0:T(2,128)(2,1)S(1)} %collective-permute-done, bf16[2,5120]{1,0:T(2,128)(2,1)} %param.5), kind=kLoop, calls=%fused_computation.15 | loop fusion | flops 81920 | bytes 81920 | tf_op jit(solution)/shard_map/concatenate | solution.py:29
  7.5 2.9 %collective-permute-start.3 = (bf16[4,5120]{1,0:T(4,128)(2,1)S(1)}, bf16[4,5120]{1,0:T(4,128)(2,1)S(1)}, u32[]{:S(2)}, u32[]{:S(2)}) collective-permute-start(bf16[4,5120]{1,0:T(4,128)(2,1)S(1)} %pad_maximum_fusion.2), channel_id=1, source_target_pairs={{0,6},{2,4},{4,2},{6,0},{8,14},{10,12},{12,10},{14,8},{1,7},{3,5},... | collective-permute-start | bytes 122888 | tf_op jit(solution)/shard_map/ppermute | solution.py:17
  11.0 1.4 %collective-permute-done.3 = bf16[4,5120]{1,0:T(4,128)(2,1)S(1)} collective-permute-done((bf16[4,5120]{1,0:T(4,128)(2,1)S(1)}, bf16[4,5120]{1,0:T(4,128)(2,1)S(1)}, u32[]{:S(2)}, u32[]{:S(2)}) %collective-permute-start.3) | collective-permute-done | bytes 40992 | tf_op jit(solution)/shard_map/ppermute | solution.py:17
  12.5 1.9 %collective-permute-done.2 = bf16[4,5120]{1,0:T(4,128)(2,1)S(1)} collective-permute-done((bf16[4,5120]{1,0:T(4,128)(2,1)S(1)}, bf16[4,5120]{1,0:T(4,128)(2,1)S(1)}, u32[]{:S(2)}, u32[]{:S(2)}) %collective-permute-start.2) | collective-permute-done | bytes 40992 | tf_op jit(solution)/shard_map/ppermute | solution.py:17
  15.1 1.4 %collective-permute-done.4.b_ref = bf16[16,5120]{1,0:T(8,128)(2,1)S(1)} collective-permute-done((bf16[16,5120]{1,0:T(8,128)(2,1)S(1)}, bf16[16,5120]{1,0:T(8,128)(2,1)S(1)}, u32[]{:S(2)}, u32[]{:S(2)}) %collective-permute-start.4) | collective-permute-done | bytes 163872 | tf_op jit(solution)/shard_map/ppermute | solution.py:16
  16.5 1.7 %copy-done = bf16[5120,256]{1,0:T(8,128)(2,1)S(1)} copy-done((bf16[5120,256]{1,0:T(8,128)(2,1)S(1)}, bf16[5120,256]{1,0:T(8,128)(2,1)}, u32[]{:S(2)}) %copy-start) | copy-done | bytes 2621464
  18.2 1.7 %copy-done.2 = bf16[256,5120]{1,0:T(8,128)(2,1)S(1)} copy-done((bf16[256,5120]{1,0:T(8,128)(2,1)S(1)}, bf16[256,5120]{1,0:T(8,128)(2,1)}, u32[]{:S(2)}) %copy-start.2) | copy-done | bytes 2621464
  20.0 0.7 %copy-done.4 = f32[5120]{0:T(1024)S(1)} copy-done((f32[5120]{0:T(1024)S(1)}, f32[5120]{0:T(1024)}, u32[]{:S(2)}) %copy-start.4) | copy-done | bytes 20504
  20.7 0.7 copy-done.5
  21.4 1.5 %encode_decode.1 = (bf16[32,5120]{1,0:T(8,128)(2,1)S(1)}, f32[32,256]{1,0:T(8,128)S(1)}, bf16[32,256]{1,0:T(8,128)(2,1)S(1)}, f32[16,5120]{1,0:T(8,128)S(1)}, f32[16,5120]{1,0:T(8,128)S(1)}) custom-call(bf16[16,5120]{1,0:T(8,128)(2,1)S(1)} %pad_maximum_fusion.a_ref, bf16[16,5120]{1,0:T(8,128)(2,1)S(1)} %collective-permute-done.4.b_ref, ...), custom_call_target="tpu_custom_call" | custom-call | tf_op jit(solution)/shard_map/encode_decode/pallas_call | solution.py:59
  23.1 1.5 %collective-permute-done.5 = f32[16,5120]{1,0:T(8,128)S(1)} collective-permute-done((f32[16,5120]{1,0:T(8,128)S(1)}, f32[16,5120]{1,0:T(8,128)S(1)}, u32[]{:S(2)}, u32[]{:S(2)}) %collective-permute-start.5) | collective-permute-done | bytes 327712 | tf_op jit(solution)/shard_map/ppermute | solution.py:16
  24.7 1.5 %collective-permute-start.7 = (f32[4,5120]{1,0:T(4,128)S(1)}, f32[4,5120]{1,0:T(4,128)S(1)}, u32[]{:S(2)}, u32[]{:S(2)}) collective-permute-start(f32[4,5120]{1,0:T(4,128)S(1)} %get-tuple-element.25), channel_id=1, source_target_pairs={{0,4},{2,6},{4,0},{6,2},{8,12},{10,14},{12,8},{14,10},{1,5},{3,7},... | collective-permute-start | bytes 245768 | tf_op jit(solution)/shard_map/ppermute | solution.py:17
  26.4 1.9 %collective-permute-start.6 = (f32[4,5120]{1,0:T(4,128)S(1)}, f32[4,5120]{1,0:T(4,128)S(1)}, u32[]{:S(2)}, u32[]{:S(2)}) collective-permute-start(f32[4,5120]{1,0:T(4,128)S(1)} %get-tuple-element.27), channel_id=1, source_target_pairs={{0,2},{2,0},{4,6},{6,4},{8,10},{10,8},{12,14},{14,12},{1,3},{3,1},... | collective-permute-start | bytes 245768 | tf_op jit(solution)/shard_map/ppermute | solution.py:17
  28.3 1.6 %collective-permute-done.7 = f32[4,5120]{1,0:T(4,128)S(1)} collective-permute-done((f32[4,5120]{1,0:T(4,128)S(1)}, f32[4,5120]{1,0:T(4,128)S(1)}, u32[]{:S(2)}, u32[]{:S(2)}) %collective-permute-start.7) | collective-permute-done | bytes 81952 | tf_op jit(solution)/shard_map/ppermute | solution.py:17
  29.9 1.8 %collective-permute-done.8 = f32[4,5120]{1,0:T(4,128)S(1)} collective-permute-done((f32[4,5120]{1,0:T(4,128)S(1)}, f32[4,5120]{1,0:T(4,128)S(1)}, u32[]{:S(2)}, u32[]{:S(2)}) %collective-permute-start.8) | collective-permute-done | bytes 81952 | tf_op jit(solution)/shard_map/ppermute | solution.py:17
  32.3 2.8 %collective-permute-start.9 = (f32[4,5120]{1,0:T(4,128)S(1)}, f32[4,5120]{1,0:T(4,128)S(1)}, u32[]{:S(2)}, u32[]{:S(2)}) collective-permute-start(f32[4,5120]{1,0:T(4,128)S(1)} %slice_add_fusion), channel_id=1, source_target_pairs={{0,8},{2,10},{4,12},{6,14},{8,0},{10,2},{12,4},{14,6},{1,9},{3,11}... | collective-permute-start | bytes 245768 | tf_op jit(solution)/shard_map/ppermute | solution.py:17
  35.1 3.9 %collective-permute-done.9 = f32[4,5120]{1,0:T(4,128)S(1)} collective-permute-done((f32[4,5120]{1,0:T(4,128)S(1)}, f32[4,5120]{1,0:T(4,128)S(1)}, u32[]{:S(2)}, u32[]{:S(2)}) %collective-permute-start.9) | collective-permute-done | bytes 81952 | tf_op jit(solution)/shard_map/ppermute | solution.py:17
  39.2 1.5 %collective-permute-start.12 = (bf16[4,5120]{1,0:T(4,128)(2,1)S(1)}, bf16[4,5120]{1,0:T(4,128)(2,1)S(1)}, u32[]{:S(2)}, u32[]{:S(2)}) collective-permute-start(bf16[4,5120]{1,0:T(4,128)(2,1)S(1)} %fusion.6), channel_id=1, source_target_pairs={{0,6},{2,4},{4,2},{6,0},{8,14},{10,12},{12,10},{14,8},{1,7},{3,5},... | collective-permute-start | bytes 122888 | tf_op jit(solution)/shard_map/ppermute | solution.py:17
  40.7 1.4 %collective-permute-start.11 = (bf16[4,5120]{1,0:T(4,128)(2,1)S(1)}, bf16[4,5120]{1,0:T(4,128)(2,1)S(1)}, u32[]{:S(2)}, u32[]{:S(2)}) collective-permute-start(bf16[4,5120]{1,0:T(4,128)(2,1)S(1)} %fusion.6), channel_id=1, source_target_pairs={{0,4},{2,6},{4,0},{6,2},{8,12},{10,14},{12,8},{14,10},{1,5},{3,7},... | collective-permute-start | bytes 122888 | tf_op jit(solution)/shard_map/ppermute | solution.py:17
  44.7 1.4 %collective-permute-done.10 = bf16[4,5120]{1,0:T(4,128)(2,1)S(1)} collective-permute-done((bf16[4,5120]{1,0:T(4,128)(2,1)S(1)}, bf16[4,5120]{1,0:T(4,128)(2,1)S(1)}, u32[]{:S(2)}, u32[]{:S(2)}) %collective-permute-start.10) | collective-permute-done | bytes 40992 | tf_op jit(solution)/shard_map/ppermute | solution.py:17
  46.3 0.6 fusion.4
  47.7 1.7 %copy-done.3 = bf16[256,5120]{1,0:T(8,128)(2,1)S(1)} copy-done((bf16[256,5120]{1,0:T(8,128)(2,1)S(1)}, bf16[256,5120]{1,0:T(8,128)(2,1)}, u32[]{:S(2)}) %copy-start.3) | copy-done | bytes 2621464
  49.5 2.9 %backward.1 = (bf16[32,256]{1,0:T(8,128)(2,1)S(1)}, f32[1,256]{1,0:T(1,128)}, f32[1,5120]{1,0:T(1,128)S(1)}) custom-call(bf16[16,5120]{1,0:T(8,128)(2,1)S(1)} %pad_maximum_fusion.1.a_ref, bf16[16,5120]{1,0:T(8,128)(2,1)S(1)} %collective-permute-done.13.b_ref, bf16[256,5120]{1,0:T(8,128)(2,1)S(1)} %copy-done.3, bf16[5120,256]{1,0:T(8,128)(2,1)S(1)} %copy-done.1, ...), custom_call_target="tpu_custom_call" | custom-call | tf_op jit(solution)/shard_map/backward/pallas_call | solution.py:95
  52.9 0.8 %collective-permute-done.14 = f32[5248]{0:T(1024)S(1)} collective-permute-done((f32[5248]{0:T(1024)S(1)}, f32[5248]{0:T(1024)S(1)}, u32[]{:S(2)}, u32[]{:S(2)}) %collective-permute-start.14) | collective-permute-done | bytes 21024 | tf_op jit(solution)/shard_map/ppermute | solution.py:16
  54.4 0.6 slice.62
  55.0 2.6 %collective-permute-done.15 = f32[5248]{0:T(1024)S(1)} collective-permute-done((f32[5248]{0:T(1024)S(1)}, f32[5248]{0:T(1024)S(1)}, u32[]{:S(2)}, u32[]{:S(2)}) %collective-permute-start.15) | collective-permute-done | bytes 21024 | tf_op jit(solution)/shard_map/ppermute | solution.py:17
  58.2 2.4 %convolution_convert_fusion.1 = bf16[5120,256]{1,0:T(8,128)(2,1)} fusion(bf16[32,5120]{1,0:T(8,128)(2,1)S(1)} %get-tuple-element.18, bf16[32,256]{1,0:T(8,128)(2,1)S(1)} %get-tuple-element.19), kind=kOutput, calls=%fused_computation.1 | convolution fusion | flops 85196800 | bytes 2965504 | tf_op jit(solution)/shard_map/dot_general | solution.py:148
  60.6 0.9 %collective-permute-done.16 = f32[5248]{0:T(1024)S(1)} collective-permute-done((f32[5248]{0:T(1024)S(1)}, f32[5248]{0:T(1024)S(1)}, u32[]{:S(2)}, u32[]{:S(2)}) %collective-permute-start.16) | collective-permute-done | bytes 21024 | tf_op jit(solution)/shard_map/ppermute | solution.py:17
  61.5 2.6 %collective-permute-start.17 = (f32[5248]{0:T(1024)S(1)}, f32[5248]{0:T(1024)S(1)}, u32[]{:S(2)}, u32[]{:S(2)}) collective-permute-start(f32[5248]{0:T(1024)S(1)} %add.50), channel_id=1, source_target_pairs={{0,8},{2,10},{4,12},{6,14},{8,0},{10,2},{12,4},{14,6},{1,9},{3,11}... | collective-permute-start | bytes 62984 | tf_op jit(solution)/shard_map/ppermute | solution.py:17
  64.0 2.4 %convolution_convert_fusion = bf16[256,5120]{1,0:T(8,128)(2,1)} fusion(bf16[32,256]{1,0:T(8,128)(2,1)S(1)} %get-tuple-element.21, bf16[16,5120]{1,0:T(8,128)(2,1)S(1)} %collective-permute-done.13.b_ref, bf16[16,5120]{1,0:T(8,128)(2,1)S(1)} %pad_maximum_fusion.1.a_ref), kind=kOutput, calls=%fused_computation | convolution fusion | flops 85852160 | bytes 2965504 | tf_op jit(solution)/shard_map/dot_general | solution.py:145
  (40 shorter events, 7.6 us)
Async XLA Ops:
  0.6 6.1 %collective-permute-start = (bf16[2,5120]{1,0:T(2,128)(2,1)}, bf16[2,5120]{1,0:T(2,128)(2,1)S(1)}, u32[]{:S(2)}, u32[]{:S(2)}) collective-permute-start(bf16[2,5120]{1,0:T(2,128)(2,1)} %param.5), channel_id=1, source_target_pairs={{0,8},{2,10},{4,12},{6,14},{8,0},{10,2},{12,4},{14,6},{1,9},{3,11}... | collective-permute-start | bytes 61448 | tf_op jit(solution)/shard_map/ppermute | solution.py:17
  7.5 5.0 %collective-permute-start.3 = (bf16[4,5120]{1,0:T(4,128)(2,1)S(1)}, bf16[4,5120]{1,0:T(4,128)(2,1)S(1)}, u32[]{:S(2)}, u32[]{:S(2)}) collective-permute-start(bf16[4,5120]{1,0:T(4,128)(2,1)S(1)} %pad_maximum_fusion.2), channel_id=1, source_target_pairs={{0,6},{2,4},{4,2},{6,0},{8,14},{10,12},{12,10},{14,8},{1,7},{3,5},... | collective-permute-start | bytes 122888 | tf_op jit(solution)/shard_map/ppermute | solution.py:17
  10.4 4.0 %collective-permute-start.2 = (bf16[4,5120]{1,0:T(4,128)(2,1)S(1)}, bf16[4,5120]{1,0:T(4,128)(2,1)S(1)}, u32[]{:S(2)}, u32[]{:S(2)}) collective-permute-start(bf16[4,5120]{1,0:T(4,128)(2,1)S(1)} %pad_maximum_fusion.2), channel_id=1, source_target_pairs={{0,4},{2,6},{4,0},{6,2},{8,12},{10,14},{12,8},{14,10},{1,5},{3,7},... | collective-permute-start | bytes 122888 | tf_op jit(solution)/shard_map/ppermute | solution.py:17
  10.9 4.0 %collective-permute-start.1 = (bf16[4,5120]{1,0:T(4,128)(2,1)S(1)}, bf16[4,5120]{1,0:T(4,128)(2,1)S(1)}, u32[]{:S(2)}, u32[]{:S(2)}) collective-permute-start(bf16[4,5120]{1,0:T(4,128)(2,1)S(1)} %pad_maximum_fusion.2), channel_id=1, source_target_pairs={{0,2},{2,0},{4,6},{6,4},{8,10},{10,8},{12,14},{14,12},{1,3},{3,1},... | collective-permute-start | bytes 122888 | tf_op jit(solution)/shard_map/ppermute | solution.py:17
  15.0 1.5 %collective-permute-start.4 = (bf16[16,5120]{1,0:T(8,128)(2,1)S(1)}, bf16[16,5120]{1,0:T(8,128)(2,1)S(1)}, u32[]{:S(2)}, u32[]{:S(2)}) collective-permute-start(bf16[16,5120]{1,0:T(8,128)(2,1)S(1)} %pad_maximum_fusion.a_ref), channel_id=1, source_target_pairs={{0,1},{1,0},{2,3},{3,2},{4,5},{5,4},{6,7},{7,6},{8,9},{9,8},{10,11... | collective-permute-start | bytes 491528 | tf_op jit(solution)/shard_map/ppermute | solution.py:16
  16.5 1.7 %copy-start = (bf16[5120,256]{1,0:T(8,128)(2,1)S(1)}, bf16[5120,256]{1,0:T(8,128)(2,1)}, u32[]{:S(2)}) copy-start(bf16[5120,256]{1,0:T(8,128)(2,1)} %enc_ref.3) | copy-start | bytes 7864324
  18.2 1.7 %copy-start.2 = (bf16[256,5120]{1,0:T(8,128)(2,1)S(1)}, bf16[256,5120]{1,0:T(8,128)(2,1)}, u32[]{:S(2)}) copy-start(bf16[256,5120]{1,0:T(8,128)(2,1)} %dec_ref.3) | copy-start | bytes 7864324
  20.0 0.7 %copy-start.4 = (f32[5120]{0:T(1024)S(1)}, f32[5120]{0:T(1024)}, u32[]{:S(2)}) copy-start(f32[5120]{0:T(1024)} %param.9) | copy-start | bytes 61444
  20.7 0.7 copy-start.5
  22.9 24.8 %copy-start.1 = (bf16[5120,256]{1,0:T(8,128)(2,1)S(1)}, bf16[5120,256]{1,0:T(8,128)(2,1)}, u32[]{:S(2)}) copy-start(bf16[5120,256]{1,0:T(8,128)(2,1)} %enc_ref.3) | copy-start | bytes 7864324
  22.9 1.7 %collective-permute-start.5 = (f32[16,5120]{1,0:T(8,128)S(1)}, f32[16,5120]{1,0:T(8,128)S(1)}, u32[]{:S(2)}, u32[]{:S(2)}) collective-permute-start(f32[16,5120]{1,0:T(8,128)S(1)} %get-tuple-element.15), channel_id=1, source_target_pairs={{0,1},{1,0},{2,3},{3,2},{4,5},{5,4},{6,7},{7,6},{8,9},{9,8},{10,11... | collective-permute-start | bytes 983048 | tf_op jit(solution)/shard_map/ppermute | solution.py:16
  24.7 5.1 %collective-permute-start.7 = (f32[4,5120]{1,0:T(4,128)S(1)}, f32[4,5120]{1,0:T(4,128)S(1)}, u32[]{:S(2)}, u32[]{:S(2)}) collective-permute-start(f32[4,5120]{1,0:T(4,128)S(1)} %get-tuple-element.25), channel_id=1, source_target_pairs={{0,4},{2,6},{4,0},{6,2},{8,12},{10,14},{12,8},{14,10},{1,5},{3,7},... | collective-permute-start | bytes 245768 | tf_op jit(solution)/shard_map/ppermute | solution.py:17
  26.3 5.4 %collective-permute-start.8 = (f32[4,5120]{1,0:T(4,128)S(1)}, f32[4,5120]{1,0:T(4,128)S(1)}, u32[]{:S(2)}, u32[]{:S(2)}) collective-permute-start(f32[4,5120]{1,0:T(4,128)S(1)} %get-tuple-element.26), channel_id=1, source_target_pairs={{0,6},{2,4},{4,2},{6,0},{8,14},{10,12},{12,10},{14,8},{1,7},{3,5},... | collective-permute-start | bytes 245768 | tf_op jit(solution)/shard_map/ppermute | solution.py:17
  26.4 5.9 %collective-permute-start.6 = (f32[4,5120]{1,0:T(4,128)S(1)}, f32[4,5120]{1,0:T(4,128)S(1)}, u32[]{:S(2)}, u32[]{:S(2)}) collective-permute-start(f32[4,5120]{1,0:T(4,128)S(1)} %get-tuple-element.27), channel_id=1, source_target_pairs={{0,2},{2,0},{4,6},{6,4},{8,10},{10,8},{12,14},{14,12},{1,3},{3,1},... | collective-permute-start | bytes 245768 | tf_op jit(solution)/shard_map/ppermute | solution.py:17
  32.3 6.7 %collective-permute-start.9 = (f32[4,5120]{1,0:T(4,128)S(1)}, f32[4,5120]{1,0:T(4,128)S(1)}, u32[]{:S(2)}, u32[]{:S(2)}) collective-permute-start(f32[4,5120]{1,0:T(4,128)S(1)} %slice_add_fusion), channel_id=1, source_target_pairs={{0,8},{2,10},{4,12},{6,14},{8,0},{10,2},{12,4},{14,6},{1,9},{3,11}... | collective-permute-start | bytes 245768 | tf_op jit(solution)/shard_map/ppermute | solution.py:17
  39.2 5.0 %collective-permute-start.12 = (bf16[4,5120]{1,0:T(4,128)(2,1)S(1)}, bf16[4,5120]{1,0:T(4,128)(2,1)S(1)}, u32[]{:S(2)}, u32[]{:S(2)}) collective-permute-start(bf16[4,5120]{1,0:T(4,128)(2,1)S(1)} %fusion.6), channel_id=1, source_target_pairs={{0,6},{2,4},{4,2},{6,0},{8,14},{10,12},{12,10},{14,8},{1,7},{3,5},... | collective-permute-start | bytes 122888 | tf_op jit(solution)/shard_map/ppermute | solution.py:17
  40.7 4.0 %collective-permute-start.11 = (bf16[4,5120]{1,0:T(4,128)(2,1)S(1)}, bf16[4,5120]{1,0:T(4,128)(2,1)S(1)}, u32[]{:S(2)}, u32[]{:S(2)}) collective-permute-start(bf16[4,5120]{1,0:T(4,128)(2,1)S(1)} %fusion.6), channel_id=1, source_target_pairs={{0,4},{2,6},{4,0},{6,2},{8,12},{10,14},{12,8},{14,10},{1,5},{3,7},... | collective-permute-start | bytes 122888 | tf_op jit(solution)/shard_map/ppermute | solution.py:17
  42.2 4.0 %collective-permute-start.10 = (bf16[4,5120]{1,0:T(4,128)(2,1)S(1)}, bf16[4,5120]{1,0:T(4,128)(2,1)S(1)}, u32[]{:S(2)}, u32[]{:S(2)}) collective-permute-start(bf16[4,5120]{1,0:T(4,128)(2,1)S(1)} %fusion.6), channel_id=1, source_target_pairs={{0,2},{2,0},{4,6},{6,4},{8,10},{10,8},{12,14},{14,12},{1,3},{3,1},... | collective-permute-start | bytes 122888 | tf_op jit(solution)/shard_map/ppermute | solution.py:17
  46.3 1.5 %collective-permute-start.13 = (bf16[16,5120]{1,0:T(8,128)(2,1)S(1)}, bf16[16,5120]{1,0:T(8,128)(2,1)S(1)}, u32[]{:S(2)}, u32[]{:S(2)}) collective-permute-start(bf16[16,5120]{1,0:T(8,128)(2,1)S(1)} %pad_maximum_fusion.1.a_ref), channel_id=1, source_target_pairs={{0,1},{1,0},{2,3},{3,2},{4,5},{5,4},{6,7},{7,6},{8,9},{9,8},{10,11... | collective-permute-start | bytes 491528 | tf_op jit(solution)/shard_map/ppermute | solution.py:16
  47.7 1.7 %copy-start.3 = (bf16[256,5120]{1,0:T(8,128)(2,1)S(1)}, bf16[256,5120]{1,0:T(8,128)(2,1)}, u32[]{:S(2)}) copy-start(bf16[256,5120]{1,0:T(8,128)(2,1)} %dec_ref.3) | copy-start | bytes 7864324
  52.4 1.4 %collective-permute-start.14 = (f32[5248]{0:T(1024)S(1)}, f32[5248]{0:T(1024)S(1)}, u32[]{:S(2)}, u32[]{:S(2)}) collective-permute-start(f32[5248]{0:T(1024)S(1)} %concatenate.22), channel_id=1, source_target_pairs={{0,1},{1,0},{2,3},{3,2},{4,5},{5,4},{6,7},{7,6},{8,9},{9,8},{10,11... | collective-permute-start | bytes 62984 | tf_op jit(solution)/shard_map/ppermute | solution.py:16
  53.8 3.8 %collective-permute-start.15 = (f32[5248]{0:T(1024)S(1)}, f32[5248]{0:T(1024)S(1)}, u32[]{:S(2)}, u32[]{:S(2)}) collective-permute-start(f32[5248]{0:T(1024)S(1)} %pad_add_fusion), channel_id=1, source_target_pairs={{0,2},{2,0},{4,6},{6,4},{8,10},{10,8},{12,14},{14,12},{1,3},{3,1},... | collective-permute-start | bytes 62984 | tf_op jit(solution)/shard_map/ppermute | solution.py:17
  57.6 3.8 %collective-permute-start.16 = (f32[5248]{0:T(1024)S(1)}, f32[5248]{0:T(1024)S(1)}, u32[]{:S(2)}, u32[]{:S(2)}) collective-permute-start(f32[5248]{0:T(1024)S(1)} %add.49), channel_id=1, source_target_pairs={{0,4},{2,6},{4,0},{6,2},{8,12},{10,14},{12,8},{14,10},{1,5},{3,7},... | collective-permute-start | bytes 62984 | tf_op jit(solution)/shard_map/ppermute | solution.py:17
  61.5 4.9 %collective-permute-start.17 = (f32[5248]{0:T(1024)S(1)}, f32[5248]{0:T(1024)S(1)}, u32[]{:S(2)}, u32[]{:S(2)}) collective-permute-start(f32[5248]{0:T(1024)S(1)} %add.50), channel_id=1, source_target_pairs={{0,8},{2,10},{4,12},{6,14},{8,0},{10,2},{12,4},{14,6},{1,9},{3,11}... | collective-permute-start | bytes 62984 | tf_op jit(solution)/shard_map/ppermute | solution.py:17

commit v3 on v2

v3 whole, which is shorter than its diff:
```python
import jax
import jax.numpy as jnp
from jax import lax
from jax.experimental import pallas as pl
from jax.experimental.pallas import tpu as pltpu
from jax.sharding import PartitionSpec as P

PENALTY = 0.2
CORES = 0
LANES = 128
LIMIT = 12 << 20
VMEM = pl.BlockSpec(memory_space=pltpu.VMEM)
HBM = pl.BlockSpec(memory_space=pltpu.HBM)
CONTRACT_FIRST = (((0,), (0,)), ((), ()))
CONTRACT_LAST = (((1,), (1,)), ((), ()))


def vmem(shape, dtype):
    return pltpu.VMEM(shape, dtype)


def in_vmem(array):
    return pltpu.with_memory_space_constraint(array, pltpu.VMEM)


def in_hbm(array):
    return pltpu.with_memory_space_constraint(array, pltpu.HBM)


TOKEN = ((8, LANES), jnp.float32)


def run(kernel, name, outs, args, after=(), flops=0, moved=0, limit=LIMIT):
    count = len(args)

    def body(*refs):
        kernel(*refs[:count], *refs[count + len(after) :])

    return pl.pallas_call(
        body,
        out_shape=[vmem(*out) for out in outs],
        in_specs=[VMEM] * (count + len(after)),
        out_specs=[VMEM] * len(outs),
        compiler_params=pltpu.CompilerParams(vmem_limit_bytes=limit),
        cost_estimate=pl.CostEstimate(flops=flops, bytes_accessed=moved, transcendentals=0),
        name=name,
    )(*[in_vmem(a) for a in args], *[in_vmem(a) for a in after])


def swap(values, mask):
    if mask == CORES:
        return lax.ppermute(values, "sub", [(i, i ^ 1) for i in range(2)])
    return lax.ppermute(values, "lat", [(i, i ^ mask) for i in range(lax.axis_size("lat"))])


def plan(lat):
    bits = [1 << b for b in range(lat.bit_length() - 1)]
    near = bits[:-1]
    steps = [[1, 2, 3]] + [[b] for b in near[2:]] if len(near) > 1 else [[b] for b in near]
    return bits[-1], steps


def load(arrays, after=()):
    count = len(arrays)

    def kernel(*refs):
        copies = [
            pltpu.make_async_copy(refs[i], refs[count + len(after) + i], refs[-1].at[i]) for i in range(count)
        ]
        for copy in copies:
            copy.start()
        for copy in copies:
            copy.wait()

    return pl.pallas_call(
        kernel,
        out_shape=[vmem(array.shape, array.dtype) for array in arrays],
        in_specs=[HBM] * count + [VMEM] * len(after),
        out_specs=[VMEM] * count,
        scratch_shapes=[pltpu.SemaphoreType.DMA((count,))],
        compiler_params=pltpu.CompilerParams(vmem_limit_bytes=LIMIT),
        cost_estimate=pl.CostEstimate(
            flops=0, bytes_accessed=2 * sum(a.size * a.dtype.itemsize for a in arrays), transcendentals=0
        ),
        name="load",
    )(*[in_hbm(a) for a in arrays], *[in_vmem(a) for a in after])


def stack(blocks, after=()):
    rows, width = blocks[0].shape

    def kernel(*refs):
        refs[-1][...] = jnp.concatenate([ref[...] for ref in refs[:-1]], axis=0)

    shape = (sum(block.shape[0] for block in blocks), width)
    return run(kernel, "stack", [(shape, blocks[0].dtype)], blocks, after)[0]


def gather(rows, steps, after=()):
    for masks in steps:
        rows = stack([rows] + [swap(rows, mask) for mask in masks], after)
    return rows


def add_parts(first, others, count):
    rows, width = first.shape
    size = rows // count

    def kernel(*refs):
        total = refs[0][...]
        for ref in refs[1 : 1 + len(others)]:
            total = total + ref[...]
        for part, ref in enumerate(refs[1 + len(others) :]):
            ref[...] = total[part * size : (part + 1) * size]

    return run(kernel, "add_parts", [((size, width), jnp.float32)] * count, [first, *others])


def halve(first, others, steps):
    for masks in steps:
        parts = add_parts(first, others, len(masks) + 1)
        first, others = parts[0], [swap(part, mask) for part, mask in zip(parts[1:], masks)]
    return add_parts(first, others, 1)[0]


def encode_decode(half_a, half_b, enc_weight, enc_bias, dec_weight, dec_bias):
    half, width = half_a.shape
    latents = enc_weight.shape[1]

    def kernel(a_ref, b_ref, enc_ref, enc_bias_ref, dec_ref, dec_bias_ref, centered_ref, active_ref, codes_ref, keep_ref, send_ref, sum_ref):
        bias = dec_bias_ref[...]
        centered_ref[:half] = (a_ref[...].astype(jnp.float32) - bias).astype(jnp.bfloat16)
        centered_ref[half:] = (b_ref[...].astype(jnp.float32) - bias).astype(jnp.bfloat16)
        preact = jnp.dot(centered_ref[...], enc_ref[...], preferred_element_type=jnp.float32) + enc_bias_ref[...]
        active = jnp.maximum(preact, 0.0)
        active_ref[...] = active
        codes = active * active
        codes_bf = codes.astype(jnp.bfloat16)
        codes_ref[...] = codes_bf
        partial = jnp.dot(codes_bf, dec_ref[...], preferred_element_type=jnp.float32)
        keep_ref[...] = partial[:half]
        send_ref[...] = partial[half:]
        sum_ref[...] = jnp.broadcast_to(jnp.sum(codes, keepdims=True), (1, LANES))

    return run(
        kernel,
        "encode_decode",
        [
            ((2 * half, width), jnp.bfloat16),
            ((2 * half, latents), jnp.float32),
            ((2 * half, latents), jnp.bfloat16),
            ((half, width), jnp.float32),
            ((half, width), jnp.float32),
            ((1, LANES), jnp.float32),
        ],
        [half_a, half_b, enc_weight, enc_bias, dec_weight, dec_bias],
    )


def residual_gradient(summed, other, paired, dec_bias, row_count):
    rows, width = summed.shape
    own = rows // 2

    def kernel(summed_ref, other_ref, paired_ref, bias_ref, recon_ref, resid_ref, own_ref, square_ref):
        total = summed_ref[...] + jnp.concatenate([other_ref[own:], other_ref[:own]], axis=0)
        recon = total + bias_ref[...]
        error = recon - paired_ref[...].astype(jnp.float32)
        grad = 2.0 / row_count * error
        recon_ref[...] = recon[:own].astype(jnp.bfloat16)
        resid_ref[...] = grad.astype(jnp.bfloat16)
        own_ref[...] = jnp.sum(grad[:own], axis=0, keepdims=True)
        square_ref[...] = jnp.broadcast_to(jnp.sum(error[:own] * error[:own], keepdims=True), (1, LANES))

    return run(
        kernel,
        "residual_gradient",
        [
            ((own, width), jnp.bfloat16),
            ((rows, width), jnp.bfloat16),
            ((1, width), jnp.float32),
            ((1, LANES), jnp.float32),
        ],
        [summed, other, paired, dec_bias],
    )


def backward(half_a, half_b, dec_weight, active, row_count):
    half, width = half_a.shape
    latents = dec_weight.shape[0]

    def kernel(a_ref, b_ref, dec_ref, active_ref, code_grad_ref, total_ref):
        resid = jnp.concatenate([a_ref[...], b_ref[...]], axis=0)
        back = lax.dot_general(resid, dec_ref[...], CONTRACT_LAST, preferred_element_type=jnp.float32)
        code_grad = 2.0 * active_ref[...] * (back + PENALTY / row_count)
        code_grad_ref[...] = code_grad.astype(jnp.bfloat16)
        total_ref[...] = jnp.sum(code_grad, axis=0, keepdims=True)

    return run(
        kernel,
        "backward",
        [((2 * half, latents), jnp.bfloat16), ((1, latents), jnp.float32)],
        [half_a, half_b, dec_weight, active],
    )


def bias_product(total, enc_weight, own_bias, square, code_sum, row_count):
    width, latents = enc_weight.shape

    def kernel(total_ref, enc_ref, own_ref, square_ref, sum_ref, terms_ref):
        values = total_ref[...]
        high = values.astype(jnp.bfloat16).astype(jnp.float32)
        rest = values - high
        middle = rest.astype(jnp.bfloat16).astype(jnp.float32)
        pieces = [high, middle, rest - middle, jnp.zeros((5, latents), jnp.float32)]
        pieces = jnp.concatenate(pieces, axis=0).astype(jnp.bfloat16)
        product = lax.dot_general(pieces, enc_ref[...], CONTRACT_LAST, preferred_element_type=jnp.float32)
        terms_ref[:, :width] = own_ref[...] - (product[0:1] + (product[1:2] + product[2:3]))
        terms_ref[:, width:] = (square_ref[...] + PENALTY * sum_ref[...]) / row_count

    return run(
        kernel,
        "bias_product",
        [((1, width + LANES), jnp.float32)],
        [total, enc_weight, own_bias, square, code_sum],
    )[0]


def dec_gradient(codes, resid_a, resid_b, recon, after, pieces=4):
    rows, latents = codes.shape
    half, width = resid_a.shape
    size = width // pieces

    def kernel(codes_ref, a_ref, b_ref, recon_ref, after_ref, grad_ref, recon_out_ref, token_ref, buffer, sems):
        recon_copy = pltpu.make_async_copy(recon_ref, recon_out_ref, sems.at[pieces])
        recon_copy.start()
        token_ref[...] = jnp.zeros_like(token_ref)
        turned = codes_ref[...].T
        copies = []
        for piece in range(pieces):
            columns = pl.ds(piece * size, size)
            resid = jnp.concatenate([a_ref[:, columns], b_ref[:, columns]], axis=0)
            buffer[:, columns] = jnp.dot(turned, resid, preferred_element_type=jnp.float32).astype(jnp.bfloat16)
            copies.append(pltpu.make_async_copy(buffer.at[:, columns], grad_ref.at[:, columns], sems.at[piece]))
            copies[-1].start()
        for copy in copies:
            copy.wait()
        recon_copy.wait()

    return pl.pallas_call(
        kernel,
        out_shape=[
            jax.ShapeDtypeStruct((latents, width), jnp.bfloat16),
            jax.ShapeDtypeStruct(recon.shape, jnp.bfloat16),
            vmem(*TOKEN),
        ],
        in_specs=[VMEM] * 5,
        out_specs=[HBM, HBM, VMEM],
        scratch_shapes=[pltpu.VMEM((latents, width), jnp.bfloat16), pltpu.SemaphoreType.DMA((pieces + 1,))],
        compiler_params=pltpu.CompilerParams(vmem_limit_bytes=LIMIT),
        cost_estimate=pl.CostEstimate(flops=2 * rows * latents * width, bytes_accessed=4 * latents * width, transcendentals=0),
        name="dec_gradient",
    )(*[in_vmem(a) for a in (codes, resid_a, resid_b, recon, after)])


def enc_gradient(centered, code_grad, total, after, pieces=4):
    rows, width = centered.shape
    latents = code_grad.shape[1]
    size = width // pieces

    def kernel(centered_ref, code_grad_ref, total_ref, after_ref, grad_ref, total_out_ref, token_ref, buffer, sems):
        total_copy = pltpu.make_async_copy(total_ref, total_out_ref, sems.at[pieces])
        total_copy.start()
        token_ref[...] = jnp.zeros_like(token_ref)
        copies = []
        for piece in range(pieces):
            part = pl.ds(piece * size, size)
            buffer[part] = lax.dot_general(
                centered_ref[:, part], code_grad_ref[...], CONTRACT_FIRST, preferred_element_type=jnp.float32
            ).astype(jnp.bfloat16)
            copies.append(pltpu.make_async_copy(buffer.at[part], grad_ref.at[part], sems.at[piece]))
            copies[-1].start()
        for copy in copies:
            copy.wait()
        total_copy.wait()

    return pl.pallas_call(
        kernel,
        out_shape=[
            jax.ShapeDtypeStruct((width, latents), jnp.bfloat16),
            jax.ShapeDtypeStruct(total.shape, jnp.float32),
            vmem(*TOKEN),
        ],
        in_specs=[VMEM] * 4,
        out_specs=[HBM, HBM, VMEM],
        scratch_shapes=[pltpu.VMEM((width, latents), jnp.bfloat16), pltpu.SemaphoreType.DMA((pieces + 1,))],
        compiler_params=pltpu.CompilerParams(vmem_limit_bytes=LIMIT),
        cost_estimate=pl.CostEstimate(flops=2 * rows * latents * width, bytes_accessed=4 * latents * width, transcendentals=0),
        name="enc_gradient",
    )(*[in_vmem(a) for a in (centered, code_grad, total, after)])


def add(terms, other, after=()):
    def kernel(terms_ref, other_ref, sum_ref):
        sum_ref[...] = terms_ref[...] + other_ref[...]

    return run(kernel, "add", [(terms.shape, jnp.float32)], [terms, other], after)[0]


def finish(terms, other, width):
    def kernel(terms_ref, other_ref, bias_ref, loss_ref):
        total = terms_ref[...] + other_ref[...]
        bias_ref[...] = total[:, :width]
        loss_ref[...] = total[:, width : width + 1] / width

    return pl.pallas_call(
        kernel,
        out_shape=[jax.ShapeDtypeStruct((1, width), jnp.float32), jax.ShapeDtypeStruct((1, 1), jnp.float32)],
        in_specs=[VMEM] * 2,
        out_specs=[VMEM] * 2,
        compiler_params=pltpu.CompilerParams(vmem_limit_bytes=2 << 20),
        name="finish",
    )(in_vmem(terms), in_vmem(other))


def local(residuals, enc_weight, enc_bias, dec_weight, dec_bias):
    own_rows, width = residuals.shape
    lat = lax.axis_size("lat")
    row_count = own_rows * lat * lax.axis_size("sub")
    far, steps = plan(lat)

    enc_vmem, own, dec_bias_row, enc_bias_row = load(
        [enc_weight, residuals, dec_bias.reshape(1, width), enc_bias.reshape(1, -1)]
    )
    paired = stack([own, swap(residuals, far)], after=[enc_vmem])
    (dec_vmem,) = load([dec_weight], after=[paired])
    rows_a = gather(paired, steps, after=[dec_vmem])
    rows_b = swap(rows_a, CORES)
    centered, active, codes_bf, keep, send, code_sum = encode_decode(
        rows_a, rows_b, enc_vmem, enc_bias_row, dec_vmem, dec_bias_row
    )

    summed = halve(keep, [swap(send, CORES)], steps[::-1])
    recon, resid_bf, own_bias, square = residual_gradient(
        summed, swap(summed, far), paired, dec_bias_row, row_count
    )

    resid_a = gather(resid_bf, steps)
    resid_b = swap(resid_a, CORES)
    code_grad_bf, total = backward(resid_a, resid_b, dec_vmem, active, row_count)
    terms = bias_product(total, enc_vmem, own_bias, square, code_sum, row_count)

    bits = [1 << b for b in range(lat.bit_length() - 1)]
    terms = add(terms, swap(terms, CORES))
    grad_enc, grad_enc_bias, enc_done = enc_gradient(centered, code_grad_bf, total, after=terms)
    for mask in bits[:-2]:
        terms = add(terms, swap(terms, mask), after=[enc_done])
    grad_dec, recon_out, dec_done = dec_gradient(codes_bf, resid_a, resid_b, recon, after=terms)
    terms = add(terms, swap(terms, bits[-2]), after=[dec_done])
    grad_dec_bias, loss_value = finish(terms, swap(terms, bits[-1]), width)
    return recon_out, loss_value[0], grad_enc, grad_enc_bias[0], grad_dec, grad_dec_bias[0]


def solution(mesh):
    placed = (
        P(("parts", "lat", "sub"), None),
        P(None, ("parts", "lat", "sub")),
        P(("parts", "lat", "sub")),
        P(("parts", "lat", "sub"), None),
        P("parts"),
    )
    return jax.shard_map(
        local,
        mesh=mesh,
        in_specs=placed,
        out_specs=(
            P(("parts", "lat", "sub"), None),
            P("parts"),
            P(None, ("parts", "lat", "sub")),
            P(("parts", "lat", "sub")),
            P(("parts", "lat", "sub"), None),
            P("parts"),
        ),
        check_vma=False,
    )
```

time: 69.7 us -> 57.7 us (0.83)
  local copies, waits for them, and re-layouts: 8.46 us -> 0 us
  Pallas kernels: 4.45 us -> 11.9 us
  matrix products: 4.74 us -> 0 us
  between operations: 3.81 us -> 0.74 us
  other arithmetic: 2.49 us -> 0 us
  starting transfers between devices: 22.2 us -> 20.8 us
  waiting for transfers between devices: 23.2 us -> 24.2 us
    pallas_call x2 -> x17, Pallas kernels: 4.45 us -> 11.9 us  [the longest x12 3.74 us: run(): pl.pallas_call(body, out_shape=[vmem(*out) for out in outs], in_specs=[VM...]
    unnamed x12 -> x0, local copies, waits for them, and re-layouts: 6.63 us -> none
    dot_general x2 -> x0, matrix products: 4.74 us -> none  [the longest x1 2.38 us: local(): lax.dot_general(centered, code_grad_bf, (((0,), (0,)), ((), ())), preferr...]
    slice x5 -> x0, local copies, waits for them, and re-layouts: 1.82 us -> none  [the longest x1 0.62 us: local(): recon_f[:own_rows].astype(jnp.bfloat16)]
    ppermute x4, waiting for transfers between devices: 3.75 us -> 5.3 us  [swap(): return lax.ppermute(values, 'sub', [(i, i ^ 1) for i in range(2)])]
    reduce_sum x3 -> x0, other arithmetic: 1.29 us -> none  [the longest x1 0.64 us: local(): sq_total = jnp.sum(own_error * own_error)]
    ppermute x14, starting transfers between devices: 21.3 us -> 20.2 us  [swap(): lax.ppermute(values, 'lat', [(i, i ^ mask) for i in range(lax.axis_size('...]
    concatenate x3 -> x0, other arithmetic: 0.98 us -> none  [gather(): jnp.concatenate([rows] + [swap(rows, mask) for mask in masks], axis=0)]
  transfers between devices with their start and end apart: 18 -> 18, of which waited for: 16 -> 17; matrix products, arithmetic and copies ran while one was open for 10% -> 0% of each run, Pallas kernels for 0% -> 13%
where the time goes in v3:
time: 57.7 us; the launch traced here: 57.6 us
  waiting for transfers between devices  24.2 us (42%)
  starting transfers between devices  20.8 us (36%)
  Pallas kernels  11.9 us (21%)
  between operations  0.74 us (1%)
    ppermute x14, starting transfers between devices, swap(): lax.ppermute(values, 'lat', [(i, i ^ mask) for i in range(lax.axis_size('...  20.2 us
    ppermute x14, waiting for transfers between devices, swap(): lax.ppermute(values, 'lat', [(i, i ^ mask) for i in range(lax.axis_size('...  18.9 us
    ppermute x4, waiting for transfers between devices, swap(): return lax.ppermute(values, 'sub', [(i, i ^ 1) for i in range(2)])  5.3 us
    pallas_call x12, Pallas kernels, run(): pl.pallas_call(body, out_shape=[vmem(*out) for out in outs], in_specs=[VM...  3.74 us
    pallas_call x2, Pallas kernels, load(): pl.pallas_call(kernel, out_shape=[vmem(array.shape, array.dtype) for arra...  3.53 us
    pallas_call x1, Pallas kernels, enc_gradient(): pl.pallas_call(kernel, out_shape=[jax.ShapeDtypeStruct((width, latents),...  2.07 us
    pallas_call x1, Pallas kernels, dec_gradient(): pl.pallas_call(kernel, out_shape=[jax.ShapeDtypeStruct((latents, width),...  1.91 us
  transfers between devices with their start and end apart: 18, of which 17 were waited for; matrix products, arithmetic and copies ran while one was open for 0% of the time, Pallas kernels for 13%

profile of v3, /device:TPU:0, one launch (start us, length us, event | category | flops | bytes accessed | tf_op | source)
XLA Modules:
  0.0 57.6 jit_solution(15286909535335640936)
XLA Ops:
  0.6 4.1 %collective-permute-start = (bf16[2,5120]{1,0:T(2,128)(2,1)}, bf16[2,5120]{1,0:T(2,128)(2,1)S(1)}, u32[]{:S(2)}, u32[]{:S(2)}) collective-permute-start(bf16[2,5120]{1,0:T(2,128)(2,1)} %refs_1_.1), channel_id=1, source_target_pairs={{0,8},{2,10},{4,12},{6,14},{8,0},{10,2},{12,4},{14,6},{1,9},{3,11}... | collective-permute-start | bytes 61448 | tf_op jit(solution)/shard_map/ppermute | solution.py:53
  4.7 1.8 %load.2 = (bf16[5120,256]{1,0:T(8,128)(2,1)S(1)}, bf16[2,5120]{1,0:T(2,128)(2,1)S(1)}, f32[1,5120]{1,0:T(1,128)S(1)}, f32[1,256]{1,0:T(1,128)S(1)}) custom-call(bf16[5120,256]{1,0:T(8,128)(2,1)} %refs_0_.2, bf16[2,5120]{1,0:T(2,128)(2,1)} %refs_1_.1, f32[1,5120]{1,0:T(1,128)} %bitcast.5, f32[1,256]{1,0:T(1,128)} %bitcast.6), custom_call_target="tpu_custom_call" | custom-call | bytes 5326848 | tf_op jit(solution)/shard_map/load/pallas_call | solution.py:75
  6.8 2.9 %collective-permute-start.3 = (bf16[4,5120]{1,0:T(4,128)(2,1)S(1)}, bf16[4,5120]{1,0:T(4,128)(2,1)S(1)}, u32[]{:S(2)}, u32[]{:S(2)}) collective-permute-start(bf16[4,5120]{1,0:T(4,128)(2,1)S(1)} %stack.3.refs_1_.refs_0_.refs_2_), channel_id=1, source_target_pairs={{0,6},{2,4},{4,2},{6,0},{8,14},{10,12},{12,10},{14,8},{1,7},{3,5},... | collective-permute-start | bytes 122888 | tf_op jit(solution)/shard_map/ppermute | solution.py:53
  10.3 1.7 %load.3.refs_4_.refs_2_ = bf16[256,5120]{1,0:T(8,128)(2,1)S(1)} custom-call(bf16[256,5120]{1,0:T(8,128)(2,1)} %refs_0_.3, bf16[4,5120]{1,0:T(4,128)(2,1)S(1)} %stack.3.refs_1_.refs_0_.refs_2_), custom_call_target="tpu_custom_call" | custom-call | bytes 5242880 | tf_op jit(solution)/shard_map/load/pallas_call | solution.py:75
  12.1 1.6 %collective-permute-done.2.refs_2_ = bf16[4,5120]{1,0:T(4,128)(2,1)S(1)} collective-permute-done((bf16[4,5120]{1,0:T(4,128)(2,1)S(1)}, bf16[4,5120]{1,0:T(4,128)(2,1)S(1)}, u32[]{:S(2)}, u32[]{:S(2)}) %collective-permute-start.2) | collective-permute-done | bytes 40992 | tf_op jit(solution)/shard_map/ppermute | solution.py:53
  13.6 0.5 collective-permute-done.1.refs_1_
  14.3 1.4 %collective-permute-done.4.refs_1_ = bf16[16,5120]{1,0:T(8,128)(2,1)S(1)} collective-permute-done((bf16[16,5120]{1,0:T(8,128)(2,1)S(1)}, bf16[16,5120]{1,0:T(8,128)(2,1)S(1)}, u32[]{:S(2)}, u32[]{:S(2)}) %collective-permute-start.4) | collective-permute-done | bytes 163872 | tf_op jit(solution)/shard_map/ppermute | solution.py:52
  15.7 1.6 %encode_decode.1 = (bf16[32,5120]{1,0:T(8,128)(2,1)S(1)}, f32[32,256]{1,0:T(8,128)S(1)}, bf16[32,256]{1,0:T(8,128)(2,1)S(1)}, f32[16,5120]{1,0:T(8,128)S(1)}, f3...) custom-call(bf16[16,5120]{1,0:T(8,128)(2,1)S(1)} %stack.4.refs_0_, bf16[16,5120]{1,0:T(8,128)(2,1)S(1)} %collective-permute-done.4.refs_1_, ...), custom_call_target="tpu_custom_call" | custom-call | tf_op jit(solution)/shard_map/encode_decode/pallas_call | solution.py:39
  17.5 1.5 %collective-permute-done.5.refs_1_ = f32[16,5120]{1,0:T(8,128)S(1)} collective-permute-done((f32[16,5120]{1,0:T(8,128)S(1)}, f32[16,5120]{1,0:T(8,128)S(1)}, u32[]{:S(2)}, u32[]{:S(2)}) %collective-permute-start.5) | collective-permute-done | bytes 327712 | tf_op jit(solution)/shard_map/ppermute | solution.py:52
  19.2 1.9 %collective-permute-start.7 = (f32[4,5120]{1,0:T(4,128)S(1)}, f32[4,5120]{1,0:T(4,128)S(1)}, u32[]{:S(2)}, u32[]{:S(2)}) collective-permute-start(f32[4,5120]{1,0:T(4,128)S(1)} %get-tuple-element.43), channel_id=1, source_target_pairs={{0,4},{2,6},{4,0},{6,2},{8,12},{10,14},{12,8},{14,10},{1,5},{3,7},... | collective-permute-start | bytes 245768 | tf_op jit(solution)/shard_map/ppermute | solution.py:53
  21.1 1.5 %collective-permute-start.8 = (f32[4,5120]{1,0:T(4,128)S(1)}, f32[4,5120]{1,0:T(4,128)S(1)}, u32[]{:S(2)}, u32[]{:S(2)}) collective-permute-start(f32[4,5120]{1,0:T(4,128)S(1)} %get-tuple-element.44), channel_id=1, source_target_pairs={{0,6},{2,4},{4,2},{6,0},{8,14},{10,12},{12,10},{14,8},{1,7},{3,5},... | collective-permute-start | bytes 245768 | tf_op jit(solution)/shard_map/ppermute | solution.py:53
  22.6 1.0 %collective-permute-done.6.refs_1_ = f32[4,5120]{1,0:T(4,128)S(1)} collective-permute-done((f32[4,5120]{1,0:T(4,128)S(1)}, f32[4,5120]{1,0:T(4,128)S(1)}, u32[]{:S(2)}, u32[]{:S(2)}) %collective-permute-start.6) | collective-permute-done | bytes 81952 | tf_op jit(solution)/shard_map/ppermute | solution.py:53
  23.8 2.9 %collective-permute-done.8.refs_3_ = f32[4,5120]{1,0:T(4,128)S(1)} collective-permute-done((f32[4,5120]{1,0:T(4,128)S(1)}, f32[4,5120]{1,0:T(4,128)S(1)}, u32[]{:S(2)}, u32[]{:S(2)}) %collective-permute-start.8) | collective-permute-done | bytes 81952 | tf_op jit(solution)/shard_map/ppermute | solution.py:53
  26.8 2.6 %collective-permute-start.9 = (f32[4,5120]{1,0:T(4,128)S(1)}, f32[4,5120]{1,0:T(4,128)S(1)}, u32[]{:S(2)}, u32[]{:S(2)}) collective-permute-start(f32[4,5120]{1,0:T(4,128)S(1)} %add_parts.3.refs_0_), channel_id=1, source_target_pairs={{0,8},{2,10},{4,12},{6,14},{8,0},{10,2},{12,4},{14,6},{1,9},{3,11}... | collective-permute-start | bytes 245768 | tf_op jit(solution)/shard_map/ppermute | solution.py:53
  29.3 3.8 %collective-permute-done.9.refs_1_ = f32[4,5120]{1,0:T(4,128)S(1)} collective-permute-done((f32[4,5120]{1,0:T(4,128)S(1)}, f32[4,5120]{1,0:T(4,128)S(1)}, u32[]{:S(2)}, u32[]{:S(2)}) %collective-permute-start.9) | collective-permute-done | bytes 81952 | tf_op jit(solution)/shard_map/ppermute | solution.py:53
  33.4 0.7 %collective-permute-start.12 = (bf16[4,5120]{1,0:T(4,128)(2,1)S(1)}, bf16[4,5120]{1,0:T(4,128)(2,1)S(1)}, u32[]{:S(2)}, u32[]{:S(2)}) collective-permute-start(bf16[4,5120]{1,0:T(4,128)(2,1)S(1)} %get-tuple-element.45.refs_0_), channel_id=1, source_target_pairs={{0,6},{2,4},{4,2},{6,0},{8,14},{10,12},{12,10},{14,8},{1,7},{3,5},... | collective-permute-start | bytes 122888 | tf_op jit(solution)/shard_map/ppermute | solution.py:53
  34.1 2.0 %collective-permute-start.11 = (bf16[4,5120]{1,0:T(4,128)(2,1)S(1)}, bf16[4,5120]{1,0:T(4,128)(2,1)S(1)}, u32[]{:S(2)}, u32[]{:S(2)}) collective-permute-start(bf16[4,5120]{1,0:T(4,128)(2,1)S(1)} %get-tuple-element.45.refs_0_), channel_id=1, source_target_pairs={{0,4},{2,6},{4,0},{6,2},{8,12},{10,14},{12,8},{14,10},{1,5},{3,7},... | collective-permute-start | bytes 122888 | tf_op jit(solution)/shard_map/ppermute | solution.py:53
  36.0 0.9 %collective-permute-start.10 = (bf16[4,5120]{1,0:T(4,128)(2,1)S(1)}, bf16[4,5120]{1,0:T(4,128)(2,1)S(1)}, u32[]{:S(2)}, u32[]{:S(2)}) collective-permute-start(bf16[4,5120]{1,0:T(4,128)(2,1)S(1)} %get-tuple-element.45.refs_0_), channel_id=1, source_target_pairs={{0,2},{2,0},{4,6},{6,4},{8,10},{10,8},{12,14},{14,12},{1,3},{3,1},... | collective-permute-start | bytes 122888 | tf_op jit(solution)/shard_map/ppermute | solution.py:53
  37.0 1.4 %collective-permute-done.12.refs_3_ = bf16[4,5120]{1,0:T(4,128)(2,1)S(1)} collective-permute-done((bf16[4,5120]{1,0:T(4,128)(2,1)S(1)}, bf16[4,5120]{1,0:T(4,128)(2,1)S(1)}, u32[]{:S(2)}, u32[]{:S(2)}) %collective-permute-start.12) | collective-permute-done | bytes 40992 | tf_op jit(solution)/shard_map/ppermute | solution.py:53
  38.5 1.6 %collective-permute-done.10.refs_1_ = bf16[4,5120]{1,0:T(4,128)(2,1)S(1)} collective-permute-done((bf16[4,5120]{1,0:T(4,128)(2,1)S(1)}, bf16[4,5120]{1,0:T(4,128)(2,1)S(1)}, u32[]{:S(2)}, u32[]{:S(2)}) %collective-permute-start.10) | collective-permute-done | bytes 40992 | tf_op jit(solution)/shard_map/ppermute | solution.py:53
  40.2 1.4 %collective-permute-done.13.refs_1_.b_ref = bf16[16,5120]{1,0:T(8,128)(2,1)S(1)} collective-permute-done((bf16[16,5120]{1,0:T(8,128)(2,1)S(1)}, bf16[16,5120]{1,0:T(8,128)(2,1)S(1)}, u32[]{:S(2)}, u32[]{:S(2)}) %collective-permute-start.13) | collective-permute-done | bytes 163872 | tf_op jit(solution)/shard_map/ppermute | solution.py:52
  41.6 0.9 %backward.1 = (bf16[32,256]{1,0:T(8,128)(2,1)S(1)}, f32[1,256]{1,0:T(1,128)S(1)}) custom-call(bf16[16,5120]{1,0:T(8,128)(2,1)S(1)} %stack.5.refs_0_.a_ref, bf16[16,5120]{1,0:T(8,128)(2,1)S(1)} %collective-permute-done.13.refs_1_.b_ref, bf16[256,5120]{1,0:T(8,128)(2,1)S(1)} %load.3.refs_4_.refs_2_, f32[32,256]{1,0:T(8,128)S(1)} %get-tuple-element.47.refs_3_), custom_call_target="tpu_custom_call" | custom-call | tf_op jit(solution)/shard_map/backward/pallas_call | solution.py:39
  42.4 0.8 %bias_product.1.refs_0_ = f32[1,5248]{1,0:T(1,128)S(1)} custom-call(f32[1,256]{1,0:T(1,128)S(1)} %get-tuple-element.48.refs_0_.total_ref, bf16[5120,256]{1,0:T(8,128)(2,1)S(1)} %get-tuple-element.35.refs_2_.refs_1_, f32[1,5120]{1,0:T(1,128)S(1)} %get-tuple-element.49.refs_2_, f32[1,128]{1,0:T(1,128)S(1)} %get-tuple-element.50.refs_3_, ...), custom_call_target="tpu_custom_call" | custom-call | tf_op jit(solution)/shard_map/bias_product/pallas_call | solution.py:39
  43.5 1.0 %collective-permute-done.14.refs_1_ = f32[1,5248]{1,0:T(1,128)S(1)} collective-permute-done((f32[1,5248]{1,0:T(1,128)S(1)}, f32[1,5248]{1,0:T(1,128)S(1)}, u32[]{:S(2)}, u32[]{:S(2)}) %collective-permute-start.14) | collective-permute-done | bytes 21024 | tf_op jit(solution)/shard_map/ppermute | solution.py:52
  44.5 0.9 %collective-permute-start.15 = (f32[1,5248]{1,0:T(1,128)S(1)}, f32[1,5248]{1,0:T(1,128)S(1)}, u32[]{:S(2)}, u32[]{:S(2)}) collective-permute-start(f32[1,5248]{1,0:T(1,128)S(1)} %add.3.after_ref.refs_0_), channel_id=1, source_target_pairs={{0,2},{2,0},{4,6},{6,4},{8,10},{10,8},{12,14},{14,12},{1,3},{3,1},... | collective-permute-start | bytes 62984 | tf_op jit(solution)/shard_map/ppermute | solution.py:53
  45.4 2.1 %enc_gradient.1 = (bf16[5120,256]{1,0:T(8,128)(2,1)}, f32[1,256]{1,0:T(1,128)}, f32[8,128]{1,0:T(8,128)S(1)}) custom-call(bf16[32,5120]{1,0:T(8,128)(2,1)S(1)} %get-tuple-element.52.centered_ref, bf16[32,256]{1,0:T(8,128)(2,1)S(1)} %get-tuple-element.53.code_grad_ref, f32[1,256]{1,0:T(1,128)S(1)} %get-tuple-element.48.refs_0_.total_ref, ...), custom_call_target="tpu_custom_call" | custom-call | flops 83886080 | bytes 5242880 | tf_op jit(solution)/shard_map/enc_gradient/pallas_call | solution.py:286
  47.5 0.8 %collective-permute-done.15.refs_1_ = f32[1,5248]{1,0:T(1,128)S(1)} collective-permute-done((f32[1,5248]{1,0:T(1,128)S(1)}, f32[1,5248]{1,0:T(1,128)S(1)}, u32[]{:S(2)}, u32[]{:S(2)}) %collective-permute-start.15) | collective-permute-done | bytes 21024 | tf_op jit(solution)/shard_map/ppermute | solution.py:53
  48.4 1.9 %dec_gradient.1 = (bf16[256,5120]{1,0:T(8,128)(2,1)}, bf16[2,5120]{1,0:T(2,128)(2,1)}, f32[8,128]{1,0:T(8,128)S(1)}) custom-call(bf16[32,256]{1,0:T(8,128)(2,1)S(1)} %get-tuple-element.38.codes_ref, bf16[16,5120]{1,0:T(8,128)(2,1)S(1)} %stack.5.refs_0_.a_ref, bf16[16,5120]{1,0:T(8,128)(2,1)S(1)} %collective-permute-done.13.refs_1_.b_ref, ...), custom_call_target="tpu_custom_call" | custom-call | flops 83886080 | bytes 5242880 | tf_op jit(solution)/shard_map/dec_gradient/pallas_call | solution.py:249
  50.3 1.8 %collective-permute-done.16.refs_1_ = f32[1,5248]{1,0:T(1,128)S(1)} collective-permute-done((f32[1,5248]{1,0:T(1,128)S(1)}, f32[1,5248]{1,0:T(1,128)S(1)}, u32[]{:S(2)}, u32[]{:S(2)}) %collective-permute-start.16) | collective-permute-done | bytes 21024 | tf_op jit(solution)/shard_map/ppermute | solution.py:53
  52.1 1.9 %collective-permute-start.17 = (f32[1,5248]{1,0:T(1,128)S(1)}, f32[1,5248]{1,0:T(1,128)S(1)}, u32[]{:S(2)}, u32[]{:S(2)}) collective-permute-start(f32[1,5248]{1,0:T(1,128)S(1)} %add.5.terms_ref), channel_id=1, source_target_pairs={{0,8},{2,10},{4,12},{6,14},{8,0},{10,2},{12,4},{14,6},{1,9},{3,11}... | collective-permute-start | bytes 62984 | tf_op jit(solution)/shard_map/ppermute | solution.py:53
  54.0 2.9 %collective-permute-done.17.other_ref = f32[1,5248]{1,0:T(1,128)S(1)} collective-permute-done((f32[1,5248]{1,0:T(1,128)S(1)}, f32[1,5248]{1,0:T(1,128)S(1)}, u32[]{:S(2)}, u32[]{:S(2)}) %collective-permute-start.17) | collective-permute-done | bytes 21024 | tf_op jit(solution)/shard_map/ppermute | solution.py:53
  56.9 0.6 %finish.1 = (f32[1,5120]{1,0:T(1,128)}, f32[1,1]{1,0:T(1,128)}) custom-call(f32[1,5248]{1,0:T(1,128)S(1)} %add.5.terms_ref, f32[1,5248]{1,0:T(1,128)S(1)} %collective-permute-done.17.other_ref), custom_call_target="tpu_custom_call" | custom-call | tf_op jit(solution)/shard_map/finish/pallas_call | solution.py:315
  (21 shorter events, 2.5 us)
Async XLA Ops:
  0.6 6.1 %collective-permute-start = (bf16[2,5120]{1,0:T(2,128)(2,1)}, bf16[2,5120]{1,0:T(2,128)(2,1)S(1)}, u32[]{:S(2)}, u32[]{:S(2)}) collective-permute-start(bf16[2,5120]{1,0:T(2,128)(2,1)} %refs_1_.1), channel_id=1, source_target_pairs={{0,8},{2,10},{4,12},{6,14},{8,0},{10,2},{12,4},{14,6},{1,9},{3,11}... | collective-permute-start | bytes 61448 | tf_op jit(solution)/shard_map/ppermute | solution.py:53
  6.8 5.3 %collective-permute-start.3 = (bf16[4,5120]{1,0:T(4,128)(2,1)S(1)}, bf16[4,5120]{1,0:T(4,128)(2,1)S(1)}, u32[]{:S(2)}, u32[]{:S(2)}) collective-permute-start(bf16[4,5120]{1,0:T(4,128)(2,1)S(1)} %stack.3.refs_1_.refs_0_.refs_2_), channel_id=1, source_target_pairs={{0,6},{2,4},{4,2},{6,0},{8,14},{10,12},{12,10},{14,8},{1,7},{3,5},... | collective-permute-start | bytes 122888 | tf_op jit(solution)/shard_map/ppermute | solution.py:53
  9.6 4.0 %collective-permute-start.2 = (bf16[4,5120]{1,0:T(4,128)(2,1)S(1)}, bf16[4,5120]{1,0:T(4,128)(2,1)S(1)}, u32[]{:S(2)}, u32[]{:S(2)}) collective-permute-start(bf16[4,5120]{1,0:T(4,128)(2,1)S(1)} %stack.3.refs_1_.refs_0_.refs_2_), channel_id=1, source_target_pairs={{0,4},{2,6},{4,0},{6,2},{8,12},{10,14},{12,8},{14,10},{1,5},{3,7},... | collective-permute-start | bytes 122888 | tf_op jit(solution)/shard_map/ppermute | solution.py:53
  10.2 4.0 %collective-permute-start.1 = (bf16[4,5120]{1,0:T(4,128)(2,1)S(1)}, bf16[4,5120]{1,0:T(4,128)(2,1)S(1)}, u32[]{:S(2)}, u32[]{:S(2)}) collective-permute-start(bf16[4,5120]{1,0:T(4,128)(2,1)S(1)} %stack.3.refs_1_.refs_0_.refs_2_), channel_id=1, source_target_pairs={{0,2},{2,0},{4,6},{6,4},{8,10},{10,8},{12,14},{14,12},{1,3},{3,1},... | collective-permute-start | bytes 122888 | tf_op jit(solution)/shard_map/ppermute | solution.py:53
  14.3 1.5 %collective-permute-start.4 = (bf16[16,5120]{1,0:T(8,128)(2,1)S(1)}, bf16[16,5120]{1,0:T(8,128)(2,1)S(1)}, u32[]{:S(2)}, u32[]{:S(2)}) collective-permute-start(bf16[16,5120]{1,0:T(8,128)(2,1)S(1)} %stack.4.refs_0_), channel_id=1, source_target_pairs={{0,1},{1,0},{2,3},{3,2},{4,5},{5,4},{6,7},{7,6},{8,9},{9,8},{10,11... | collective-permute-start | bytes 491528 | tf_op jit(solution)/shard_map/ppermute | solution.py:52
  17.3 1.7 %collective-permute-start.5 = (f32[16,5120]{1,0:T(8,128)S(1)}, f32[16,5120]{1,0:T(8,128)S(1)}, u32[]{:S(2)}, u32[]{:S(2)}) collective-permute-start(f32[16,5120]{1,0:T(8,128)S(1)} %get-tuple-element.40), channel_id=1, source_target_pairs={{0,1},{1,0},{2,3},{3,2},{4,5},{5,4},{6,7},{7,6},{8,9},{9,8},{10,11... | collective-permute-start | bytes 983048 | tf_op jit(solution)/shard_map/ppermute | solution.py:52
  19.0 4.6 %collective-permute-start.6 = (f32[4,5120]{1,0:T(4,128)S(1)}, f32[4,5120]{1,0:T(4,128)S(1)}, u32[]{:S(2)}, u32[]{:S(2)}) collective-permute-start(f32[4,5120]{1,0:T(4,128)S(1)} %get-tuple-element.42), channel_id=1, source_target_pairs={{0,2},{2,0},{4,6},{6,4},{8,10},{10,8},{12,14},{14,12},{1,3},{3,1},... | collective-permute-start | bytes 245768 | tf_op jit(solution)/shard_map/ppermute | solution.py:53
  19.2 4.6 %collective-permute-start.7 = (f32[4,5120]{1,0:T(4,128)S(1)}, f32[4,5120]{1,0:T(4,128)S(1)}, u32[]{:S(2)}, u32[]{:S(2)}) collective-permute-start(f32[4,5120]{1,0:T(4,128)S(1)} %get-tuple-element.43), channel_id=1, source_target_pairs={{0,4},{2,6},{4,0},{6,2},{8,12},{10,14},{12,8},{14,10},{1,5},{3,7},... | collective-permute-start | bytes 245768 | tf_op jit(solution)/shard_map/ppermute | solution.py:53
  21.1 5.6 %collective-permute-start.8 = (f32[4,5120]{1,0:T(4,128)S(1)}, f32[4,5120]{1,0:T(4,128)S(1)}, u32[]{:S(2)}, u32[]{:S(2)}) collective-permute-start(f32[4,5120]{1,0:T(4,128)S(1)} %get-tuple-element.44), channel_id=1, source_target_pairs={{0,6},{2,4},{4,2},{6,0},{8,14},{10,12},{12,10},{14,8},{1,7},{3,5},... | collective-permute-start | bytes 245768 | tf_op jit(solution)/shard_map/ppermute | solution.py:53
  26.8 6.4 %collective-permute-start.9 = (f32[4,5120]{1,0:T(4,128)S(1)}, f32[4,5120]{1,0:T(4,128)S(1)}, u32[]{:S(2)}, u32[]{:S(2)}) collective-permute-start(f32[4,5120]{1,0:T(4,128)S(1)} %add_parts.3.refs_0_), channel_id=1, source_target_pairs={{0,8},{2,10},{4,12},{6,14},{8,0},{10,2},{12,4},{14,6},{1,9},{3,11}... | collective-permute-start | bytes 245768 | tf_op jit(solution)/shard_map/ppermute | solution.py:53
  33.4 5.0 %collective-permute-start.12 = (bf16[4,5120]{1,0:T(4,128)(2,1)S(1)}, bf16[4,5120]{1,0:T(4,128)(2,1)S(1)}, u32[]{:S(2)}, u32[]{:S(2)}) collective-permute-start(bf16[4,5120]{1,0:T(4,128)(2,1)S(1)} %get-tuple-element.45.refs_0_), channel_id=1, source_target_pairs={{0,6},{2,4},{4,2},{6,0},{8,14},{10,12},{12,10},{14,8},{1,7},{3,5},... | collective-permute-start | bytes 122888 | tf_op jit(solution)/shard_map/ppermute | solution.py:53
  34.1 4.4 %collective-permute-start.11 = (bf16[4,5120]{1,0:T(4,128)(2,1)S(1)}, bf16[4,5120]{1,0:T(4,128)(2,1)S(1)}, u32[]{:S(2)}, u32[]{:S(2)}) collective-permute-start(bf16[4,5120]{1,0:T(4,128)(2,1)S(1)} %get-tuple-element.45.refs_0_), channel_id=1, source_target_pairs={{0,4},{2,6},{4,0},{6,2},{8,12},{10,14},{12,8},{14,10},{1,5},{3,7},... | collective-permute-start | bytes 122888 | tf_op jit(solution)/shard_map/ppermute | solution.py:53
  36.0 4.0 %collective-permute-start.10 = (bf16[4,5120]{1,0:T(4,128)(2,1)S(1)}, bf16[4,5120]{1,0:T(4,128)(2,1)S(1)}, u32[]{:S(2)}, u32[]{:S(2)}) collective-permute-start(bf16[4,5120]{1,0:T(4,128)(2,1)S(1)} %get-tuple-element.45.refs_0_), channel_id=1, source_target_pairs={{0,2},{2,0},{4,6},{6,4},{8,10},{10,8},{12,14},{14,12},{1,3},{3,1},... | collective-permute-start | bytes 122888 | tf_op jit(solution)/shard_map/ppermute | solution.py:53
  40.1 1.5 %collective-permute-start.13 = (bf16[16,5120]{1,0:T(8,128)(2,1)S(1)}, bf16[16,5120]{1,0:T(8,128)(2,1)S(1)}, u32[]{:S(2)}, u32[]{:S(2)}) collective-permute-start(bf16[16,5120]{1,0:T(8,128)(2,1)S(1)} %stack.5.refs_0_.a_ref), channel_id=1, source_target_pairs={{0,1},{1,0},{2,3},{3,2},{4,5},{5,4},{6,7},{7,6},{8,9},{9,8},{10,11... | collective-permute-start | bytes 491528 | tf_op jit(solution)/shard_map/ppermute | solution.py:52
  43.2 1.3 %collective-permute-start.14 = (f32[1,5248]{1,0:T(1,128)S(1)}, f32[1,5248]{1,0:T(1,128)S(1)}, u32[]{:S(2)}, u32[]{:S(2)}) collective-permute-start(f32[1,5248]{1,0:T(1,128)S(1)} %bias_product.1.refs_0_), channel_id=1, source_target_pairs={{0,1},{1,0},{2,3},{3,2},{4,5},{5,4},{6,7},{7,6},{8,9},{9,8},{10,11... | collective-permute-start | bytes 62984 | tf_op jit(solution)/shard_map/ppermute | solution.py:52
  44.5 3.8 %collective-permute-start.15 = (f32[1,5248]{1,0:T(1,128)S(1)}, f32[1,5248]{1,0:T(1,128)S(1)}, u32[]{:S(2)}, u32[]{:S(2)}) collective-permute-start(f32[1,5248]{1,0:T(1,128)S(1)} %add.3.after_ref.refs_0_), channel_id=1, source_target_pairs={{0,2},{2,0},{4,6},{6,4},{8,10},{10,8},{12,14},{14,12},{1,3},{3,1},... | collective-permute-start | bytes 62984 | tf_op jit(solution)/shard_map/ppermute | solution.py:53
  48.3 3.8 %collective-permute-start.16 = (f32[1,5248]{1,0:T(1,128)S(1)}, f32[1,5248]{1,0:T(1,128)S(1)}, u32[]{:S(2)}, u32[]{:S(2)}) collective-permute-start(f32[1,5248]{1,0:T(1,128)S(1)} %add.4.after_ref.refs_0_), channel_id=1, source_target_pairs={{0,4},{2,6},{4,0},{6,2},{8,12},{10,14},{12,8},{14,10},{1,5},{3,7},... | collective-permute-start | bytes 62984 | tf_op jit(solution)/shard_map/ppermute | solution.py:53
  52.1 4.8 %collective-permute-start.17 = (f32[1,5248]{1,0:T(1,128)S(1)}, f32[1,5248]{1,0:T(1,128)S(1)}, u32[]{:S(2)}, u32[]{:S(2)}) collective-permute-start(f32[1,5248]{1,0:T(1,128)S(1)} %add.5.terms_ref), channel_id=1, source_target_pairs={{0,8},{2,10},{4,12},{6,14},{8,0},{10,2},{12,4},{14,6},{1,9},{3,11}... | collective-permute-start | bytes 62984 | tf_op jit(solution)/shard_map/ppermute | solution.py:53

commit v4 on v3

v4 whole, which is shorter than its diff:
```python
import jax
import jax.numpy as jnp
from jax import lax
from jax.experimental import pallas as pl
from jax.experimental.pallas import tpu as pltpu
from jax.sharding import PartitionSpec as P

PENALTY = 0.2
CORES = 0
LANES = 128
LIMIT = 12 << 20
VMEM = pl.BlockSpec(memory_space=pltpu.VMEM)
HBM = pl.BlockSpec(memory_space=pltpu.HBM)
CONTRACT_FIRST = (((0,), (0,)), ((), ()))


def vmem(shape, dtype):
    return pltpu.VMEM(shape, dtype)


def in_vmem(array):
    return pltpu.with_memory_space_constraint(array, pltpu.VMEM)


def in_hbm(array):
    return pltpu.with_memory_space_constraint(array, pltpu.HBM)


TOKEN = ((8, LANES), jnp.float32)


def run(kernel, name, outs, args, after=(), flops=0, moved=0, limit=LIMIT):
    count = len(args)

    def body(*refs):
        kernel(*refs[:count], *refs[count + len(after) :])

    return pl.pallas_call(
        body,
        out_shape=[vmem(*out) for out in outs],
        in_specs=[VMEM] * (count + len(after)),
        out_specs=[VMEM] * len(outs),
        compiler_params=pltpu.CompilerParams(vmem_limit_bytes=limit),
        cost_estimate=pl.CostEstimate(flops=flops, bytes_accessed=moved, transcendentals=0),
        name=name,
    )(*[in_vmem(a) for a in args], *[in_vmem(a) for a in after])


def swap(values, mask):
    if mask == CORES:
        return lax.ppermute(values, "sub", [(i, i ^ 1) for i in range(2)])
    return lax.ppermute(values, "lat", [(i, i ^ mask) for i in range(lax.axis_size("lat"))])


ROWS_ORDER, SUM_ORDER, RESID_ORDER, TERMS_ORDER = (3, 1, 2), (2, 1, 3), (3, 1, 2), (3, 1, 2)


def plan(lat):
    bits = [1 << b for b in range(lat.bit_length() - 1)]
    near = bits[:-1]
    steps = [[1, 2, 3]] + [[b] for b in near[2:]] if len(near) > 1 else [[b] for b in near]
    return bits[-1], steps


def load(arrays, after=()):
    count = len(arrays)

    def kernel(*refs):
        copies = [
            pltpu.make_async_copy(refs[i], refs[count + len(after) + i], refs[-1].at[i]) for i in range(count)
        ]
        for copy in copies:
            copy.start()
        for copy in copies:
            copy.wait()

    return pl.pallas_call(
        kernel,
        out_shape=[vmem(array.shape, array.dtype) for array in arrays],
        in_specs=[HBM] * count + [VMEM] * len(after),
        out_specs=[VMEM] * count,
        scratch_shapes=[pltpu.SemaphoreType.DMA((count,))],
        compiler_params=pltpu.CompilerParams(vmem_limit_bytes=LIMIT),
        cost_estimate=pl.CostEstimate(
            flops=0, bytes_accessed=2 * sum(a.size * a.dtype.itemsize for a in arrays), transcendentals=0
        ),
        name="load",
    )(*[in_hbm(a) for a in arrays], *[in_vmem(a) for a in after])


def stack(blocks, after=(), order=None):
    width = blocks[0].shape[1]
    order = order or list(range(len(blocks)))

    def kernel(*refs):
        refs[-1][...] = jnp.concatenate([refs[order.index(i)][...] for i in range(len(blocks))], axis=0)

    shape = (sum(block.shape[0] for block in blocks), width)
    return run(kernel, "stack", [(shape, blocks[0].dtype)], [blocks[i] for i in order], after)[0]


def gather(rows, steps, order, after=()):
    for masks in steps:
        rows = stack([rows] + [swap(rows, mask) for mask in masks], after, [0, *order] if len(masks) > 1 else None)
    return rows


def add_parts(first, others, count, after=()):
    rows, width = first.shape
    size = rows // count

    def kernel(*refs):
        total = refs[0][...]
        for ref in refs[1 : 1 + len(others)]:
            total = total + ref[...]
        for part, ref in enumerate(refs[1 + len(others) :]):
            ref[...] = total[part * size : (part + 1) * size]

    return run(kernel, "add_parts", [((size, width), jnp.float32)] * count, [first, *others], after)


def halve(first, others, steps, dec_weight):
    for masks in steps:
        parts = add_parts(first, others, len(masks) + 1)
        dec_turned = turn(dec_weight, [parts[0]])
        first, others = parts[0], [swap(part, mask) for part, mask in zip(parts[1:], masks)]
        if len(masks) > 1:
            others = [others[mask - 1] for mask in SUM_ORDER]
    return add_parts(first, others, 1, after=[dec_turned])[0], dec_turned


def encode_rows(rows, weight, bias, dec_bias):
    centered = (rows.astype(jnp.float32) - dec_bias).astype(jnp.bfloat16)
    preact = jnp.dot(centered, weight, preferred_element_type=jnp.float32) + bias
    active = jnp.maximum(preact, 0.0)
    return centered, active, (active * active).astype(jnp.bfloat16)


def encoded(half, width, latents):
    return [((half, width), jnp.bfloat16), ((half, latents), jnp.float32), ((half, latents), jnp.bfloat16)]


def encode(rows, enc_weight, enc_bias, dec_bias):
    half, width = rows.shape
    latents = enc_weight.shape[1]

    def kernel(rows_ref, enc_ref, enc_bias_ref, dec_bias_ref, *outs):
        for ref, values in zip(outs, encode_rows(rows_ref[...], enc_ref[...], enc_bias_ref[...], dec_bias_ref[...])):
            ref[...] = values

    return run(
        kernel,
        "encode",
        encoded(half, width, latents),
        [rows, enc_weight, enc_bias, dec_bias],
        flops=2 * half * width * latents,
    )


def encode_decode(rows, codes, enc_weight, enc_bias, dec_weight, dec_bias):
    half, width = rows.shape
    latents = enc_weight.shape[1]

    def kernel(rows_ref, codes_ref, enc_ref, enc_bias_ref, dec_ref, dec_bias_ref, *outs):
        results = encode_rows(rows_ref[...], enc_ref[...], enc_bias_ref[...], dec_bias_ref[...])
        both = jnp.concatenate([codes_ref[...], results[2]], axis=0)
        partial = jnp.dot(both, dec_ref[...], preferred_element_type=jnp.float32)
        for ref, values in zip(outs, [*results, partial[:half], partial[half:]]):
            ref[...] = values

    return run(
        kernel,
        "encode_decode",
        encoded(half, width, latents) + [((half, width), jnp.float32)] * 2,
        [rows, codes, enc_weight, enc_bias, dec_weight, dec_bias],
    )


def code_sum(active_a, active_b):
    def kernel(a_ref, b_ref, sum_ref):
        total = jnp.sum(a_ref[...] * a_ref[...] + b_ref[...] * b_ref[...], keepdims=True)
        sum_ref[...] = jnp.broadcast_to(total, (1, LANES))

    return run(kernel, "code_sum", [((1, LANES), jnp.float32)], [active_a, active_b])[0]


def errors(summed_ref, other_ref, paired_ref, bias_ref):
    own = summed_ref.shape[0] // 2
    total = summed_ref[...] + jnp.concatenate([other_ref[own:], other_ref[:own]], axis=0)
    recon = total + bias_ref[...]
    return recon, recon - paired_ref[...].astype(jnp.float32)


def residual_gradient(summed, other, paired, dec_bias, row_count, after):
    def kernel(summed_ref, other_ref, paired_ref, bias_ref, resid_ref):
        _, error = errors(summed_ref, other_ref, paired_ref, bias_ref)
        resid_ref[...] = (2.0 / row_count * error).astype(jnp.bfloat16)

    return run(
        kernel, "residual_gradient", [(summed.shape, jnp.bfloat16)], [summed, other, paired, dec_bias], after
    )[0]


def own_terms(summed, other, paired, dec_bias, row_count, after):
    rows, width = summed.shape
    own = rows // 2

    def kernel(summed_ref, other_ref, paired_ref, bias_ref, recon_ref, own_ref, square_ref):
        recon, error = errors(summed_ref, other_ref, paired_ref, bias_ref)
        error = error[:own]
        recon_ref[...] = recon[:own].astype(jnp.bfloat16)
        own_ref[...] = jnp.sum(2.0 / row_count * error, axis=0, keepdims=True)
        square_ref[...] = jnp.broadcast_to(jnp.sum(error * error, keepdims=True), (1, LANES))

    return run(
        kernel,
        "own_terms",
        [((own, width), jnp.bfloat16), ((1, width), jnp.float32), ((1, LANES), jnp.float32)],
        [summed, other, paired, dec_bias],
        after,
    )


def turn(weight, after):
    rows, columns = weight.shape

    def kernel(weight_ref, turned_ref):
        turned_ref[...] = weight_ref[...].T

    return run(kernel, "turn", [((columns, rows), weight.dtype)], [weight], after, moved=4 * rows * columns)[0]


def backward(half_a, half_b, dec_weight, active_a, active_b, row_count):
    half, width = half_a.shape
    latents = dec_weight.shape[1]

    def kernel(a_ref, b_ref, dec_ref, active_a_ref, active_b_ref, code_grad_ref, total_ref):
        resid = jnp.concatenate([a_ref[...], b_ref[...]], axis=0)
        back = jnp.dot(resid, dec_ref[...], preferred_element_type=jnp.float32)
        active = jnp.concatenate([active_a_ref[...], active_b_ref[...]], axis=0)
        code_grad = 2.0 * active * (back + PENALTY / row_count)
        code_grad_ref[...] = code_grad.astype(jnp.bfloat16)
        total_ref[...] = jnp.sum(code_grad, axis=0, keepdims=True)

    return run(
        kernel,
        "backward",
        [((2 * half, latents), jnp.bfloat16), ((1, latents), jnp.float32)],
        [half_a, half_b, dec_weight, active_a, active_b],
    )


def bias_product(total, enc_weight, own_bias, square, code_sum, row_count):
    latents, width = enc_weight.shape

    def kernel(total_ref, enc_ref, own_ref, square_ref, sum_ref, terms_ref):
        values = total_ref[...]
        high = values.astype(jnp.bfloat16).astype(jnp.float32)
        rest = values - high
        middle = rest.astype(jnp.bfloat16).astype(jnp.float32)
        pieces = [high, middle, rest - middle, jnp.zeros((5, latents), jnp.float32)]
        pieces = jnp.concatenate(pieces, axis=0).astype(jnp.bfloat16)
        product = jnp.dot(pieces, enc_ref[...], preferred_element_type=jnp.float32)
        terms_ref[:, :width] = own_ref[...] - (product[0:1] + (product[1:2] + product[2:3]))
        terms_ref[:, width:] = (square_ref[...] + PENALTY * sum_ref[...]) / row_count

    return run(
        kernel,
        "bias_product",
        [((1, width + LANES), jnp.float32)],
        [total, enc_weight, own_bias, square, code_sum],
    )[0]


def enc_gradient(centered_a, centered_b, code_grad, after):
    half, width = centered_a.shape
    latents = code_grad.shape[1]

    def kernel(a_ref, b_ref, code_grad_ref, grad_ref):
        centered = jnp.concatenate([a_ref[...], b_ref[...]], axis=0)
        grad_ref[...] = lax.dot_general(
            centered, code_grad_ref[...], CONTRACT_FIRST, preferred_element_type=jnp.float32
        ).astype(jnp.bfloat16)

    return run(
        kernel,
        "enc_gradient",
        [((width, latents), jnp.bfloat16)],
        [centered_a, centered_b, code_grad],
        after,
        flops=4 * half * width * latents,
    )[0]


def dec_gradient(codes_a, codes_b, resid_a, resid_b, stored, after):
    half, latents = codes_a.shape
    width = resid_a.shape[1]
    count = len(stored)

    def kernel(*refs):
        codes_a_ref, codes_b_ref, a_ref, b_ref = refs[:4]
        outs, grad_ref, sems = refs[5 + count : 5 + 2 * count], refs[-2], refs[-1]
        copies = [pltpu.make_async_copy(refs[4 + i], outs[i], sems.at[i]) for i in range(count)]
        for copy in copies:
            copy.start()
        codes = jnp.concatenate([codes_a_ref[...], codes_b_ref[...]], axis=0)
        resid = jnp.concatenate([a_ref[...], b_ref[...]], axis=0)
        grad_ref[...] = lax.dot_general(
            codes, resid, CONTRACT_FIRST, preferred_element_type=jnp.float32
        ).astype(jnp.bfloat16)
        for copy in copies:
            copy.wait()

    *outs, grad = pl.pallas_call(
        kernel,
        out_shape=[jax.ShapeDtypeStruct(a.shape, a.dtype) for a in stored] + [vmem((latents, width), jnp.bfloat16)],
        in_specs=[VMEM] * (5 + count),
        out_specs=[HBM] * count + [VMEM],
        scratch_shapes=[pltpu.SemaphoreType.DMA((count,))],
        compiler_params=pltpu.CompilerParams(vmem_limit_bytes=LIMIT),
        cost_estimate=pl.CostEstimate(flops=4 * half * latents * width, bytes_accessed=4 * latents * width, transcendentals=0),
        name="dec_gradient",
    )(*[in_vmem(a) for a in (codes_a, codes_b, resid_a, resid_b, *stored, after)])
    return outs, grad


def store(arrays, after):
    count = len(arrays)

    def kernel(*refs):
        outs, token_ref, sems = refs[count + 1 : 2 * count + 1], refs[-2], refs[-1]
        copies = [pltpu.make_async_copy(refs[i], outs[i], sems.at[i]) for i in range(count)]
        for copy in copies:
            copy.start()
        token_ref[...] = jnp.zeros_like(token_ref)
        for copy in copies:
            copy.wait()

    return pl.pallas_call(
        kernel,
        out_shape=[jax.ShapeDtypeStruct(a.shape, a.dtype) for a in arrays] + [vmem(*TOKEN)],
        in_specs=[VMEM] * (count + 1),
        out_specs=[HBM] * count + [VMEM],
        scratch_shapes=[pltpu.SemaphoreType.DMA((count,))],
        compiler_params=pltpu.CompilerParams(vmem_limit_bytes=LIMIT),
        cost_estimate=pl.CostEstimate(
            flops=0, bytes_accessed=2 * sum(a.size * a.dtype.itemsize for a in arrays), transcendentals=0
        ),
        name="store",
    )(*[in_vmem(a) for a in (*arrays, after)])


def add(*terms, after=(), order=None):
    order = order or list(range(len(terms)))

    def kernel(*refs):
        values = [refs[order.index(i)][...] for i in range(len(terms))]
        while len(values) > 1:
            values = [left + right for left, right in zip(values[::2], values[1::2])]
        refs[-1][...] = values[0]

    return run(kernel, "add", [(terms[0].shape, jnp.float32)], [terms[i] for i in order], after)[0]


def finish(terms, other, width, after):
    def kernel(terms_ref, other_ref, after_ref, bias_ref, loss_ref):
        total = terms_ref[...] + other_ref[...]
        bias_ref[...] = total[:, :width]
        loss_ref[...] = total[:, width : width + 1] / width

    return pl.pallas_call(
        kernel,
        out_shape=[jax.ShapeDtypeStruct((1, width), jnp.float32), jax.ShapeDtypeStruct((1, 1), jnp.float32)],
        in_specs=[VMEM] * 3,
        out_specs=[VMEM] * 2,
        compiler_params=pltpu.CompilerParams(vmem_limit_bytes=2 << 20),
        name="finish",
    )(in_vmem(terms), in_vmem(other), in_vmem(after))


def local(residuals, enc_weight, enc_bias, dec_weight, dec_bias):
    own_rows, width = residuals.shape
    lat = lax.axis_size("lat")
    row_count = own_rows * lat * lax.axis_size("sub")
    far, steps = plan(lat)

    enc_vmem, own, dec_bias_row, enc_bias_row = load(
        [enc_weight, residuals, dec_bias.reshape(1, width), enc_bias.reshape(1, -1)]
    )
    paired = stack([own, swap(residuals, far)], after=[enc_vmem])
    (dec_vmem,) = load([dec_weight], after=[paired])
    rows_a = gather(paired, steps, ROWS_ORDER, after=[dec_vmem])
    rows_b = swap(rows_a, CORES)
    centered_a, active_a, codes_a = encode(rows_a, enc_vmem, enc_bias_row, dec_bias_row)
    centered_b, active_b, codes_b, keep, send = encode_decode(
        rows_b, codes_a, enc_vmem, enc_bias_row, dec_vmem, dec_bias_row
    )

    summed, dec_turned = halve(keep, [swap(send, CORES)], steps[::-1], dec_vmem)
    enc_turned = turn(enc_vmem, [summed])
    error_args = summed, swap(summed, far), paired, dec_bias_row, row_count
    resid_bf = residual_gradient(*error_args, [enc_turned])

    resid_a = gather(resid_bf, steps, RESID_ORDER)
    resid_b = swap(resid_a, CORES)
    recon, own_bias, square = own_terms(*error_args, [resid_bf])
    code_grad_bf, total = backward(resid_a, resid_b, dec_turned, active_a, active_b, row_count)
    terms = bias_product(total, enc_turned, own_bias, square, code_sum(active_a, active_b), row_count)

    grad_enc = enc_gradient(centered_a, centered_b, code_grad_bf, [terms])
    terms = add(terms, swap(terms, CORES), after=[grad_enc])
    (grad_enc, total), grad_dec = dec_gradient(codes_a, codes_b, resid_a, resid_b, [grad_enc, total], terms)
    for masks in steps:
        terms = add(
            terms,
            *[swap(terms, mask) for mask in masks],
            after=[grad_dec],
            order=[0, *TERMS_ORDER] if len(masks) > 1 else None,
        )
    grad_dec, recon, stored = store([grad_dec, recon], terms)
    grad_dec_bias, loss_value = finish(terms, swap(terms, far), width, stored)
    return recon, loss_value[0], grad_enc, total[0], grad_dec, grad_dec_bias[0]


def solution(mesh):
    placed = (
        P(("parts", "lat", "sub"), None),
        P(None, ("parts", "lat", "sub")),
        P(("parts", "lat", "sub")),
        P(("parts", "lat", "sub"), None),
        P("parts"),
    )
    return jax.shard_map(
        local,
        mesh=mesh,
        in_specs=placed,
        out_specs=(
            P(("parts", "lat", "sub"), None),
            P("parts"),
            P(None, ("parts", "lat", "sub")),
            P(("parts", "lat", "sub")),
            P(("parts", "lat", "sub"), None),
            P("parts"),
        ),
        check_vma=False,
    )
```

time: 57.7 us -> 54.1 us (0.938)
  waiting for transfers between devices: 24.2 us -> 15.6 us
  starting transfers between devices: 20.8 us -> 24.2 us
  Pallas kernels: 11.9 us -> 13.2 us
    ppermute x14 -> x15, waiting for transfers between devices: 18.9 us -> 12.1 us  [swap(): lax.ppermute(values, 'lat', [(i, i ^ mask) for i in range(lax.axis_size('...]
    ppermute x14 -> x15, starting transfers between devices: 20.2 us -> 23.7 us  [swap(): lax.ppermute(values, 'lat', [(i, i ^ mask) for i in range(lax.axis_size('...]
    pallas_call x12 -> x17, Pallas kernels: 3.74 us -> 6.06 us  [run(): pl.pallas_call(body, out_shape=[vmem(*out) for out in outs], in_specs=[VM...]
    ppermute x4, waiting for transfers between devices: 5.3 us -> 3.54 us  [swap(): return lax.ppermute(values, 'sub', [(i, i ^ 1) for i in range(2)])]
    pallas_call x2, Pallas kernels: 3.99 us -> 3.02 us  [the longest x1 1.51 us: dec_gradient(): pl.pallas_call(kernel, out_shape=[jax.ShapeDtypeStruct(a.shape, a.dtype)...]
  transfers between devices with their start and end apart: 18 -> 19, of which waited for: 17 -> 16; matrix products, arithmetic and copies ran while one was open for 0% -> 0% of each run, Pallas kernels for 13% -> 18%
where the time goes in v4:
time: 54.1 us; the launch traced here: 53.9 us
  starting transfers between devices  24.2 us (45%)
  waiting for transfers between devices  15.6 us (29%)
  Pallas kernels  13.2 us (24%)
  between operations  0.78 us (1%)
    ppermute x15, starting transfers between devices, swap(): lax.ppermute(values, 'lat', [(i, i ^ mask) for i in range(lax.axis_size('...  23.7 us
    ppermute x15, waiting for transfers between devices, swap(): lax.ppermute(values, 'lat', [(i, i ^ mask) for i in range(lax.axis_size('...  12.1 us
    pallas_call x17, Pallas kernels, run(): pl.pallas_call(body, out_shape=[vmem(*out) for out in outs], in_specs=[VM...  6.06 us
    ppermute x4, waiting for transfers between devices, swap(): return lax.ppermute(values, 'sub', [(i, i ^ 1) for i in range(2)])  3.54 us
    pallas_call x2, Pallas kernels, load(): pl.pallas_call(kernel, out_shape=[vmem(array.shape, array.dtype) for arra...  3.53 us
    pallas_call x1, Pallas kernels, dec_gradient(): pl.pallas_call(kernel, out_shape=[jax.ShapeDtypeStruct(a.shape, a.dtype)...  1.51 us
    pallas_call x1, Pallas kernels, store(): pl.pallas_call(kernel, out_shape=[jax.ShapeDtypeStruct(a.shape, a.dtype)...  1.51 us
  transfers between devices with their start and end apart: 19, of which 16 were waited for; matrix products, arithmetic and copies ran while one was open for 0% of the time, Pallas kernels for 18%

profile of v4, /device:TPU:0, one launch (start us, length us, event | category | flops | bytes accessed | tf_op | source)
XLA Modules:
  0.0 53.9 jit_solution(15821336506784515653)
XLA Ops:
  0.6 4.1 %collective-permute-start = (bf16[2,5120]{1,0:T(2,128)(2,1)}, bf16[2,5120]{1,0:T(2,128)(2,1)S(1)}, u32[]{:S(2)}, u32[]{:S(2)}) collective-permute-start(bf16[2,5120]{1,0:T(2,128)(2,1)} %refs_1_.1), channel_id=1, source_target_pairs={{0,8},{2,10},{4,12},{6,14},{8,0},{10,2},{12,4},{14,6},{1,9},{3,11}... | collective-permute-start | bytes 61448 | tf_op jit(solution)/shard_map/ppermute | solution.py:52
  4.7 1.8 %load.2 = (bf16[5120,256]{1,0:T(8,128)(2,1)S(1)}, bf16[2,5120]{1,0:T(2,128)(2,1)S(1)}, f32[1,5120]{1,0:T(1,128)S(1)}, f32[1,256]{1,0:T(1,128)S(1)}) custom-call(bf16[5120,256]{1,0:T(8,128)(2,1)} %refs_0_.2, bf16[2,5120]{1,0:T(2,128)(2,1)} %refs_1_.1, f32[1,5120]{1,0:T(1,128)} %bitcast.5, f32[1,256]{1,0:T(1,128)} %bitcast.6), custom_call_target="tpu_custom_call" | custom-call | bytes 5326848 | tf_op jit(solution)/shard_map/load/pallas_call | solution.py:77
  6.8 2.9 %collective-permute-start.1 = (bf16[4,5120]{1,0:T(4,128)(2,1)S(1)}, bf16[4,5120]{1,0:T(4,128)(2,1)S(1)}, u32[]{:S(2)}, u32[]{:S(2)}) collective-permute-start(bf16[4,5120]{1,0:T(4,128)(2,1)S(1)} %stack.3.refs_1_.refs_0_.refs_2_), channel_id=1, source_target_pairs={{0,6},{2,4},{4,2},{6,0},{8,14},{10,12},{12,10},{14,8},{1,7},{3,5},... | collective-permute-start | bytes 122888 | tf_op jit(solution)/shard_map/ppermute | solution.py:52
  10.3 1.7 %load.3.refs_4_.refs_0_ = bf16[256,5120]{1,0:T(8,128)(2,1)S(1)} custom-call(bf16[256,5120]{1,0:T(8,128)(2,1)} %refs_0_.3, bf16[4,5120]{1,0:T(4,128)(2,1)S(1)} %stack.3.refs_1_.refs_0_.refs_2_), custom_call_target="tpu_custom_call" | custom-call | bytes 5242880 | tf_op jit(solution)/shard_map/load/pallas_call | solution.py:77
  12.1 1.6 %collective-permute-done.2.refs_2_ = bf16[4,5120]{1,0:T(4,128)(2,1)S(1)} collective-permute-done((bf16[4,5120]{1,0:T(4,128)(2,1)S(1)}, bf16[4,5120]{1,0:T(4,128)(2,1)S(1)}, u32[]{:S(2)}, u32[]{:S(2)}) %collective-permute-start.2) | collective-permute-done | bytes 40992 | tf_op jit(solution)/shard_map/ppermute | solution.py:52
  14.8 0.9 %collective-permute-done.4.refs_0_ = bf16[16,5120]{1,0:T(8,128)(2,1)S(1)} collective-permute-done((bf16[16,5120]{1,0:T(8,128)(2,1)S(1)}, bf16[16,5120]{1,0:T(8,128)(2,1)S(1)}, u32[]{:S(2)}, u32[]{:S(2)}) %collective-permute-start.4) | collective-permute-done | bytes 163872 | tf_op jit(solution)/shard_map/ppermute | solution.py:51
  15.7 1.5 %encode_decode.1 = (bf16[16,5120]{1,0:T(8,128)(2,1)S(1)}, f32[16,256]{1,0:T(8,128)S(1)}, bf16[16,256]{1,0:T(8,128)(2,1)S(1)}, f32[16,5120]{1,0:T(8,128)S(1)}, f32[16,5120]{1,0:T(8,128)S(1)}) custom-call(bf16[16,5120]{1,0:T(8,128)(2,1)S(1)} %collective-permute-done.4.refs_0_, bf16[16,256]{1,0:T(8,128)(2,1)S(1)} %get-tuple-element.39.refs_1_.refs_0_, ...), custom_call_target="tpu_custom_call" | custom-call | tf_op jit(solution)/shard_map/encode_decode/pallas_call | solution.py:38
  17.4 1.5 %collective-permute-done.5.refs_1_ = f32[16,5120]{1,0:T(8,128)S(1)} collective-permute-done((f32[16,5120]{1,0:T(8,128)S(1)}, f32[16,5120]{1,0:T(8,128)S(1)}, u32[]{:S(2)}, u32[]{:S(2)}) %collective-permute-start.5) | collective-permute-done | bytes 327712 | tf_op jit(solution)/shard_map/ppermute | solution.py:51
  19.1 1.9 %collective-permute-start.7 = (f32[4,5120]{1,0:T(4,128)S(1)}, f32[4,5120]{1,0:T(4,128)S(1)}, u32[]{:S(2)}, u32[]{:S(2)}) collective-permute-start(f32[4,5120]{1,0:T(4,128)S(1)} %get-tuple-element.45), channel_id=1, source_target_pairs={{0,2},{2,0},{4,6},{6,4},{8,10},{10,8},{12,14},{14,12},{1,3},{3,1},... | collective-permute-start | bytes 245768 | tf_op jit(solution)/shard_map/ppermute | solution.py:52
  21.0 1.5 %collective-permute-start.8 = (f32[4,5120]{1,0:T(4,128)S(1)}, f32[4,5120]{1,0:T(4,128)S(1)}, u32[]{:S(2)}, u32[]{:S(2)}) collective-permute-start(f32[4,5120]{1,0:T(4,128)S(1)} %get-tuple-element.46), channel_id=1, source_target_pairs={{0,6},{2,4},{4,2},{6,0},{8,14},{10,12},{12,10},{14,8},{1,7},{3,5},... | collective-permute-start | bytes 245768 | tf_op jit(solution)/shard_map/ppermute | solution.py:52
  22.5 0.7 %turn.2.refs_4_.refs_2_ = bf16[5120,256]{1,0:T(8,128)(2,1)S(1)} custom-call(bf16[256,5120]{1,0:T(8,128)(2,1)S(1)} %load.3.refs_4_.refs_0_, f32[4,5120]{1,0:T(4,128)S(1)} %get-tuple-element.43.refs_1_.refs_0_), custom_call_target="tpu_custom_call" | custom-call | bytes 5242880 | tf_op jit(solution)/shard_map/turn/pallas_call | solution.py:38
  23.2 0.8 %collective-permute-done.6.refs_1_ = f32[4,5120]{1,0:T(4,128)S(1)} collective-permute-done((f32[4,5120]{1,0:T(4,128)S(1)}, f32[4,5120]{1,0:T(4,128)S(1)}, u32[]{:S(2)}, u32[]{:S(2)}) %collective-permute-start.6) | collective-permute-done | bytes 81952 | tf_op jit(solution)/shard_map/ppermute | solution.py:52
  24.1 0.6 %collective-permute-done.7.refs_2_ = f32[4,5120]{1,0:T(4,128)S(1)} collective-permute-done((f32[4,5120]{1,0:T(4,128)S(1)}, f32[4,5120]{1,0:T(4,128)S(1)}, u32[]{:S(2)}, u32[]{:S(2)}) %collective-permute-start.7) | collective-permute-done | bytes 81952 | tf_op jit(solution)/shard_map/ppermute | solution.py:52
  24.7 1.7 %collective-permute-done.8.refs_3_ = f32[4,5120]{1,0:T(4,128)S(1)} collective-permute-done((f32[4,5120]{1,0:T(4,128)S(1)}, f32[4,5120]{1,0:T(4,128)S(1)}, u32[]{:S(2)}, u32[]{:S(2)}) %collective-permute-start.8) | collective-permute-done | bytes 81952 | tf_op jit(solution)/shard_map/ppermute | solution.py:52
  26.4 2.6 %collective-permute-start.9 = (f32[4,5120]{1,0:T(4,128)S(1)}, f32[4,5120]{1,0:T(4,128)S(1)}, u32[]{:S(2)}, u32[]{:S(2)}) collective-permute-start(f32[4,5120]{1,0:T(4,128)S(1)} %add_parts.3.refs_1_.refs_0_), channel_id=1, source_target_pairs={{0,8},{2,10},{4,12},{6,14},{8,0},{10,2},{12,4},{14,6},{1,9},{3,11}... | collective-permute-start | bytes 245768 | tf_op jit(solution)/shard_map/ppermute | solution.py:52
  29.0 0.8 %turn.3.refs_4_.refs_1_ = bf16[256,5120]{1,0:T(8,128)(2,1)S(1)} custom-call(bf16[5120,256]{1,0:T(8,128)(2,1)S(1)} %get-tuple-element.36.refs_2_.refs_1_.refs_0_, f32[4,5120]{1,0:T(4,128)S(1)} %add_parts.3.refs_1_.refs_0_), custom_call_target="tpu_custom_call" | custom-call | bytes 5242880 | tf_op jit(solution)/shard_map/turn/pallas_call | solution.py:38
  29.7 2.1 %collective-permute-done.9.refs_1_ = f32[4,5120]{1,0:T(4,128)S(1)} collective-permute-done((f32[4,5120]{1,0:T(4,128)S(1)}, f32[4,5120]{1,0:T(4,128)S(1)}, u32[]{:S(2)}, u32[]{:S(2)}) %collective-permute-start.9) | collective-permute-done | bytes 81952 | tf_op jit(solution)/shard_map/ppermute | solution.py:52
  31.9 1.8 %collective-permute-start.10 = (bf16[4,5120]{1,0:T(4,128)(2,1)S(1)}, bf16[4,5120]{1,0:T(4,128)(2,1)S(1)}, u32[]{:S(2)}, u32[]{:S(2)}) collective-permute-start(bf16[4,5120]{1,0:T(4,128)(2,1)S(1)} %residual_gradient.1.refs_0_.refs_4_), channel_id=1, source_target_pairs={{0,6},{2,4},{4,2},{6,0},{8,14},{10,12},{12,10},{14,8},{1,7},{3,5},... | collective-permute-start | bytes 122888 | tf_op jit(solution)/shard_map/ppermute | solution.py:52
  33.7 1.2 %collective-permute-start.11 = (bf16[4,5120]{1,0:T(4,128)(2,1)S(1)}, bf16[4,5120]{1,0:T(4,128)(2,1)S(1)}, u32[]{:S(2)}, u32[]{:S(2)}) collective-permute-start(bf16[4,5120]{1,0:T(4,128)(2,1)S(1)} %residual_gradient.1.refs_0_.refs_4_), channel_id=1, source_target_pairs={{0,2},{2,0},{4,6},{6,4},{8,10},{10,8},{12,14},{14,12},{1,3},{3,1},... | collective-permute-start | bytes 122888 | tf_op jit(solution)/shard_map/ppermute | solution.py:52
  35.4 1.4 %collective-permute-done.10.refs_1_ = bf16[4,5120]{1,0:T(4,128)(2,1)S(1)} collective-permute-done((bf16[4,5120]{1,0:T(4,128)(2,1)S(1)}, bf16[4,5120]{1,0:T(4,128)(2,1)S(1)}, u32[]{:S(2)}, u32[]{:S(2)}) %collective-permute-start.10) | collective-permute-done | bytes 40992 | tf_op jit(solution)/shard_map/ppermute | solution.py:52
  36.8 0.9 %collective-permute-done.11.refs_2_ = bf16[4,5120]{1,0:T(4,128)(2,1)S(1)} collective-permute-done((bf16[4,5120]{1,0:T(4,128)(2,1)S(1)}, bf16[4,5120]{1,0:T(4,128)(2,1)S(1)}, u32[]{:S(2)}, u32[]{:S(2)}) %collective-permute-start.11) | collective-permute-done | bytes 40992 | tf_op jit(solution)/shard_map/ppermute | solution.py:52
  37.7 1.2 %collective-permute-done.12.refs_3_ = bf16[4,5120]{1,0:T(4,128)(2,1)S(1)} collective-permute-done((bf16[4,5120]{1,0:T(4,128)(2,1)S(1)}, bf16[4,5120]{1,0:T(4,128)(2,1)S(1)}, u32[]{:S(2)}, u32[]{:S(2)}) %collective-permute-start.12) | collective-permute-done | bytes 40992 | tf_op jit(solution)/shard_map/ppermute | solution.py:52
  39.4 1.0 %collective-permute-done.13.refs_1_.refs_3_ = bf16[16,5120]{1,0:T(8,128)(2,1)S(1)} collective-permute-done((bf16[16,5120]{1,0:T(8,128)(2,1)S(1)}, bf16[16,5120]{1,0:T(8,128)(2,1)S(1)}, u32[]{:S(2)}, u32[]{:S(2)}) %collective-permute-start.13) | collective-permute-done | bytes 163872 | tf_op jit(solution)/shard_map/ppermute | solution.py:51
  41.6 0.9 %enc_gradient.1.refs_2_.refs_4_ = bf16[5120,256]{1,0:T(8,128)(2,1)S(1)} custom-call(bf16[16,5120]{1,0:T(8,128)(2,1)S(1)} %get-tuple-element.47.refs_0_, bf16[16,5120]{1,0:T(8,128)(2,1)S(1)} %get-tuple-element.48.refs_1_, bf16[32,256]{1,0:T(8,128)(2,1)S(1)} %get-tuple-element.51.refs_2_, f32[1,5248]{1,0:T(1,128)S(1)} %bias_product.1.refs_3_.refs_0_), custom_call_target="tpu_custom_call" | custom-call | flops 83886080 | tf_op jit(solution)/shard_map/enc_gradient/pallas_call | solution.py:38
  42.7 0.7 %collective-permute-start.15 = (f32[1,5248]{1,0:T(1,128)S(1)}, f32[1,5248]{1,0:T(1,128)S(1)}, u32[]{:S(2)}, u32[]{:S(2)}) collective-permute-start(f32[1,5248]{1,0:T(1,128)S(1)} %add.2.refs_6_.refs_0_), channel_id=1, source_target_pairs={{0,6},{2,4},{4,2},{6,0},{8,14},{10,12},{12,10},{14,8},{1,7},{3,5},... | collective-permute-start | bytes 62984 | tf_op jit(solution)/shard_map/ppermute | solution.py:52
  43.4 1.3 %collective-permute-start.16 = (f32[1,5248]{1,0:T(1,128)S(1)}, f32[1,5248]{1,0:T(1,128)S(1)}, u32[]{:S(2)}, u32[]{:S(2)}) collective-permute-start(f32[1,5248]{1,0:T(1,128)S(1)} %add.2.refs_6_.refs_0_), channel_id=1, source_target_pairs={{0,2},{2,0},{4,6},{6,4},{8,10},{10,8},{12,14},{14,12},{1,3},{3,1},... | collective-permute-start | bytes 62984 | tf_op jit(solution)/shard_map/ppermute | solution.py:52
  44.7 1.5 %collective-permute-start.17 = (f32[1,5248]{1,0:T(1,128)S(1)}, f32[1,5248]{1,0:T(1,128)S(1)}, u32[]{:S(2)}, u32[]{:S(2)}) collective-permute-start(f32[1,5248]{1,0:T(1,128)S(1)} %add.2.refs_6_.refs_0_), channel_id=1, source_target_pairs={{0,4},{2,6},{4,0},{6,2},{8,12},{10,14},{12,8},{14,10},{1,5},{3,7},... | collective-permute-start | bytes 62984 | tf_op jit(solution)/shard_map/ppermute | solution.py:52
  46.2 1.5 %dec_gradient.1 = (bf16[5120,256]{1,0:T(8,128)(2,1)}, f32[1,256]{1,0:T(1,128)}, bf16[256,5120]{1,0:T(8,128)(2,1)S(1)}) custom-call(bf16[16,256]{1,0:T(8,128)(2,1)S(1)} %get-tuple-element.39.refs_1_.refs_0_, bf16[16,256]{1,0:T(8,128)(2,1)S(1)} %get-tuple-element.40.refs_1_, bf16[16,5120]{1,0:T(8,128)(2,1)S(1)} %stack.5.refs_0_.refs_2_, ...), custom_call_target="tpu_custom_call" | custom-call | flops 83886080 | bytes 5242880 | tf_op jit(solution)/shard_map/dec_gradient/pallas_call | solution.py:314
  47.7 0.8 %collective-permute-done.17.refs_3_ = f32[1,5248]{1,0:T(1,128)S(1)} collective-permute-done((f32[1,5248]{1,0:T(1,128)S(1)}, f32[1,5248]{1,0:T(1,128)S(1)}, u32[]{:S(2)}, u32[]{:S(2)}) %collective-permute-start.17) | collective-permute-done | bytes 21024 | tf_op jit(solution)/shard_map/ppermute | solution.py:52
  48.5 2.9 %collective-permute-start.18 = (f32[1,5248]{1,0:T(1,128)S(1)}, f32[1,5248]{1,0:T(1,128)S(1)}, u32[]{:S(2)}, u32[]{:S(2)}) collective-permute-start(f32[1,5248]{1,0:T(1,128)S(1)} %add.3.refs_2_.terms_ref), channel_id=1, source_target_pairs={{0,8},{2,10},{4,12},{6,14},{8,0},{10,2},{12,4},{14,6},{1,9},{3,11}... | collective-permute-start | bytes 62984 | tf_op jit(solution)/shard_map/ppermute | solution.py:52
  51.4 1.5 %store.1 = (bf16[256,5120]{1,0:T(8,128)(2,1)}, bf16[2,5120]{1,0:T(2,128)(2,1)}, f32[8,128]{1,0:T(8,128)S(1)}) custom-call(bf16[256,5120]{1,0:T(8,128)(2,1)S(1)} %get-tuple-element.55.refs_4_.refs_0_, bf16[2,5120]{1,0:T(2,128)(2,1)S(1)} %get-tuple-element.56.refs_1_, f32[1,5248]{1,0:T(1,128)S(1)} %add.3.refs_2_.terms_ref), custom_call_target="tpu_custom_call" | custom-call | bytes 5283840 | tf_op jit(solution)/shard_map/store/pallas_call | solution.py:339
  53.3 0.6 %finish.1 = (f32[1,5120]{1,0:T(1,128)}, f32[1,1]{1,0:T(1,128)}) custom-call(f32[1,5248]{1,0:T(1,128)S(1)} %add.3.refs_2_.terms_ref, f32[1,5248]{1,0:T(1,128)S(1)} %collective-permute-done.18.other_ref, f32[8,128]{1,0:T(8,128)S(1)} %get-tuple-element.58.after_ref), custom_call_target="tpu_custom_call" | custom-call | tf_op jit(solution)/shard_map/finish/pallas_call | solution.py:371
  (28 shorter events, 5.4 us)
Async XLA Ops:
  0.6 6.1 %collective-permute-start = (bf16[2,5120]{1,0:T(2,128)(2,1)}, bf16[2,5120]{1,0:T(2,128)(2,1)S(1)}, u32[]{:S(2)}, u32[]{:S(2)}) collective-permute-start(bf16[2,5120]{1,0:T(2,128)(2,1)} %refs_1_.1), channel_id=1, source_target_pairs={{0,8},{2,10},{4,12},{6,14},{8,0},{10,2},{12,4},{14,6},{1,9},{3,11}... | collective-permute-start | bytes 61448 | tf_op jit(solution)/shard_map/ppermute | solution.py:52
  6.8 5.3 %collective-permute-start.1 = (bf16[4,5120]{1,0:T(4,128)(2,1)S(1)}, bf16[4,5120]{1,0:T(4,128)(2,1)S(1)}, u32[]{:S(2)}, u32[]{:S(2)}) collective-permute-start(bf16[4,5120]{1,0:T(4,128)(2,1)S(1)} %stack.3.refs_1_.refs_0_.refs_2_), channel_id=1, source_target_pairs={{0,6},{2,4},{4,2},{6,0},{8,14},{10,12},{12,10},{14,8},{1,7},{3,5},... | collective-permute-start | bytes 122888 | tf_op jit(solution)/shard_map/ppermute | solution.py:52
  9.6 4.0 %collective-permute-start.2 = (bf16[4,5120]{1,0:T(4,128)(2,1)S(1)}, bf16[4,5120]{1,0:T(4,128)(2,1)S(1)}, u32[]{:S(2)}, u32[]{:S(2)}) collective-permute-start(bf16[4,5120]{1,0:T(4,128)(2,1)S(1)} %stack.3.refs_1_.refs_0_.refs_2_), channel_id=1, source_target_pairs={{0,2},{2,0},{4,6},{6,4},{8,10},{10,8},{12,14},{14,12},{1,3},{3,1},... | collective-permute-start | bytes 122888 | tf_op jit(solution)/shard_map/ppermute | solution.py:52
  10.2 4.0 %collective-permute-start.3 = (bf16[4,5120]{1,0:T(4,128)(2,1)S(1)}, bf16[4,5120]{1,0:T(4,128)(2,1)S(1)}, u32[]{:S(2)}, u32[]{:S(2)}) collective-permute-start(bf16[4,5120]{1,0:T(4,128)(2,1)S(1)} %stack.3.refs_1_.refs_0_.refs_2_), channel_id=1, source_target_pairs={{0,4},{2,6},{4,0},{6,2},{8,12},{10,14},{12,8},{14,10},{1,5},{3,7},... | collective-permute-start | bytes 122888 | tf_op jit(solution)/shard_map/ppermute | solution.py:52
  14.2 1.5 %collective-permute-start.4 = (bf16[16,5120]{1,0:T(8,128)(2,1)S(1)}, bf16[16,5120]{1,0:T(8,128)(2,1)S(1)}, u32[]{:S(2)}, u32[]{:S(2)}) collective-permute-start(bf16[16,5120]{1,0:T(8,128)(2,1)S(1)} %stack.4.refs_0_), channel_id=1, source_target_pairs={{0,1},{1,0},{2,3},{3,2},{4,5},{5,4},{6,7},{7,6},{8,9},{9,8},{10,11... | collective-permute-start | bytes 491528 | tf_op jit(solution)/shard_map/ppermute | solution.py:51
  17.2 1.7 %collective-permute-start.5 = (f32[16,5120]{1,0:T(8,128)S(1)}, f32[16,5120]{1,0:T(8,128)S(1)}, u32[]{:S(2)}, u32[]{:S(2)}) collective-permute-start(f32[16,5120]{1,0:T(8,128)S(1)} %get-tuple-element.42), channel_id=1, source_target_pairs={{0,1},{1,0},{2,3},{3,2},{4,5},{5,4},{6,7},{7,6},{8,9},{9,8},{10,11... | collective-permute-start | bytes 983048 | tf_op jit(solution)/shard_map/ppermute | solution.py:51
  18.9 5.1 %collective-permute-start.6 = (f32[4,5120]{1,0:T(4,128)S(1)}, f32[4,5120]{1,0:T(4,128)S(1)}, u32[]{:S(2)}, u32[]{:S(2)}) collective-permute-start(f32[4,5120]{1,0:T(4,128)S(1)} %get-tuple-element.44), channel_id=1, source_target_pairs={{0,4},{2,6},{4,0},{6,2},{8,12},{10,14},{12,8},{14,10},{1,5},{3,7},... | collective-permute-start | bytes 245768 | tf_op jit(solution)/shard_map/ppermute | solution.py:52
  19.1 5.5 %collective-permute-start.7 = (f32[4,5120]{1,0:T(4,128)S(1)}, f32[4,5120]{1,0:T(4,128)S(1)}, u32[]{:S(2)}, u32[]{:S(2)}) collective-permute-start(f32[4,5120]{1,0:T(4,128)S(1)} %get-tuple-element.45), channel_id=1, source_target_pairs={{0,2},{2,0},{4,6},{6,4},{8,10},{10,8},{12,14},{14,12},{1,3},{3,1},... | collective-permute-start | bytes 245768 | tf_op jit(solution)/shard_map/ppermute | solution.py:52
  21.0 5.3 %collective-permute-start.8 = (f32[4,5120]{1,0:T(4,128)S(1)}, f32[4,5120]{1,0:T(4,128)S(1)}, u32[]{:S(2)}, u32[]{:S(2)}) collective-permute-start(f32[4,5120]{1,0:T(4,128)S(1)} %get-tuple-element.46), channel_id=1, source_target_pairs={{0,6},{2,4},{4,2},{6,0},{8,14},{10,12},{12,10},{14,8},{1,7},{3,5},... | collective-permute-start | bytes 245768 | tf_op jit(solution)/shard_map/ppermute | solution.py:52
  26.4 5.4 %collective-permute-start.9 = (f32[4,5120]{1,0:T(4,128)S(1)}, f32[4,5120]{1,0:T(4,128)S(1)}, u32[]{:S(2)}, u32[]{:S(2)}) collective-permute-start(f32[4,5120]{1,0:T(4,128)S(1)} %add_parts.3.refs_1_.refs_0_), channel_id=1, source_target_pairs={{0,8},{2,10},{4,12},{6,14},{8,0},{10,2},{12,4},{14,6},{1,9},{3,11}... | collective-permute-start | bytes 245768 | tf_op jit(solution)/shard_map/ppermute | solution.py:52
  31.9 5.0 %collective-permute-start.10 = (bf16[4,5120]{1,0:T(4,128)(2,1)S(1)}, bf16[4,5120]{1,0:T(4,128)(2,1)S(1)}, u32[]{:S(2)}, u32[]{:S(2)}) collective-permute-start(bf16[4,5120]{1,0:T(4,128)(2,1)S(1)} %residual_gradient.1.refs_0_.refs_4_), channel_id=1, source_target_pairs={{0,6},{2,4},{4,2},{6,0},{8,14},{10,12},{12,10},{14,8},{1,7},{3,5},... | collective-permute-start | bytes 122888 | tf_op jit(solution)/shard_map/ppermute | solution.py:52
  33.7 4.0 %collective-permute-start.11 = (bf16[4,5120]{1,0:T(4,128)(2,1)S(1)}, bf16[4,5120]{1,0:T(4,128)(2,1)S(1)}, u32[]{:S(2)}, u32[]{:S(2)}) collective-permute-start(bf16[4,5120]{1,0:T(4,128)(2,1)S(1)} %residual_gradient.1.refs_0_.refs_4_), channel_id=1, source_target_pairs={{0,2},{2,0},{4,6},{6,4},{8,10},{10,8},{12,14},{14,12},{1,3},{3,1},... | collective-permute-start | bytes 122888 | tf_op jit(solution)/shard_map/ppermute | solution.py:52
  34.9 4.0 %collective-permute-start.12 = (bf16[4,5120]{1,0:T(4,128)(2,1)S(1)}, bf16[4,5120]{1,0:T(4,128)(2,1)S(1)}, u32[]{:S(2)}, u32[]{:S(2)}) collective-permute-start(bf16[4,5120]{1,0:T(4,128)(2,1)S(1)} %residual_gradient.1.refs_0_.refs_4_), channel_id=1, source_target_pairs={{0,4},{2,6},{4,0},{6,2},{8,12},{10,14},{12,8},{14,10},{1,5},{3,7},... | collective-permute-start | bytes 122888 | tf_op jit(solution)/shard_map/ppermute | solution.py:52
  38.9 1.5 %collective-permute-start.13 = (bf16[16,5120]{1,0:T(8,128)(2,1)S(1)}, bf16[16,5120]{1,0:T(8,128)(2,1)S(1)}, u32[]{:S(2)}, u32[]{:S(2)}) collective-permute-start(bf16[16,5120]{1,0:T(8,128)(2,1)S(1)} %stack.5.refs_0_.refs_2_), channel_id=1, source_target_pairs={{0,1},{1,0},{2,3},{3,2},{4,5},{5,4},{6,7},{7,6},{8,9},{9,8},{10,11... | collective-permute-start | bytes 491528 | tf_op jit(solution)/shard_map/ppermute | solution.py:51
  41.4 1.3 %collective-permute-start.14 = (f32[1,5248]{1,0:T(1,128)S(1)}, f32[1,5248]{1,0:T(1,128)S(1)}, u32[]{:S(2)}, u32[]{:S(2)}) collective-permute-start(f32[1,5248]{1,0:T(1,128)S(1)} %bias_product.1.refs_3_.refs_0_), channel_id=1, source_target_pairs={{0,1},{1,0},{2,3},{3,2},{4,5},{5,4},{6,7},{7,6},{8,9},{9,8},{10,11... | collective-permute-start | bytes 62984 | tf_op jit(solution)/shard_map/ppermute | solution.py:51
  42.7 5.0 %collective-permute-start.15 = (f32[1,5248]{1,0:T(1,128)S(1)}, f32[1,5248]{1,0:T(1,128)S(1)}, u32[]{:S(2)}, u32[]{:S(2)}) collective-permute-start(f32[1,5248]{1,0:T(1,128)S(1)} %add.2.refs_6_.refs_0_), channel_id=1, source_target_pairs={{0,6},{2,4},{4,2},{6,0},{8,14},{10,12},{12,10},{14,8},{1,7},{3,5},... | collective-permute-start | bytes 62984 | tf_op jit(solution)/shard_map/ppermute | solution.py:52
  43.4 4.3 %collective-permute-start.16 = (f32[1,5248]{1,0:T(1,128)S(1)}, f32[1,5248]{1,0:T(1,128)S(1)}, u32[]{:S(2)}, u32[]{:S(2)}) collective-permute-start(f32[1,5248]{1,0:T(1,128)S(1)} %add.2.refs_6_.refs_0_), channel_id=1, source_target_pairs={{0,2},{2,0},{4,6},{6,4},{8,10},{10,8},{12,14},{14,12},{1,3},{3,1},... | collective-permute-start | bytes 62984 | tf_op jit(solution)/shard_map/ppermute | solution.py:52
  44.7 3.8 %collective-permute-start.17 = (f32[1,5248]{1,0:T(1,128)S(1)}, f32[1,5248]{1,0:T(1,128)S(1)}, u32[]{:S(2)}, u32[]{:S(2)}) collective-permute-start(f32[1,5248]{1,0:T(1,128)S(1)} %add.2.refs_6_.refs_0_), channel_id=1, source_target_pairs={{0,4},{2,6},{4,0},{6,2},{8,12},{10,14},{12,8},{14,10},{1,5},{3,7},... | collective-permute-start | bytes 62984 | tf_op jit(solution)/shard_map/ppermute | solution.py:52
  48.5 4.8 %collective-permute-start.18 = (f32[1,5248]{1,0:T(1,128)S(1)}, f32[1,5248]{1,0:T(1,128)S(1)}, u32[]{:S(2)}, u32[]{:S(2)}) collective-permute-start(f32[1,5248]{1,0:T(1,128)S(1)} %add.3.refs_2_.terms_ref), channel_id=1, source_target_pairs={{0,8},{2,10},{4,12},{6,14},{8,0},{10,2},{12,4},{14,6},{1,9},{3,11}... | collective-permute-start | bytes 62984 | tf_op jit(solution)/shard_map/ppermute | solution.py:52

commit v5 on v4

--- a/solution.py
+++ b/solution.py
@@ -52,7 +52,7 @@
     return lax.ppermute(values, "lat", [(i, i ^ mask) for i in range(lax.axis_size("lat"))])
 
 
-ROWS_ORDER, SUM_ORDER, RESID_ORDER, TERMS_ORDER = (3, 1, 2), (2, 1, 3), (3, 1, 2), (3, 1, 2)
+ROWS_ORDER, SUM_ORDER, RESID_ORDER, TERMS_ORDER = (2, 1, 3), (2, 1, 3), (2, 1, 3), (2, 1, 3)
 
 
 def plan(lat):
@@ -119,60 +119,49 @@
     return run(kernel, "add_parts", [((size, width), jnp.float32)] * count, [first, *others], after)
 
 
-def halve(first, others, steps, dec_weight):
-    for masks in steps:
-        parts = add_parts(first, others, len(masks) + 1)
-        dec_turned = turn(dec_weight, [parts[0]])
-        first, others = parts[0], [swap(part, mask) for part, mask in zip(parts[1:], masks)]
+def halve(parts, steps, dec_weight):
+    dec_turned = turn(dec_weight, [parts[0]])
+    for step, masks in enumerate(steps):
+        others = [swap(part, mask) for part, mask in zip(parts[1:], masks)]
         if len(masks) > 1:
             others = [others[mask - 1] for mask in SUM_ORDER]
-    return add_parts(first, others, 1, after=[dec_turned])[0], dec_turned
-
-
-def encode_rows(rows, weight, bias, dec_bias):
-    centered = (rows.astype(jnp.float32) - dec_bias).astype(jnp.bfloat16)
-    preact = jnp.dot(centered, weight, preferred_element_type=jnp.float32) + bias
-    active = jnp.maximum(preact, 0.0)
-    return centered, active, (active * active).astype(jnp.bfloat16)
-
-
-def encoded(half, width, latents):
-    return [((half, width), jnp.bfloat16), ((half, latents), jnp.float32), ((half, latents), jnp.bfloat16)]
-
-
-def encode(rows, enc_weight, enc_bias, dec_bias):
-    half, width = rows.shape
-    latents = enc_weight.shape[1]
-
-    def kernel(rows_ref, enc_ref, enc_bias_ref, dec_bias_ref, *outs):
-        for ref, values in zip(outs, encode_rows(rows_ref[...], enc_ref[...], enc_bias_ref[...], dec_bias_ref[...])):
-            ref[...] = values
-
-    return run(
-        kernel,
-        "encode",
-        encoded(half, width, latents),
-        [rows, enc_weight, enc_bias, dec_bias],
-        flops=2 * half * width * latents,
-    )
-
-
-def encode_decode(rows, codes, enc_weight, enc_bias, dec_weight, dec_bias):
-    half, width = rows.shape
-    latents = enc_weight.shape[1]
-
-    def kernel(rows_ref, codes_ref, enc_ref, enc_bias_ref, dec_ref, dec_bias_ref, *outs):
-        results = encode_rows(rows_ref[...], enc_ref[...], enc_bias_ref[...], dec_bias_ref[...])
-        both = jnp.concatenate([codes_ref[...], results[2]], axis=0)
-        partial = jnp.dot(both, dec_ref[...], preferred_element_type=jnp.float32)
-        for ref, values in zip(outs, [*results, partial[:half], partial[half:]]):
-            ref[...] = values
+        count = len(steps[step + 1]) + 1 if step + 1 < len(steps) else 1
+        parts = add_parts(parts[0], others, count, after=[dec_turned])
+    return parts[0], dec_turned
+
+
+def encode_decode(rows, weights, dec_bias, count):
+    height, width = rows.shape
+    latents = weights[0][0].shape[1]
+    sets = len(weights)
+
+    def kernel(rows_ref, dec_bias_ref, *refs):
+        centered_ref, outs = refs[3 * sets], refs[3 * sets + 1 :]
+        centered = (rows_ref[...].astype(jnp.float32) - dec_bias_ref[...]).astype(jnp.bfloat16)
+        centered_ref[...] = centered
+        codes = []
+        for i in range(sets):
+            enc_ref, enc_bias_ref = refs[3 * i], refs[3 * i + 1]
+            preact = jnp.dot(centered, enc_ref[...], preferred_element_type=jnp.float32) + enc_bias_ref[...]
+            active = jnp.maximum(preact, 0.0)
+            outs[i][...] = active
+            codes.append((active * active).astype(jnp.bfloat16))
+        total = None
+        for i in range(sets):
+            partial = jnp.dot(codes[i], refs[3 * i + 2][...], preferred_element_type=jnp.float32)
+            total = partial if total is None else total + partial
+        size = height // count
+        for part, ref in enumerate(outs[sets:]):
+            ref[...] = total[part * size : (part + 1) * size]
 
     return run(
         kernel,
         "encode_decode",
-        encoded(half, width, latents) + [((half, width), jnp.float32)] * 2,
-        [rows, codes, enc_weight, enc_bias, dec_weight, dec_bias],
+        [((height, width), jnp.bfloat16)]
+        + [((height, latents), jnp.float32)] * sets
+        + [((height // count, width), jnp.float32)] * count,
+        [rows, dec_bias, *[array for weight in weights for array in weight]],
+        flops=4 * sets * height * width * latents,
     )
 
 
@@ -292,18 +281,19 @@
     )[0]
 
 
-def dec_gradient(codes_a, codes_b, resid_a, resid_b, stored, after):
-    half, latents = codes_a.shape
+def dec_gradient(active_a, active_b, resid_a, resid_b, stored, after):
+    half, latents = active_a.shape
     width = resid_a.shape[1]
     count = len(stored)
 
     def kernel(*refs):
-        codes_a_ref, codes_b_ref, a_ref, b_ref = refs[:4]
+        active_a_ref, active_b_ref, a_ref, b_ref = refs[:4]
         outs, grad_ref, sems = refs[5 + count : 5 + 2 * count], refs[-2], refs[-1]
         copies = [pltpu.make_async_copy(refs[4 + i], outs[i], sems.at[i]) for i in range(count)]
         for copy in copies:
             copy.start()
-        codes = jnp.concatenate([codes_a_ref[...], codes_b_ref[...]], axis=0)
+        active = jnp.concatenate([active_a_ref[...], active_b_ref[...]], axis=0)
+        codes = (active * active).astype(jnp.bfloat16)
         resid = jnp.concatenate([a_ref[...], b_ref[...]], axis=0)
         grad_ref[...] = lax.dot_general(
             codes, resid, CONTRACT_FIRST, preferred_element_type=jnp.float32
@@ -320,7 +310,7 @@
         compiler_params=pltpu.CompilerParams(vmem_limit_bytes=LIMIT),
         cost_estimate=pl.CostEstimate(flops=4 * half * latents * width, bytes_accessed=4 * latents * width, transcendentals=0),
         name="dec_gradient",
-    )(*[in_vmem(a) for a in (codes_a, codes_b, resid_a, resid_b, *stored, after)])
+    )(*[in_vmem(a) for a in (active_a, active_b, resid_a, resid_b, *stored, after)])
     return outs, grad
 
 
@@ -384,22 +374,23 @@
     row_count = own_rows * lat * lax.axis_size("sub")
     far, steps = plan(lat)
 
-    enc_vmem, own, dec_bias_row, enc_bias_row = load(
-        [enc_weight, residuals, dec_bias.reshape(1, width), enc_bias.reshape(1, -1)]
-    )
-    paired = stack([own, swap(residuals, far)], after=[enc_vmem])
+    enc_bias = enc_bias.reshape(1, -1)
+    other = swap(residuals, far)
+    siblings = swap(enc_weight, CORES), swap(enc_bias, CORES), swap(dec_weight, CORES)
+    enc_vmem, own, dec_bias_row, enc_bias_row = load([enc_weight, residuals, dec_bias.reshape(1, width), enc_bias])
+    paired = stack([own, other], after=[enc_vmem])
     (dec_vmem,) = load([dec_weight], after=[paired])
-    rows_a = gather(paired, steps, ROWS_ORDER, after=[dec_vmem])
-    rows_b = swap(rows_a, CORES)
-    centered_a, active_a, codes_a = encode(rows_a, enc_vmem, enc_bias_row, dec_bias_row)
-    centered_b, active_b, codes_b, keep, send = encode_decode(
-        rows_b, codes_a, enc_vmem, enc_bias_row, dec_vmem, dec_bias_row
-    )
-
-    summed, dec_turned = halve(keep, [swap(send, CORES)], steps[::-1], dec_vmem)
+    rows = gather(paired, steps, ROWS_ORDER, after=[dec_vmem])
+    centered_a, active_a, active_sibling, *parts = encode_decode(
+        rows, [(enc_vmem, enc_bias_row, dec_vmem), siblings], dec_bias_row, len(steps[-1]) + 1
+    )
+
+    summed, dec_turned = halve(parts, steps[::-1], dec_vmem)
+    active_b = swap(active_sibling, CORES)
+    centered_b = swap(centered_a, CORES)
     enc_turned = turn(enc_vmem, [summed])
     error_args = summed, swap(summed, far), paired, dec_bias_row, row_count
-    resid_bf = residual_gradient(*error_args, [enc_turned])
+    resid_bf = residual_gradient(*error_args, [enc_turned, active_b, centered_b])
 
     resid_a = gather(resid_bf, steps, RESID_ORDER)
     resid_b = swap(resid_a, CORES)
@@ -409,7 +400,7 @@
 
     grad_enc = enc_gradient(centered_a, centered_b, code_grad_bf, [terms])
     terms = add(terms, swap(terms, CORES), after=[grad_enc])
-    (grad_enc, total), grad_dec = dec_gradient(codes_a, codes_b, resid_a, resid_b, [grad_enc, total], terms)
+    (grad_enc, total), grad_dec = dec_gradient(active_a, active_b, resid_a, resid_b, [grad_enc, total], terms)
     for masks in steps:
         terms = add(
             terms,

time: 54.1 us -> 53.2 us (0.983)
    ppermute x15, waiting for transfers between devices: 12.1 us -> 14.2 us  [swap(): lax.ppermute(values, 'lat', [(i, i ^ mask) for i in range(lax.axis_size('...]
    ppermute x4 -> x7, waiting for transfers between devices: 3.54 us -> 1.55 us  [swap(): return lax.ppermute(values, 'sub', [(i, i ^ 1) for i in range(2)])]
    ppermute x15, starting transfers between devices: 23.7 us -> 22.9 us  [swap(): lax.ppermute(values, 'lat', [(i, i ^ mask) for i in range(lax.axis_size('...]
    pallas_call x17 -> x15, Pallas kernels: 6.06 us -> 5.61 us  [run(): pl.pallas_call(body, out_shape=[vmem(*out) for out in outs], in_specs=[VM...]
  transfers between devices with their start and end apart: 19 -> 22, of which waited for: 16 -> 16; matrix products, arithmetic and copies ran while one was open for 0% -> 0% of each run, Pallas kernels for 18% -> 18%
where the time goes in v5:
time: 53.2 us; the launch traced here: 53 us
  starting transfers between devices  23.8 us (45%)
  waiting for transfers between devices  15.7 us (30%)
  Pallas kernels  12.8 us (24%)
  between operations  0.78 us (1%)
    ppermute x15, starting transfers between devices, swap(): lax.ppermute(values, 'lat', [(i, i ^ mask) for i in range(lax.axis_size('...  22.9 us
    ppermute x15, waiting for transfers between devices, swap(): lax.ppermute(values, 'lat', [(i, i ^ mask) for i in range(lax.axis_size('...  14.2 us
    pallas_call x15, Pallas kernels, run(): pl.pallas_call(body, out_shape=[vmem(*out) for out in outs], in_specs=[VM...  5.61 us
    pallas_call x2, Pallas kernels, load(): pl.pallas_call(kernel, out_shape=[vmem(array.shape, array.dtype) for arra...  3.54 us
    ppermute x7, waiting for transfers between devices, swap(): return lax.ppermute(values, 'sub', [(i, i ^ 1) for i in range(2)])  1.55 us
    pallas_call x1, Pallas kernels, dec_gradient(): pl.pallas_call(kernel, out_shape=[jax.ShapeDtypeStruct(a.shape, a.dtype)...  1.51 us
    pallas_call x1, Pallas kernels, store(): pl.pallas_call(kernel, out_shape=[jax.ShapeDtypeStruct(a.shape, a.dtype)...  1.51 us
  transfers between devices with their start and end apart: 22, of which 16 were waited for; matrix products, arithmetic and copies ran while one was open for 0% of the time, Pallas kernels for 18%

profile of v5, /device:TPU:0, one launch (start us, length us, event | category | flops | bytes accessed | tf_op | source)
XLA Modules:
  0.0 53.0 jit_solution(15687492151666797609)
XLA Ops:
  1.2 4.0 %collective-permute-start = (bf16[2,5120]{1,0:T(2,128)(2,1)}, bf16[2,5120]{1,0:T(2,128)(2,1)S(1)}, u32[]{:S(2)}, u32[]{:S(2)}) collective-permute-start(bf16[2,5120]{1,0:T(2,128)(2,1)} %refs_1_.1), channel_id=1, source_target_pairs={{0,8},{2,10},{4,12},{6,14},{8,0},{10,2},{12,4},{14,6},{1,9},{3,11}... | collective-permute-start | bytes 61448 | tf_op jit(solution)/shard_map/ppermute | solution.py:52
  5.2 1.8 %load.2 = (bf16[5120,256]{1,0:T(8,128)(2,1)S(1)}, bf16[2,5120]{1,0:T(2,128)(2,1)S(1)}, f32[1,5120]{1,0:T(1,128)S(1)}, f32[1,256]{1,0:T(1,128)S(1)}) custom-call(bf16[5120,256]{1,0:T(8,128)(2,1)} %refs_0_.2, bf16[2,5120]{1,0:T(2,128)(2,1)} %refs_1_.1, f32[1,5120]{1,0:T(1,128)} %bitcast.5, f32[1,256]{1,0:T(1,128)} %bitcast.6), custom_call_target="tpu_custom_call" | custom-call | bytes 5326848 | tf_op jit(solution)/shard_map/load/pallas_call | solution.py:77
  7.3 2.9 %collective-permute-start.3 = (bf16[4,5120]{1,0:T(4,128)(2,1)S(1)}, bf16[4,5120]{1,0:T(4,128)(2,1)S(1)}, u32[]{:S(2)}, u32[]{:S(2)}) collective-permute-start(bf16[4,5120]{1,0:T(4,128)(2,1)S(1)} %stack.3.refs_1_.refs_0_.refs_2_), channel_id=1, source_target_pairs={{0,6},{2,4},{4,2},{6,0},{8,14},{10,12},{12,10},{14,8},{1,7},{3,5},... | collective-permute-start | bytes 122888 | tf_op jit(solution)/shard_map/ppermute | solution.py:52
  10.8 1.5 %collective-permute-done.3.refs_3_ = bf16[4,5120]{1,0:T(4,128)(2,1)S(1)} collective-permute-done((bf16[4,5120]{1,0:T(4,128)(2,1)S(1)}, bf16[4,5120]{1,0:T(4,128)(2,1)S(1)}, u32[]{:S(2)}, u32[]{:S(2)}) %collective-permute-start.3) | collective-permute-done | bytes 40992 | tf_op jit(solution)/shard_map/ppermute | solution.py:52
  12.3 1.7 %load.3.refs_4_.refs_0_ = bf16[256,5120]{1,0:T(8,128)(2,1)S(1)} custom-call(bf16[256,5120]{1,0:T(8,128)(2,1)} %refs_0_.3, bf16[4,5120]{1,0:T(4,128)(2,1)S(1)} %stack.3.refs_1_.refs_0_.refs_2_), custom_call_target="tpu_custom_call" | custom-call | bytes 5242880 | tf_op jit(solution)/shard_map/load/pallas_call | solution.py:77
  14.8 1.6 %encode_decode.1 = (bf16[16,5120]{1,0:T(8,128)(2,1)S(1)}, f32[16,256]{1,0:T(8,128)S(1)}, f32[16,256]{1,0:T(8,128)S(1)}, f32[4,5120]{1,0:T(4,128)S(1)}, f32[4,512...) custom-call(bf16[16,5120]{1,0:T(8,128)(2,1)S(1)} %stack.4.refs_0_, ...), custom_call_target="tpu_custom_call" | custom-call | flops 167772160 | tf_op jit(solution)/shard_map/encode_decode/pallas_call | solution.py:38
  16.3 1.4 %collective-permute-start.8 = (f32[4,5120]{1,0:T(4,128)S(1)}, f32[4,5120]{1,0:T(4,128)S(1)}, u32[]{:S(2)}, u32[]{:S(2)}) collective-permute-start(f32[4,5120]{1,0:T(4,128)S(1)} %get-tuple-element.37), channel_id=1, source_target_pairs={{0,4},{2,6},{4,0},{6,2},{8,12},{10,14},{12,8},{14,10},{1,5},{3,7},... | collective-permute-start | bytes 245768 | tf_op jit(solution)/shard_map/ppermute | solution.py:52
  17.8 1.3 %collective-permute-start.9 = (f32[4,5120]{1,0:T(4,128)S(1)}, f32[4,5120]{1,0:T(4,128)S(1)}, u32[]{:S(2)}, u32[]{:S(2)}) collective-permute-start(f32[4,5120]{1,0:T(4,128)S(1)} %get-tuple-element.38), channel_id=1, source_target_pairs={{0,2},{2,0},{4,6},{6,4},{8,10},{10,8},{12,14},{14,12},{1,3},{3,1},... | collective-permute-start | bytes 245768 | tf_op jit(solution)/shard_map/ppermute | solution.py:52
  19.1 0.8 %collective-permute-start.10 = (f32[4,5120]{1,0:T(4,128)S(1)}, f32[4,5120]{1,0:T(4,128)S(1)}, u32[]{:S(2)}, u32[]{:S(2)}) collective-permute-start(f32[4,5120]{1,0:T(4,128)S(1)} %get-tuple-element.39), channel_id=1, source_target_pairs={{0,6},{2,4},{4,2},{6,0},{8,14},{10,12},{12,10},{14,8},{1,7},{3,5},... | collective-permute-start | bytes 245768 | tf_op jit(solution)/shard_map/ppermute | solution.py:52
  19.9 0.7 %turn.2.refs_4_.refs_2_ = bf16[5120,256]{1,0:T(8,128)(2,1)S(1)} custom-call(bf16[256,5120]{1,0:T(8,128)(2,1)S(1)} %load.3.refs_4_.refs_0_, f32[4,5120]{1,0:T(4,128)S(1)} %get-tuple-element.36.refs_1_.refs_0_), custom_call_target="tpu_custom_call" | custom-call | bytes 5242880 | tf_op jit(solution)/shard_map/turn/pallas_call | solution.py:38
  20.9 2.1 %collective-permute-done.9.refs_2_ = f32[4,5120]{1,0:T(4,128)S(1)} collective-permute-done((f32[4,5120]{1,0:T(4,128)S(1)}, f32[4,5120]{1,0:T(4,128)S(1)}, u32[]{:S(2)}, u32[]{:S(2)}) %collective-permute-start.9) | collective-permute-done | bytes 81952 | tf_op jit(solution)/shard_map/ppermute | solution.py:52
  23.0 1.5 %collective-permute-done.10.refs_3_ = f32[4,5120]{1,0:T(4,128)S(1)} collective-permute-done((f32[4,5120]{1,0:T(4,128)S(1)}, f32[4,5120]{1,0:T(4,128)S(1)}, u32[]{:S(2)}, u32[]{:S(2)}) %collective-permute-start.10) | collective-permute-done | bytes 81952 | tf_op jit(solution)/shard_map/ppermute | solution.py:52
  24.4 2.8 %collective-permute-start.11 = (f32[4,5120]{1,0:T(4,128)S(1)}, f32[4,5120]{1,0:T(4,128)S(1)}, u32[]{:S(2)}, u32[]{:S(2)}) collective-permute-start(f32[4,5120]{1,0:T(4,128)S(1)} %add_parts.1.refs_1_.refs_0_), channel_id=1, source_target_pairs={{0,8},{2,10},{4,12},{6,14},{8,0},{10,2},{12,4},{14,6},{1,9},{3,11}... | collective-permute-start | bytes 245768 | tf_op jit(solution)/shard_map/ppermute | solution.py:52
  27.2 0.8 %turn.3.refs_4_.refs_1_ = bf16[256,5120]{1,0:T(8,128)(2,1)S(1)} custom-call(bf16[5120,256]{1,0:T(8,128)(2,1)S(1)} %get-tuple-element.31.refs_2_.refs_0_, f32[4,5120]{1,0:T(4,128)S(1)} %add_parts.1.refs_1_.refs_0_), custom_call_target="tpu_custom_call" | custom-call | bytes 5242880 | tf_op jit(solution)/shard_map/turn/pallas_call | solution.py:38
  28.4 2.3 %collective-permute-done.11.refs_1_ = f32[4,5120]{1,0:T(4,128)S(1)} collective-permute-done((f32[4,5120]{1,0:T(4,128)S(1)}, f32[4,5120]{1,0:T(4,128)S(1)}, u32[]{:S(2)}, u32[]{:S(2)}) %collective-permute-start.11) | collective-permute-done | bytes 81952 | tf_op jit(solution)/shard_map/ppermute | solution.py:52
  30.8 0.6 %collective-permute-start.15 = (bf16[4,5120]{1,0:T(4,128)(2,1)S(1)}, bf16[4,5120]{1,0:T(4,128)(2,1)S(1)}, u32[]{:S(2)}, u32[]{:S(2)}) collective-permute-start(bf16[4,5120]{1,0:T(4,128)(2,1)S(1)} %residual_gradient.1.refs_0_.refs_4_), channel_id=1, source_target_pairs={{0,6},{2,4},{4,2},{6,0},{8,14},{10,12},{12,10},{14,8},{1,7},{3,5},... | collective-permute-start | bytes 122888 | tf_op jit(solution)/shard_map/ppermute | solution.py:52
  31.4 1.0 %collective-permute-start.14 = (bf16[4,5120]{1,0:T(4,128)(2,1)S(1)}, bf16[4,5120]{1,0:T(4,128)(2,1)S(1)}, u32[]{:S(2)}, u32[]{:S(2)}) collective-permute-start(bf16[4,5120]{1,0:T(4,128)(2,1)S(1)} %residual_gradient.1.refs_0_.refs_4_), channel_id=1, source_target_pairs={{0,2},{2,0},{4,6},{6,4},{8,10},{10,8},{12,14},{14,12},{1,3},{3,1},... | collective-permute-start | bytes 122888 | tf_op jit(solution)/shard_map/ppermute | solution.py:52
  32.4 1.9 %collective-permute-start.13 = (bf16[4,5120]{1,0:T(4,128)(2,1)S(1)}, bf16[4,5120]{1,0:T(4,128)(2,1)S(1)}, u32[]{:S(2)}, u32[]{:S(2)}) collective-permute-start(bf16[4,5120]{1,0:T(4,128)(2,1)S(1)} %residual_gradient.1.refs_0_.refs_4_), channel_id=1, source_target_pairs={{0,4},{2,6},{4,0},{6,2},{8,12},{10,14},{12,8},{14,10},{1,5},{3,7},... | collective-permute-start | bytes 122888 | tf_op jit(solution)/shard_map/ppermute | solution.py:52
  34.3 1.5 %collective-permute-done.15.refs_3_ = bf16[4,5120]{1,0:T(4,128)(2,1)S(1)} collective-permute-done((bf16[4,5120]{1,0:T(4,128)(2,1)S(1)}, bf16[4,5120]{1,0:T(4,128)(2,1)S(1)}, u32[]{:S(2)}, u32[]{:S(2)}) %collective-permute-start.15) | collective-permute-done | bytes 40992 | tf_op jit(solution)/shard_map/ppermute | solution.py:52
  35.8 0.6 %collective-permute-done.13.refs_1_ = bf16[4,5120]{1,0:T(4,128)(2,1)S(1)} collective-permute-done((bf16[4,5120]{1,0:T(4,128)(2,1)S(1)}, bf16[4,5120]{1,0:T(4,128)(2,1)S(1)}, u32[]{:S(2)}, u32[]{:S(2)}) %collective-permute-start.13) | collective-permute-done | bytes 40992 | tf_op jit(solution)/shard_map/ppermute | solution.py:52
  37.0 1.0 %collective-permute-done.16.refs_1_.refs_3_ = bf16[16,5120]{1,0:T(8,128)(2,1)S(1)} collective-permute-done((bf16[16,5120]{1,0:T(8,128)(2,1)S(1)}, bf16[16,5120]{1,0:T(8,128)(2,1)S(1)}, u32[]{:S(2)}, u32[]{:S(2)}) %collective-permute-start.16) | collective-permute-done | bytes 163872 | tf_op jit(solution)/shard_map/ppermute | solution.py:51
  38.0 0.6 %backward.1 = (bf16[32,256]{1,0:T(8,128)(2,1)S(1)}, f32[1,256]{1,0:T(1,128)S(1)}) custom-call(bf16[16,5120]{1,0:T(8,128)(2,1)S(1)} %stack.5.refs_0_.refs_2_, bf16[16,5120]{1,0:T(8,128)(2,1)S(1)} %collective-permute-done.16.refs_1_.refs_3_, bf16[5120,256]{1,0:T(8,128)(2,1)S(1)} %turn.2.refs_4_.refs_2_, f32[16,256]{1,0:T(8,128)S(1)} %get-tuple-element.34.refs_3_.refs_0_, ...), custom_call_target="tpu_custom_call" | custom-call | tf_op jit(solution)/shard_map/backward/pallas_call | solution.py:38
  39.2 0.9 %enc_gradient.1.refs_2_.refs_4_ = bf16[5120,256]{1,0:T(8,128)(2,1)S(1)} custom-call(bf16[16,5120]{1,0:T(8,128)(2,1)S(1)} %get-tuple-element.40.refs_0_, bf16[16,5120]{1,0:T(8,128)(2,1)S(1)} %collective-permute-done.12.refs_6_.refs_1_, bf16[32,256]{1,0:T(8,128)(2,1)S(1)} %get-tuple-element.41.refs_2_, f32[1,5248]{1,0:T(1,128)S(1)} %bias_product.1.refs_3_.refs_0_), custom_call_target="tpu_custom_call" | custom-call | flops 83886080 | tf_op jit(solution)/shard_map/enc_gradient/pallas_call | solution.py:38
  40.3 2.3 %collective-permute-start.20 = (f32[1,5248]{1,0:T(1,128)S(1)}, f32[1,5248]{1,0:T(1,128)S(1)}, u32[]{:S(2)}, u32[]{:S(2)}) collective-permute-start(f32[1,5248]{1,0:T(1,128)S(1)} %add.2.refs_6_.refs_0_), channel_id=1, source_target_pairs={{0,6},{2,4},{4,2},{6,0},{8,14},{10,12},{12,10},{14,8},{1,7},{3,5},... | collective-permute-start | bytes 62984 | tf_op jit(solution)/shard_map/ppermute | solution.py:52
  42.6 1.0 %collective-permute-start.19 = (f32[1,5248]{1,0:T(1,128)S(1)}, f32[1,5248]{1,0:T(1,128)S(1)}, u32[]{:S(2)}, u32[]{:S(2)}) collective-permute-start(f32[1,5248]{1,0:T(1,128)S(1)} %add.2.refs_6_.refs_0_), channel_id=1, source_target_pairs={{0,2},{2,0},{4,6},{6,4},{8,10},{10,8},{12,14},{14,12},{1,3},{3,1},... | collective-permute-start | bytes 62984 | tf_op jit(solution)/shard_map/ppermute | solution.py:52
  43.7 1.5 %dec_gradient.1 = (bf16[5120,256]{1,0:T(8,128)(2,1)}, f32[1,256]{1,0:T(1,128)}, bf16[256,5120]{1,0:T(8,128)(2,1)S(1)}) custom-call(f32[16,256]{1,0:T(8,128)S(1)} %get-tuple-element.34.refs_3_.refs_0_, f32[16,256]{1,0:T(8,128)S(1)} %collective-permute-done.7.refs_5_.refs_4_.refs_1_, bf16[16,5120]{1,0:T(8,128)(2,1)S(1)} %stack.5.refs_0_.refs_2_, ...), custom_call_target="tpu_custom_call" | custom-call | flops 83886080 | bytes 5242880 | tf_op jit(solution)/shard_map/dec_gradient/pallas_call | solution.py:304
  45.3 1.1 %collective-permute-done.19.refs_2_ = f32[1,5248]{1,0:T(1,128)S(1)} collective-permute-done((f32[1,5248]{1,0:T(1,128)S(1)}, f32[1,5248]{1,0:T(1,128)S(1)}, u32[]{:S(2)}, u32[]{:S(2)}) %collective-permute-start.19) | collective-permute-done | bytes 21024 | tf_op jit(solution)/shard_map/ppermute | solution.py:52
  46.4 1.0 %collective-permute-done.18.refs_1_ = f32[1,5248]{1,0:T(1,128)S(1)} collective-permute-done((f32[1,5248]{1,0:T(1,128)S(1)}, f32[1,5248]{1,0:T(1,128)S(1)}, u32[]{:S(2)}, u32[]{:S(2)}) %collective-permute-start.18) | collective-permute-done | bytes 21024 | tf_op jit(solution)/shard_map/ppermute | solution.py:52
  47.4 2.0 %collective-permute-start.21 = (f32[1,5248]{1,0:T(1,128)S(1)}, f32[1,5248]{1,0:T(1,128)S(1)}, u32[]{:S(2)}, u32[]{:S(2)}) collective-permute-start(f32[1,5248]{1,0:T(1,128)S(1)} %add.3.refs_2_.terms_ref), channel_id=1, source_target_pairs={{0,8},{2,10},{4,12},{6,14},{8,0},{10,2},{12,4},{14,6},{1,9},{3,11}... | collective-permute-start | bytes 62984 | tf_op jit(solution)/shard_map/ppermute | solution.py:52
  49.4 1.5 %store.1 = (bf16[256,5120]{1,0:T(8,128)(2,1)}, bf16[2,5120]{1,0:T(2,128)(2,1)}, f32[8,128]{1,0:T(8,128)S(1)}) custom-call(bf16[256,5120]{1,0:T(8,128)(2,1)S(1)} %get-tuple-element.45.refs_4_.refs_0_, bf16[2,5120]{1,0:T(2,128)(2,1)S(1)} %get-tuple-element.46.refs_1_, f32[1,5248]{1,0:T(1,128)S(1)} %add.3.refs_2_.terms_ref), custom_call_target="tpu_custom_call" | custom-call | bytes 5283840 | tf_op jit(solution)/shard_map/store/pallas_call | solution.py:329
  50.9 1.5 %collective-permute-done.21.other_ref = f32[1,5248]{1,0:T(1,128)S(1)} collective-permute-done((f32[1,5248]{1,0:T(1,128)S(1)}, f32[1,5248]{1,0:T(1,128)S(1)}, u32[]{:S(2)}, u32[]{:S(2)}) %collective-permute-start.21) | collective-permute-done | bytes 21024 | tf_op jit(solution)/shard_map/ppermute | solution.py:52
  52.4 0.6 %finish.1 = (f32[1,5120]{1,0:T(1,128)}, f32[1,1]{1,0:T(1,128)}) custom-call(f32[1,5248]{1,0:T(1,128)S(1)} %add.3.refs_2_.terms_ref, f32[1,5248]{1,0:T(1,128)S(1)} %collective-permute-done.21.other_ref, f32[8,128]{1,0:T(8,128)S(1)} %get-tuple-element.48.after_ref), custom_call_target="tpu_custom_call" | custom-call | tf_op jit(solution)/shard_map/finish/pallas_call | solution.py:361
  (34 shorter events, 4.4 us)
Async XLA Ops:
  0.6 14.1 %collective-permute-start.4 = (bf16[5120,256]{1,0:T(8,128)(2,1)}, bf16[5120,256]{1,0:T(8,128)(2,1)S(1)}, u32[]{:S(2)}, u32[]{:S(2)}) collective-permute-start(bf16[5120,256]{1,0:T(8,128)(2,1)} %refs_0_.2), channel_id=1, source_target_pairs={{0,1},{1,0},{2,3},{3,2},{4,5},{5,4},{6,7},{7,6},{8,9},{9,8},{10,11... | collective-permute-start | bytes 7864328 | tf_op jit(solution)/shard_map/ppermute | solution.py:51
  1.2 13.6 %collective-permute-start.6 = (bf16[256,5120]{1,0:T(8,128)(2,1)}, bf16[256,5120]{1,0:T(8,128)(2,1)S(1)}, u32[]{:S(2)}, u32[]{:S(2)}) collective-permute-start(bf16[256,5120]{1,0:T(8,128)(2,1)} %refs_0_.3), channel_id=1, source_target_pairs={{0,1},{1,0},{2,3},{3,2},{4,5},{5,4},{6,7},{7,6},{8,9},{9,8},{10,11... | collective-permute-start | bytes 7864328 | tf_op jit(solution)/shard_map/ppermute | solution.py:51
  1.2 6.0 %collective-permute-start = (bf16[2,5120]{1,0:T(2,128)(2,1)}, bf16[2,5120]{1,0:T(2,128)(2,1)S(1)}, u32[]{:S(2)}, u32[]{:S(2)}) collective-permute-start(bf16[2,5120]{1,0:T(2,128)(2,1)} %refs_1_.1), channel_id=1, source_target_pairs={{0,8},{2,10},{4,12},{6,14},{8,0},{10,2},{12,4},{14,6},{1,9},{3,11}... | collective-permute-start | bytes 61448 | tf_op jit(solution)/shard_map/ppermute | solution.py:52
  5.2 7.0 %copy-start = (f32[256]{0:T(256)S(1)}, f32[256]{0:T(256)}, u32[]{:S(2)}) copy-start(f32[256]{0:T(256)} %param.7) | copy-start | bytes 3076
  7.3 5.0 %collective-permute-start.3 = (bf16[4,5120]{1,0:T(4,128)(2,1)S(1)}, bf16[4,5120]{1,0:T(4,128)(2,1)S(1)}, u32[]{:S(2)}, u32[]{:S(2)}) collective-permute-start(bf16[4,5120]{1,0:T(4,128)(2,1)S(1)} %stack.3.refs_1_.refs_0_.refs_2_), channel_id=1, source_target_pairs={{0,6},{2,4},{4,2},{6,0},{8,14},{10,12},{12,10},{14,8},{1,7},{3,5},... | collective-permute-start | bytes 122888 | tf_op jit(solution)/shard_map/ppermute | solution.py:52
  10.2 4.0 %collective-permute-start.2 = (bf16[4,5120]{1,0:T(4,128)(2,1)S(1)}, bf16[4,5120]{1,0:T(4,128)(2,1)S(1)}, u32[]{:S(2)}, u32[]{:S(2)}) collective-permute-start(bf16[4,5120]{1,0:T(4,128)(2,1)S(1)} %stack.3.refs_1_.refs_0_.refs_2_), channel_id=1, source_target_pairs={{0,2},{2,0},{4,6},{6,4},{8,10},{10,8},{12,14},{14,12},{1,3},{3,1},... | collective-permute-start | bytes 122888 | tf_op jit(solution)/shard_map/ppermute | solution.py:52
  10.7 4.0 %collective-permute-start.1 = (bf16[4,5120]{1,0:T(4,128)(2,1)S(1)}, bf16[4,5120]{1,0:T(4,128)(2,1)S(1)}, u32[]{:S(2)}, u32[]{:S(2)}) collective-permute-start(bf16[4,5120]{1,0:T(4,128)(2,1)S(1)} %stack.3.refs_1_.refs_0_.refs_2_), channel_id=1, source_target_pairs={{0,4},{2,6},{4,0},{6,2},{8,12},{10,14},{12,8},{14,10},{1,5},{3,7},... | collective-permute-start | bytes 122888 | tf_op jit(solution)/shard_map/ppermute | solution.py:52
  12.3 2.5 %collective-permute-start.5 = (f32[1,256]{1,0:T(1,128)S(1)}, f32[1,256]{1,0:T(1,128)S(1)}, u32[]{:S(2)}, u32[]{:S(2)}) collective-permute-start(f32[1,256]{1,0:T(1,128)S(1)} %bitcast.7), channel_id=1, source_target_pairs={{0,1},{1,0},{2,3},{3,2},{4,5},{5,4},{6,7},{7,6},{8,9},{9,8},{10,11... | collective-permute-start | bytes 3080 | tf_op jit(solution)/shard_map/ppermute | solution.py:51
  16.3 4.5 %collective-permute-start.8 = (f32[4,5120]{1,0:T(4,128)S(1)}, f32[4,5120]{1,0:T(4,128)S(1)}, u32[]{:S(2)}, u32[]{:S(2)}) collective-permute-start(f32[4,5120]{1,0:T(4,128)S(1)} %get-tuple-element.37), channel_id=1, source_target_pairs={{0,4},{2,6},{4,0},{6,2},{8,12},{10,14},{12,8},{14,10},{1,5},{3,7},... | collective-permute-start | bytes 245768 | tf_op jit(solution)/shard_map/ppermute | solution.py:52
  17.8 5.2 %collective-permute-start.9 = (f32[4,5120]{1,0:T(4,128)S(1)}, f32[4,5120]{1,0:T(4,128)S(1)}, u32[]{:S(2)}, u32[]{:S(2)}) collective-permute-start(f32[4,5120]{1,0:T(4,128)S(1)} %get-tuple-element.38), channel_id=1, source_target_pairs={{0,2},{2,0},{4,6},{6,4},{8,10},{10,8},{12,14},{14,12},{1,3},{3,1},... | collective-permute-start | bytes 245768 | tf_op jit(solution)/shard_map/ppermute | solution.py:52
  19.1 5.3 %collective-permute-start.10 = (f32[4,5120]{1,0:T(4,128)S(1)}, f32[4,5120]{1,0:T(4,128)S(1)}, u32[]{:S(2)}, u32[]{:S(2)}) collective-permute-start(f32[4,5120]{1,0:T(4,128)S(1)} %get-tuple-element.39), channel_id=1, source_target_pairs={{0,6},{2,4},{4,2},{6,0},{8,14},{10,12},{12,10},{14,8},{1,7},{3,5},... | collective-permute-start | bytes 245768 | tf_op jit(solution)/shard_map/ppermute | solution.py:52
  19.9 10.9 %collective-permute-start.12 = (bf16[16,5120]{1,0:T(8,128)(2,1)S(1)}, bf16[16,5120]{1,0:T(8,128)(2,1)S(1)}, u32[]{:S(2)}, u32[]{:S(2)}) collective-permute-start(bf16[16,5120]{1,0:T(8,128)(2,1)S(1)} %get-tuple-element.40.refs_0_), channel_id=1, source_target_pairs={{0,1},{1,0},{2,3},{3,2},{4,5},{5,4},{6,7},{7,6},{8,9},{9,8},{10,11... | collective-permute-start | bytes 491528 | tf_op jit(solution)/shard_map/ppermute | solution.py:51
  24.4 6.3 %collective-permute-start.11 = (f32[4,5120]{1,0:T(4,128)S(1)}, f32[4,5120]{1,0:T(4,128)S(1)}, u32[]{:S(2)}, u32[]{:S(2)}) collective-permute-start(f32[4,5120]{1,0:T(4,128)S(1)} %add_parts.1.refs_1_.refs_0_), channel_id=1, source_target_pairs={{0,8},{2,10},{4,12},{6,14},{8,0},{10,2},{12,4},{14,6},{1,9},{3,11}... | collective-permute-start | bytes 245768 | tf_op jit(solution)/shard_map/ppermute | solution.py:52
  27.2 1.2 %collective-permute-start.7 = (f32[16,256]{1,0:T(8,128)S(1)}, f32[16,256]{1,0:T(8,128)S(1)}, u32[]{:S(2)}, u32[]{:S(2)}) collective-permute-start(f32[16,256]{1,0:T(8,128)S(1)} %get-tuple-element.35), channel_id=1, source_target_pairs={{0,1},{1,0},{2,3},{3,2},{4,5},{5,4},{6,7},{7,6},{8,9},{9,8},{10,11... | collective-permute-start | bytes 49160 | tf_op jit(solution)/shard_map/ppermute | solution.py:51
  30.8 5.1 %collective-permute-start.15 = (bf16[4,5120]{1,0:T(4,128)(2,1)S(1)}, bf16[4,5120]{1,0:T(4,128)(2,1)S(1)}, u32[]{:S(2)}, u32[]{:S(2)}) collective-permute-start(bf16[4,5120]{1,0:T(4,128)(2,1)S(1)} %residual_gradient.1.refs_0_.refs_4_), channel_id=1, source_target_pairs={{0,6},{2,4},{4,2},{6,0},{8,14},{10,12},{12,10},{14,8},{1,7},{3,5},... | collective-permute-start | bytes 122888 | tf_op jit(solution)/shard_map/ppermute | solution.py:52
  31.4 4.4 %collective-permute-start.14 = (bf16[4,5120]{1,0:T(4,128)(2,1)S(1)}, bf16[4,5120]{1,0:T(4,128)(2,1)S(1)}, u32[]{:S(2)}, u32[]{:S(2)}) collective-permute-start(bf16[4,5120]{1,0:T(4,128)(2,1)S(1)} %residual_gradient.1.refs_0_.refs_4_), channel_id=1, source_target_pairs={{0,2},{2,0},{4,6},{6,4},{8,10},{10,8},{12,14},{14,12},{1,3},{3,1},... | collective-permute-start | bytes 122888 | tf_op jit(solution)/shard_map/ppermute | solution.py:52
  32.4 4.0 %collective-permute-start.13 = (bf16[4,5120]{1,0:T(4,128)(2,1)S(1)}, bf16[4,5120]{1,0:T(4,128)(2,1)S(1)}, u32[]{:S(2)}, u32[]{:S(2)}) collective-permute-start(bf16[4,5120]{1,0:T(4,128)(2,1)S(1)} %residual_gradient.1.refs_0_.refs_4_), channel_id=1, source_target_pairs={{0,4},{2,6},{4,0},{6,2},{8,12},{10,14},{12,8},{14,10},{1,5},{3,7},... | collective-permute-start | bytes 122888 | tf_op jit(solution)/shard_map/ppermute | solution.py:52
  36.5 1.5 %collective-permute-start.16 = (bf16[16,5120]{1,0:T(8,128)(2,1)S(1)}, bf16[16,5120]{1,0:T(8,128)(2,1)S(1)}, u32[]{:S(2)}, u32[]{:S(2)}) collective-permute-start(bf16[16,5120]{1,0:T(8,128)(2,1)S(1)} %stack.5.refs_0_.refs_2_), channel_id=1, source_target_pairs={{0,1},{1,0},{2,3},{3,2},{4,5},{5,4},{6,7},{7,6},{8,9},{9,8},{10,11... | collective-permute-start | bytes 491528 | tf_op jit(solution)/shard_map/ppermute | solution.py:51
  39.0 1.3 %collective-permute-start.17 = (f32[1,5248]{1,0:T(1,128)S(1)}, f32[1,5248]{1,0:T(1,128)S(1)}, u32[]{:S(2)}, u32[]{:S(2)}) collective-permute-start(f32[1,5248]{1,0:T(1,128)S(1)} %bias_product.1.refs_3_.refs_0_), channel_id=1, source_target_pairs={{0,1},{1,0},{2,3},{3,2},{4,5},{5,4},{6,7},{7,6},{8,9},{9,8},{10,11... | collective-permute-start | bytes 62984 | tf_op jit(solution)/shard_map/ppermute | solution.py:51
  40.3 5.0 %collective-permute-start.20 = (f32[1,5248]{1,0:T(1,128)S(1)}, f32[1,5248]{1,0:T(1,128)S(1)}, u32[]{:S(2)}, u32[]{:S(2)}) collective-permute-start(f32[1,5248]{1,0:T(1,128)S(1)} %add.2.refs_6_.refs_0_), channel_id=1, source_target_pairs={{0,6},{2,4},{4,2},{6,0},{8,14},{10,12},{12,10},{14,8},{1,7},{3,5},... | collective-permute-start | bytes 62984 | tf_op jit(solution)/shard_map/ppermute | solution.py:52
  42.6 3.8 %collective-permute-start.19 = (f32[1,5248]{1,0:T(1,128)S(1)}, f32[1,5248]{1,0:T(1,128)S(1)}, u32[]{:S(2)}, u32[]{:S(2)}) collective-permute-start(f32[1,5248]{1,0:T(1,128)S(1)} %add.2.refs_6_.refs_0_), channel_id=1, source_target_pairs={{0,2},{2,0},{4,6},{6,4},{8,10},{10,8},{12,14},{14,12},{1,3},{3,1},... | collective-permute-start | bytes 62984 | tf_op jit(solution)/shard_map/ppermute | solution.py:52
  43.6 3.8 %collective-permute-start.18 = (f32[1,5248]{1,0:T(1,128)S(1)}, f32[1,5248]{1,0:T(1,128)S(1)}, u32[]{:S(2)}, u32[]{:S(2)}) collective-permute-start(f32[1,5248]{1,0:T(1,128)S(1)} %add.2.refs_6_.refs_0_), channel_id=1, source_target_pairs={{0,4},{2,6},{4,0},{6,2},{8,12},{10,14},{12,8},{14,10},{1,5},{3,7},... | collective-permute-start | bytes 62984 | tf_op jit(solution)/shard_map/ppermute | solution.py:52
  47.4 5.0 %collective-permute-start.21 = (f32[1,5248]{1,0:T(1,128)S(1)}, f32[1,5248]{1,0:T(1,128)S(1)}, u32[]{:S(2)}, u32[]{:S(2)}) collective-permute-start(f32[1,5248]{1,0:T(1,128)S(1)} %add.3.refs_2_.terms_ref), channel_id=1, source_target_pairs={{0,8},{2,10},{4,12},{6,14},{8,0},{10,2},{12,4},{14,6},{1,9},{3,11}... | collective-permute-start | bytes 62984 | tf_op jit(solution)/shard_map/ppermute | solution.py:52

commit v6 on v5

--- a/solution.py
+++ b/solution.py
@@ -52,7 +52,7 @@
     return lax.ppermute(values, "lat", [(i, i ^ mask) for i in range(lax.axis_size("lat"))])
 
 
-ROWS_ORDER, SUM_ORDER, RESID_ORDER, TERMS_ORDER = (2, 1, 3), (2, 1, 3), (2, 1, 3), (2, 1, 3)
+ROWS_ORDER, SUM_ORDER, RESID_ORDER, TERMS_ORDER = (2, 3, 1), (1, 3, 2), (2, 1, 3), (2, 3, 1)
 
 
 def plan(lat):

time: 53.2 us -> 52.1 us (0.979)
  waiting for transfers between devices: 15.7 us -> 13.7 us
  starting transfers between devices: 23.8 us -> 24.7 us
    ppermute x15, waiting for transfers between devices: 14.2 us -> 12.1 us  [swap(): lax.ppermute(values, 'lat', [(i, i ^ mask) for i in range(lax.axis_size('...]
    ppermute x15, starting transfers between devices: 22.9 us -> 23.8 us  [swap(): lax.ppermute(values, 'lat', [(i, i ^ mask) for i in range(lax.axis_size('...]
where the time goes in v6:
time: 52.1 us; the launch traced here: 52 us
  starting transfers between devices  24.7 us (47%)
  waiting for transfers between devices  13.7 us (26%)
  Pallas kernels  12.8 us (25%)
  between operations  0.78 us (1%)
    ppermute x15, starting transfers between devices, swap(): lax.ppermute(values, 'lat', [(i, i ^ mask) for i in range(lax.axis_size('...  23.8 us
    ppermute x15, waiting for transfers between devices, swap(): lax.ppermute(values, 'lat', [(i, i ^ mask) for i in range(lax.axis_size('...  12.1 us
    pallas_call x15, Pallas kernels, run(): pl.pallas_call(body, out_shape=[vmem(*out) for out in outs], in_specs=[VM...  5.61 us
    pallas_call x2, Pallas kernels, load(): pl.pallas_call(kernel, out_shape=[vmem(array.shape, array.dtype) for arra...  3.54 us
    ppermute x7, waiting for transfers between devices, swap(): return lax.ppermute(values, 'sub', [(i, i ^ 1) for i in range(2)])  1.55 us
    pallas_call x1, Pallas kernels, dec_gradient(): pl.pallas_call(kernel, out_shape=[jax.ShapeDtypeStruct(a.shape, a.dtype)...  1.51 us
    pallas_call x1, Pallas kernels, store(): pl.pallas_call(kernel, out_shape=[jax.ShapeDtypeStruct(a.shape, a.dtype)...  1.51 us
  transfers between devices with their start and end apart: 22, of which 16 were waited for; matrix products, arithmetic and copies ran while one was open for 0% of the time, Pallas kernels for 18%

profile of v6, /device:TPU:0, one launch (start us, length us, event | category | flops | bytes accessed | tf_op | source)
XLA Modules:
  0.0 52.0 jit_solution(8573122770385159725)
XLA Ops:
  1.2 4.0 %collective-permute-start = (bf16[2,5120]{1,0:T(2,128)(2,1)}, bf16[2,5120]{1,0:T(2,128)(2,1)S(1)}, u32[]{:S(2)}, u32[]{:S(2)}) collective-permute-start(bf16[2,5120]{1,0:T(2,128)(2,1)} %refs_1_.1), channel_id=1, source_target_pairs={{0,8},{2,10},{4,12},{6,14},{8,0},{10,2},{12,4},{14,6},{1,9},{3,11}... | collective-permute-start | bytes 61448 | tf_op jit(solution)/shard_map/ppermute | solution.py:52
  5.2 1.8 %load.2 = (bf16[5120,256]{1,0:T(8,128)(2,1)S(1)}, bf16[2,5120]{1,0:T(2,128)(2,1)S(1)}, f32[1,5120]{1,0:T(1,128)S(1)}, f32[1,256]{1,0:T(1,128)S(1)}) custom-call(bf16[5120,256]{1,0:T(8,128)(2,1)} %refs_0_.2, bf16[2,5120]{1,0:T(2,128)(2,1)} %refs_1_.1, f32[1,5120]{1,0:T(1,128)} %bitcast.5, f32[1,256]{1,0:T(1,128)} %bitcast.6), custom_call_target="tpu_custom_call" | custom-call | bytes 5326848 | tf_op jit(solution)/shard_map/load/pallas_call | solution.py:77
  7.3 1.9 %collective-permute-start.3 = (bf16[4,5120]{1,0:T(4,128)(2,1)S(1)}, bf16[4,5120]{1,0:T(4,128)(2,1)S(1)}, u32[]{:S(2)}, u32[]{:S(2)}) collective-permute-start(bf16[4,5120]{1,0:T(4,128)(2,1)S(1)} %stack.3.refs_1_.refs_0_.refs_2_), channel_id=1, source_target_pairs={{0,2},{2,0},{4,6},{6,4},{8,10},{10,8},{12,14},{14,12},{1,3},{3,1},... | collective-permute-start | bytes 122888 | tf_op jit(solution)/shard_map/ppermute | solution.py:52
  9.2 1.5 %collective-permute-start.2 = (bf16[4,5120]{1,0:T(4,128)(2,1)S(1)}, bf16[4,5120]{1,0:T(4,128)(2,1)S(1)}, u32[]{:S(2)}, u32[]{:S(2)}) collective-permute-start(bf16[4,5120]{1,0:T(4,128)(2,1)S(1)} %stack.3.refs_1_.refs_0_.refs_2_), channel_id=1, source_target_pairs={{0,6},{2,4},{4,2},{6,0},{8,14},{10,12},{12,10},{14,8},{1,7},{3,5},... | collective-permute-start | bytes 122888 | tf_op jit(solution)/shard_map/ppermute | solution.py:52
  11.3 1.7 %load.3.refs_4_.refs_0_ = bf16[256,5120]{1,0:T(8,128)(2,1)S(1)} custom-call(bf16[256,5120]{1,0:T(8,128)(2,1)} %refs_0_.3, bf16[4,5120]{1,0:T(4,128)(2,1)S(1)} %stack.3.refs_1_.refs_0_.refs_2_), custom_call_target="tpu_custom_call" | custom-call | bytes 5242880 | tf_op jit(solution)/shard_map/load/pallas_call | solution.py:77
  13.1 1.0 %collective-permute-done.2.refs_2_ = bf16[4,5120]{1,0:T(4,128)(2,1)S(1)} collective-permute-done((bf16[4,5120]{1,0:T(4,128)(2,1)S(1)}, bf16[4,5120]{1,0:T(4,128)(2,1)S(1)}, u32[]{:S(2)}, u32[]{:S(2)}) %collective-permute-start.2) | collective-permute-done | bytes 40992 | tf_op jit(solution)/shard_map/ppermute | solution.py:52
  14.8 1.6 %encode_decode.1 = (bf16[16,5120]{1,0:T(8,128)(2,1)S(1)}, f32[16,256]{1,0:T(8,128)S(1)}, f32[16,256]{1,0:T(8,128)S(1)}, f32[4,5120]{1,0:T(4,128)S(1)}, f32[4,512...) custom-call(bf16[16,5120]{1,0:T(8,128)(2,1)S(1)} %stack.4.refs_0_, ...), custom_call_target="tpu_custom_call" | custom-call | flops 167772160 | tf_op jit(solution)/shard_map/encode_decode/pallas_call | solution.py:38
  16.3 1.5 %collective-permute-start.8 = (f32[4,5120]{1,0:T(4,128)S(1)}, f32[4,5120]{1,0:T(4,128)S(1)}, u32[]{:S(2)}, u32[]{:S(2)}) collective-permute-start(f32[4,5120]{1,0:T(4,128)S(1)} %get-tuple-element.37), channel_id=1, source_target_pairs={{0,2},{2,0},{4,6},{6,4},{8,10},{10,8},{12,14},{14,12},{1,3},{3,1},... | collective-permute-start | bytes 245768 | tf_op jit(solution)/shard_map/ppermute | solution.py:52
  17.9 0.9 %collective-permute-start.9 = (f32[4,5120]{1,0:T(4,128)S(1)}, f32[4,5120]{1,0:T(4,128)S(1)}, u32[]{:S(2)}, u32[]{:S(2)}) collective-permute-start(f32[4,5120]{1,0:T(4,128)S(1)} %get-tuple-element.38), channel_id=1, source_target_pairs={{0,6},{2,4},{4,2},{6,0},{8,14},{10,12},{12,10},{14,8},{1,7},{3,5},... | collective-permute-start | bytes 245768 | tf_op jit(solution)/shard_map/ppermute | solution.py:52
  18.8 1.1 %collective-permute-start.10 = (f32[4,5120]{1,0:T(4,128)S(1)}, f32[4,5120]{1,0:T(4,128)S(1)}, u32[]{:S(2)}, u32[]{:S(2)}) collective-permute-start(f32[4,5120]{1,0:T(4,128)S(1)} %get-tuple-element.39), channel_id=1, source_target_pairs={{0,4},{2,6},{4,0},{6,2},{8,12},{10,14},{12,8},{14,10},{1,5},{3,7},... | collective-permute-start | bytes 245768 | tf_op jit(solution)/shard_map/ppermute | solution.py:52
  19.9 0.7 %turn.2.refs_4_.refs_2_ = bf16[5120,256]{1,0:T(8,128)(2,1)S(1)} custom-call(bf16[256,5120]{1,0:T(8,128)(2,1)S(1)} %load.3.refs_4_.refs_0_, f32[4,5120]{1,0:T(4,128)S(1)} %get-tuple-element.36.refs_1_.refs_0_), custom_call_target="tpu_custom_call" | custom-call | bytes 5242880 | tf_op jit(solution)/shard_map/turn/pallas_call | solution.py:38
  20.6 1.1 %collective-permute-done.8.refs_1_ = f32[4,5120]{1,0:T(4,128)S(1)} collective-permute-done((f32[4,5120]{1,0:T(4,128)S(1)}, f32[4,5120]{1,0:T(4,128)S(1)}, u32[]{:S(2)}, u32[]{:S(2)}) %collective-permute-start.8) | collective-permute-done | bytes 81952 | tf_op jit(solution)/shard_map/ppermute | solution.py:52
  21.7 1.7 %collective-permute-done.9.refs_2_ = f32[4,5120]{1,0:T(4,128)S(1)} collective-permute-done((f32[4,5120]{1,0:T(4,128)S(1)}, f32[4,5120]{1,0:T(4,128)S(1)}, u32[]{:S(2)}, u32[]{:S(2)}) %collective-permute-start.9) | collective-permute-done | bytes 81952 | tf_op jit(solution)/shard_map/ppermute | solution.py:52
  23.4 3.1 %collective-permute-start.11 = (f32[4,5120]{1,0:T(4,128)S(1)}, f32[4,5120]{1,0:T(4,128)S(1)}, u32[]{:S(2)}, u32[]{:S(2)}) collective-permute-start(f32[4,5120]{1,0:T(4,128)S(1)} %add_parts.1.refs_1_.refs_0_), channel_id=1, source_target_pairs={{0,8},{2,10},{4,12},{6,14},{8,0},{10,2},{12,4},{14,6},{1,9},{3,11}... | collective-permute-start | bytes 245768 | tf_op jit(solution)/shard_map/ppermute | solution.py:52
  26.6 0.8 %turn.3.refs_4_.refs_1_ = bf16[256,5120]{1,0:T(8,128)(2,1)S(1)} custom-call(bf16[5120,256]{1,0:T(8,128)(2,1)S(1)} %get-tuple-element.31.refs_2_.refs_0_, f32[4,5120]{1,0:T(4,128)S(1)} %add_parts.1.refs_1_.refs_0_), custom_call_target="tpu_custom_call" | custom-call | bytes 5242880 | tf_op jit(solution)/shard_map/turn/pallas_call | solution.py:38
  27.7 2.2 %collective-permute-done.11.refs_1_ = f32[4,5120]{1,0:T(4,128)S(1)} collective-permute-done((f32[4,5120]{1,0:T(4,128)S(1)}, f32[4,5120]{1,0:T(4,128)S(1)}, u32[]{:S(2)}, u32[]{:S(2)}) %collective-permute-start.11) | collective-permute-done | bytes 81952 | tf_op jit(solution)/shard_map/ppermute | solution.py:52
  30.0 1.2 %collective-permute-start.15 = (bf16[4,5120]{1,0:T(4,128)(2,1)S(1)}, bf16[4,5120]{1,0:T(4,128)(2,1)S(1)}, u32[]{:S(2)}, u32[]{:S(2)}) collective-permute-start(bf16[4,5120]{1,0:T(4,128)(2,1)S(1)} %residual_gradient.1.refs_0_.refs_4_), channel_id=1, source_target_pairs={{0,6},{2,4},{4,2},{6,0},{8,14},{10,12},{12,10},{14,8},{1,7},{3,5},... | collective-permute-start | bytes 122888 | tf_op jit(solution)/shard_map/ppermute | solution.py:52
  31.2 1.0 %collective-permute-start.14 = (bf16[4,5120]{1,0:T(4,128)(2,1)S(1)}, bf16[4,5120]{1,0:T(4,128)(2,1)S(1)}, u32[]{:S(2)}, u32[]{:S(2)}) collective-permute-start(bf16[4,5120]{1,0:T(4,128)(2,1)S(1)} %residual_gradient.1.refs_0_.refs_4_), channel_id=1, source_target_pairs={{0,2},{2,0},{4,6},{6,4},{8,10},{10,8},{12,14},{14,12},{1,3},{3,1},... | collective-permute-start | bytes 122888 | tf_op jit(solution)/shard_map/ppermute | solution.py:52
  32.2 1.3 %collective-permute-start.13 = (bf16[4,5120]{1,0:T(4,128)(2,1)S(1)}, bf16[4,5120]{1,0:T(4,128)(2,1)S(1)}, u32[]{:S(2)}, u32[]{:S(2)}) collective-permute-start(bf16[4,5120]{1,0:T(4,128)(2,1)S(1)} %residual_gradient.1.refs_0_.refs_4_), channel_id=1, source_target_pairs={{0,4},{2,6},{4,0},{6,2},{8,12},{10,14},{12,8},{14,10},{1,5},{3,7},... | collective-permute-start | bytes 122888 | tf_op jit(solution)/shard_map/ppermute | solution.py:52
  33.5 1.4 %collective-permute-done.15.refs_3_ = bf16[4,5120]{1,0:T(4,128)(2,1)S(1)} collective-permute-done((bf16[4,5120]{1,0:T(4,128)(2,1)S(1)}, bf16[4,5120]{1,0:T(4,128)(2,1)S(1)}, u32[]{:S(2)}, u32[]{:S(2)}) %collective-permute-start.15) | collective-permute-done | bytes 40992 | tf_op jit(solution)/shard_map/ppermute | solution.py:52
  35.4 0.8 %collective-permute-done.13.refs_1_ = bf16[4,5120]{1,0:T(4,128)(2,1)S(1)} collective-permute-done((bf16[4,5120]{1,0:T(4,128)(2,1)S(1)}, bf16[4,5120]{1,0:T(4,128)(2,1)S(1)}, u32[]{:S(2)}, u32[]{:S(2)}) %collective-permute-start.13) | collective-permute-done | bytes 40992 | tf_op jit(solution)/shard_map/ppermute | solution.py:52
  36.7 1.0 %collective-permute-done.16.refs_1_.refs_3_ = bf16[16,5120]{1,0:T(8,128)(2,1)S(1)} collective-permute-done((bf16[16,5120]{1,0:T(8,128)(2,1)S(1)}, bf16[16,5120]{1,0:T(8,128)(2,1)S(1)}, u32[]{:S(2)}, u32[]{:S(2)}) %collective-permute-start.16) | collective-permute-done | bytes 163872 | tf_op jit(solution)/shard_map/ppermute | solution.py:51
  38.9 0.9 %enc_gradient.1.refs_2_.refs_4_ = bf16[5120,256]{1,0:T(8,128)(2,1)S(1)} custom-call(bf16[16,5120]{1,0:T(8,128)(2,1)S(1)} %get-tuple-element.40.refs_0_, bf16[16,5120]{1,0:T(8,128)(2,1)S(1)} %collective-permute-done.12.refs_6_.refs_1_, bf16[32,256]{1,0:T(8,128)(2,1)S(1)} %get-tuple-element.41.refs_2_, f32[1,5248]{1,0:T(1,128)S(1)} %bias_product.1.refs_3_.refs_0_), custom_call_target="tpu_custom_call" | custom-call | flops 83886080 | tf_op jit(solution)/shard_map/enc_gradient/pallas_call | solution.py:38
  40.0 1.0 %collective-permute-start.20 = (f32[1,5248]{1,0:T(1,128)S(1)}, f32[1,5248]{1,0:T(1,128)S(1)}, u32[]{:S(2)}, u32[]{:S(2)}) collective-permute-start(f32[1,5248]{1,0:T(1,128)S(1)} %add.2.refs_6_.refs_0_), channel_id=1, source_target_pairs={{0,2},{2,0},{4,6},{6,4},{8,10},{10,8},{12,14},{14,12},{1,3},{3,1},... | collective-permute-start | bytes 62984 | tf_op jit(solution)/shard_map/ppermute | solution.py:52
  41.0 1.7 %collective-permute-start.19 = (f32[1,5248]{1,0:T(1,128)S(1)}, f32[1,5248]{1,0:T(1,128)S(1)}, u32[]{:S(2)}, u32[]{:S(2)}) collective-permute-start(f32[1,5248]{1,0:T(1,128)S(1)} %add.2.refs_6_.refs_0_), channel_id=1, source_target_pairs={{0,6},{2,4},{4,2},{6,0},{8,14},{10,12},{12,10},{14,8},{1,7},{3,5},... | collective-permute-start | bytes 62984 | tf_op jit(solution)/shard_map/ppermute | solution.py:52
  42.8 0.7 %collective-permute-start.18 = (f32[1,5248]{1,0:T(1,128)S(1)}, f32[1,5248]{1,0:T(1,128)S(1)}, u32[]{:S(2)}, u32[]{:S(2)}) collective-permute-start(f32[1,5248]{1,0:T(1,128)S(1)} %add.2.refs_6_.refs_0_), channel_id=1, source_target_pairs={{0,4},{2,6},{4,0},{6,2},{8,12},{10,14},{12,8},{14,10},{1,5},{3,7},... | collective-permute-start | bytes 62984 | tf_op jit(solution)/shard_map/ppermute | solution.py:52
  43.5 1.5 %dec_gradient.1 = (bf16[5120,256]{1,0:T(8,128)(2,1)}, f32[1,256]{1,0:T(1,128)}, bf16[256,5120]{1,0:T(8,128)(2,1)S(1)}) custom-call(f32[16,256]{1,0:T(8,128)S(1)} %get-tuple-element.34.refs_3_.refs_0_, f32[16,256]{1,0:T(8,128)S(1)} %collective-permute-done.7.refs_5_.refs_4_.refs_1_, bf16[16,5120]{1,0:T(8,128)(2,1)S(1)} %stack.5.refs_0_.refs_2_, ...), custom_call_target="tpu_custom_call" | custom-call | flops 83886080 | bytes 5242880 | tf_op jit(solution)/shard_map/dec_gradient/pallas_call | solution.py:304
  45.0 0.7 %collective-permute-done.19.refs_2_ = f32[1,5248]{1,0:T(1,128)S(1)} collective-permute-done((f32[1,5248]{1,0:T(1,128)S(1)}, f32[1,5248]{1,0:T(1,128)S(1)}, u32[]{:S(2)}, u32[]{:S(2)}) %collective-permute-start.19) | collective-permute-done | bytes 21024 | tf_op jit(solution)/shard_map/ppermute | solution.py:52
  45.7 0.8 %collective-permute-done.18.refs_1_ = f32[1,5248]{1,0:T(1,128)S(1)} collective-permute-done((f32[1,5248]{1,0:T(1,128)S(1)}, f32[1,5248]{1,0:T(1,128)S(1)}, u32[]{:S(2)}, u32[]{:S(2)}) %collective-permute-start.18) | collective-permute-done | bytes 21024 | tf_op jit(solution)/shard_map/ppermute | solution.py:52
  46.6 2.6 %collective-permute-start.21 = (f32[1,5248]{1,0:T(1,128)S(1)}, f32[1,5248]{1,0:T(1,128)S(1)}, u32[]{:S(2)}, u32[]{:S(2)}) collective-permute-start(f32[1,5248]{1,0:T(1,128)S(1)} %add.3.refs_2_.terms_ref), channel_id=1, source_target_pairs={{0,8},{2,10},{4,12},{6,14},{8,0},{10,2},{12,4},{14,6},{1,9},{3,11}... | collective-permute-start | bytes 62984 | tf_op jit(solution)/shard_map/ppermute | solution.py:52
  49.2 1.5 %store.1 = (bf16[256,5120]{1,0:T(8,128)(2,1)}, bf16[2,5120]{1,0:T(2,128)(2,1)}, f32[8,128]{1,0:T(8,128)S(1)}) custom-call(bf16[256,5120]{1,0:T(8,128)(2,1)S(1)} %get-tuple-element.45.refs_4_.refs_0_, bf16[2,5120]{1,0:T(2,128)(2,1)S(1)} %get-tuple-element.46.refs_1_, f32[1,5248]{1,0:T(1,128)S(1)} %add.3.refs_2_.terms_ref), custom_call_target="tpu_custom_call" | custom-call | bytes 5283840 | tf_op jit(solution)/shard_map/store/pallas_call | solution.py:329
  50.7 0.7 %collective-permute-done.21.other_ref = f32[1,5248]{1,0:T(1,128)S(1)} collective-permute-done((f32[1,5248]{1,0:T(1,128)S(1)}, f32[1,5248]{1,0:T(1,128)S(1)}, u32[]{:S(2)}, u32[]{:S(2)}) %collective-permute-start.21) | collective-permute-done | bytes 21024 | tf_op jit(solution)/shard_map/ppermute | solution.py:52
  (34 shorter events, 5.6 us)
Async XLA Ops:
  0.6 14.1 %collective-permute-start.4 = (bf16[5120,256]{1,0:T(8,128)(2,1)}, bf16[5120,256]{1,0:T(8,128)(2,1)S(1)}, u32[]{:S(2)}, u32[]{:S(2)}) collective-permute-start(bf16[5120,256]{1,0:T(8,128)(2,1)} %refs_0_.2), channel_id=1, source_target_pairs={{0,1},{1,0},{2,3},{3,2},{4,5},{5,4},{6,7},{7,6},{8,9},{9,8},{10,11... | collective-permute-start | bytes 7864328 | tf_op jit(solution)/shard_map/ppermute | solution.py:51
  1.2 13.6 %collective-permute-start.6 = (bf16[256,5120]{1,0:T(8,128)(2,1)}, bf16[256,5120]{1,0:T(8,128)(2,1)S(1)}, u32[]{:S(2)}, u32[]{:S(2)}) collective-permute-start(bf16[256,5120]{1,0:T(8,128)(2,1)} %refs_0_.3), channel_id=1, source_target_pairs={{0,1},{1,0},{2,3},{3,2},{4,5},{5,4},{6,7},{7,6},{8,9},{9,8},{10,11... | collective-permute-start | bytes 7864328 | tf_op jit(solution)/shard_map/ppermute | solution.py:51
  1.2 6.0 %collective-permute-start = (bf16[2,5120]{1,0:T(2,128)(2,1)}, bf16[2,5120]{1,0:T(2,128)(2,1)S(1)}, u32[]{:S(2)}, u32[]{:S(2)}) collective-permute-start(bf16[2,5120]{1,0:T(2,128)(2,1)} %refs_1_.1), channel_id=1, source_target_pairs={{0,8},{2,10},{4,12},{6,14},{8,0},{10,2},{12,4},{14,6},{1,9},{3,11}... | collective-permute-start | bytes 61448 | tf_op jit(solution)/shard_map/ppermute | solution.py:52
  5.2 6.1 %copy-start = (f32[256]{0:T(256)S(1)}, f32[256]{0:T(256)}, u32[]{:S(2)}) copy-start(f32[256]{0:T(256)} %param.7) | copy-start | bytes 3076
  7.3 4.1 %collective-permute-start.3 = (bf16[4,5120]{1,0:T(4,128)(2,1)S(1)}, bf16[4,5120]{1,0:T(4,128)(2,1)S(1)}, u32[]{:S(2)}, u32[]{:S(2)}) collective-permute-start(bf16[4,5120]{1,0:T(4,128)(2,1)S(1)} %stack.3.refs_1_.refs_0_.refs_2_), channel_id=1, source_target_pairs={{0,2},{2,0},{4,6},{6,4},{8,10},{10,8},{12,14},{14,12},{1,3},{3,1},... | collective-permute-start | bytes 122888 | tf_op jit(solution)/shard_map/ppermute | solution.py:52
  9.2 4.9 %collective-permute-start.2 = (bf16[4,5120]{1,0:T(4,128)(2,1)S(1)}, bf16[4,5120]{1,0:T(4,128)(2,1)S(1)}, u32[]{:S(2)}, u32[]{:S(2)}) collective-permute-start(bf16[4,5120]{1,0:T(4,128)(2,1)S(1)} %stack.3.refs_1_.refs_0_.refs_2_), channel_id=1, source_target_pairs={{0,6},{2,4},{4,2},{6,0},{8,14},{10,12},{12,10},{14,8},{1,7},{3,5},... | collective-permute-start | bytes 122888 | tf_op jit(solution)/shard_map/ppermute | solution.py:52
  10.7 4.0 %collective-permute-start.1 = (bf16[4,5120]{1,0:T(4,128)(2,1)S(1)}, bf16[4,5120]{1,0:T(4,128)(2,1)S(1)}, u32[]{:S(2)}, u32[]{:S(2)}) collective-permute-start(bf16[4,5120]{1,0:T(4,128)(2,1)S(1)} %stack.3.refs_1_.refs_0_.refs_2_), channel_id=1, source_target_pairs={{0,4},{2,6},{4,0},{6,2},{8,12},{10,14},{12,8},{14,10},{1,5},{3,7},... | collective-permute-start | bytes 122888 | tf_op jit(solution)/shard_map/ppermute | solution.py:52
  11.3 3.4 %collective-permute-start.5 = (f32[1,256]{1,0:T(1,128)S(1)}, f32[1,256]{1,0:T(1,128)S(1)}, u32[]{:S(2)}, u32[]{:S(2)}) collective-permute-start(f32[1,256]{1,0:T(1,128)S(1)} %bitcast.7), channel_id=1, source_target_pairs={{0,1},{1,0},{2,3},{3,2},{4,5},{5,4},{6,7},{7,6},{8,9},{9,8},{10,11... | collective-permute-start | bytes 3080 | tf_op jit(solution)/shard_map/ppermute | solution.py:51
  16.3 5.3 %collective-permute-start.8 = (f32[4,5120]{1,0:T(4,128)S(1)}, f32[4,5120]{1,0:T(4,128)S(1)}, u32[]{:S(2)}, u32[]{:S(2)}) collective-permute-start(f32[4,5120]{1,0:T(4,128)S(1)} %get-tuple-element.37), channel_id=1, source_target_pairs={{0,2},{2,0},{4,6},{6,4},{8,10},{10,8},{12,14},{14,12},{1,3},{3,1},... | collective-permute-start | bytes 245768 | tf_op jit(solution)/shard_map/ppermute | solution.py:52
  17.9 5.5 %collective-permute-start.9 = (f32[4,5120]{1,0:T(4,128)S(1)}, f32[4,5120]{1,0:T(4,128)S(1)}, u32[]{:S(2)}, u32[]{:S(2)}) collective-permute-start(f32[4,5120]{1,0:T(4,128)S(1)} %get-tuple-element.38), channel_id=1, source_target_pairs={{0,6},{2,4},{4,2},{6,0},{8,14},{10,12},{12,10},{14,8},{1,7},{3,5},... | collective-permute-start | bytes 245768 | tf_op jit(solution)/shard_map/ppermute | solution.py:52
  18.8 4.6 %collective-permute-start.10 = (f32[4,5120]{1,0:T(4,128)S(1)}, f32[4,5120]{1,0:T(4,128)S(1)}, u32[]{:S(2)}, u32[]{:S(2)}) collective-permute-start(f32[4,5120]{1,0:T(4,128)S(1)} %get-tuple-element.39), channel_id=1, source_target_pairs={{0,4},{2,6},{4,0},{6,2},{8,12},{10,14},{12,8},{14,10},{1,5},{3,7},... | collective-permute-start | bytes 245768 | tf_op jit(solution)/shard_map/ppermute | solution.py:52
  19.9 10.0 %collective-permute-start.12 = (bf16[16,5120]{1,0:T(8,128)(2,1)S(1)}, bf16[16,5120]{1,0:T(8,128)(2,1)S(1)}, u32[]{:S(2)}, u32[]{:S(2)}) collective-permute-start(bf16[16,5120]{1,0:T(8,128)(2,1)S(1)} %get-tuple-element.40.refs_0_), channel_id=1, source_target_pairs={{0,1},{1,0},{2,3},{3,2},{4,5},{5,4},{6,7},{7,6},{8,9},{9,8},{10,11... | collective-permute-start | bytes 491528 | tf_op jit(solution)/shard_map/ppermute | solution.py:51
  23.4 6.5 %collective-permute-start.11 = (f32[4,5120]{1,0:T(4,128)S(1)}, f32[4,5120]{1,0:T(4,128)S(1)}, u32[]{:S(2)}, u32[]{:S(2)}) collective-permute-start(f32[4,5120]{1,0:T(4,128)S(1)} %add_parts.1.refs_1_.refs_0_), channel_id=1, source_target_pairs={{0,8},{2,10},{4,12},{6,14},{8,0},{10,2},{12,4},{14,6},{1,9},{3,11}... | collective-permute-start | bytes 245768 | tf_op jit(solution)/shard_map/ppermute | solution.py:52
  26.6 1.2 %collective-permute-start.7 = (f32[16,256]{1,0:T(8,128)S(1)}, f32[16,256]{1,0:T(8,128)S(1)}, u32[]{:S(2)}, u32[]{:S(2)}) collective-permute-start(f32[16,256]{1,0:T(8,128)S(1)} %get-tuple-element.35), channel_id=1, source_target_pairs={{0,1},{1,0},{2,3},{3,2},{4,5},{5,4},{6,7},{7,6},{8,9},{9,8},{10,11... | collective-permute-start | bytes 49160 | tf_op jit(solution)/shard_map/ppermute | solution.py:51
  30.0 5.0 %collective-permute-start.15 = (bf16[4,5120]{1,0:T(4,128)(2,1)S(1)}, bf16[4,5120]{1,0:T(4,128)(2,1)S(1)}, u32[]{:S(2)}, u32[]{:S(2)}) collective-permute-start(bf16[4,5120]{1,0:T(4,128)(2,1)S(1)} %residual_gradient.1.refs_0_.refs_4_), channel_id=1, source_target_pairs={{0,6},{2,4},{4,2},{6,0},{8,14},{10,12},{12,10},{14,8},{1,7},{3,5},... | collective-permute-start | bytes 122888 | tf_op jit(solution)/shard_map/ppermute | solution.py:52
  31.2 4.2 %collective-permute-start.14 = (bf16[4,5120]{1,0:T(4,128)(2,1)S(1)}, bf16[4,5120]{1,0:T(4,128)(2,1)S(1)}, u32[]{:S(2)}, u32[]{:S(2)}) collective-permute-start(bf16[4,5120]{1,0:T(4,128)(2,1)S(1)} %residual_gradient.1.refs_0_.refs_4_), channel_id=1, source_target_pairs={{0,2},{2,0},{4,6},{6,4},{8,10},{10,8},{12,14},{14,12},{1,3},{3,1},... | collective-permute-start | bytes 122888 | tf_op jit(solution)/shard_map/ppermute | solution.py:52
  32.2 4.0 %collective-permute-start.13 = (bf16[4,5120]{1,0:T(4,128)(2,1)S(1)}, bf16[4,5120]{1,0:T(4,128)(2,1)S(1)}, u32[]{:S(2)}, u32[]{:S(2)}) collective-permute-start(bf16[4,5120]{1,0:T(4,128)(2,1)S(1)} %residual_gradient.1.refs_0_.refs_4_), channel_id=1, source_target_pairs={{0,4},{2,6},{4,0},{6,2},{8,12},{10,14},{12,8},{14,10},{1,5},{3,7},... | collective-permute-start | bytes 122888 | tf_op jit(solution)/shard_map/ppermute | solution.py:52
  36.2 1.5 %collective-permute-start.16 = (bf16[16,5120]{1,0:T(8,128)(2,1)S(1)}, bf16[16,5120]{1,0:T(8,128)(2,1)S(1)}, u32[]{:S(2)}, u32[]{:S(2)}) collective-permute-start(bf16[16,5120]{1,0:T(8,128)(2,1)S(1)} %stack.5.refs_0_.refs_2_), channel_id=1, source_target_pairs={{0,1},{1,0},{2,3},{3,2},{4,5},{5,4},{6,7},{7,6},{8,9},{9,8},{10,11... | collective-permute-start | bytes 491528 | tf_op jit(solution)/shard_map/ppermute | solution.py:51
  38.7 1.3 %collective-permute-start.17 = (f32[1,5248]{1,0:T(1,128)S(1)}, f32[1,5248]{1,0:T(1,128)S(1)}, u32[]{:S(2)}, u32[]{:S(2)}) collective-permute-start(f32[1,5248]{1,0:T(1,128)S(1)} %bias_product.1.refs_3_.refs_0_), channel_id=1, source_target_pairs={{0,1},{1,0},{2,3},{3,2},{4,5},{5,4},{6,7},{7,6},{8,9},{9,8},{10,11... | collective-permute-start | bytes 62984 | tf_op jit(solution)/shard_map/ppermute | solution.py:51
  40.0 5.0 %collective-permute-start.20 = (f32[1,5248]{1,0:T(1,128)S(1)}, f32[1,5248]{1,0:T(1,128)S(1)}, u32[]{:S(2)}, u32[]{:S(2)}) collective-permute-start(f32[1,5248]{1,0:T(1,128)S(1)} %add.2.refs_6_.refs_0_), channel_id=1, source_target_pairs={{0,2},{2,0},{4,6},{6,4},{8,10},{10,8},{12,14},{14,12},{1,3},{3,1},... | collective-permute-start | bytes 62984 | tf_op jit(solution)/shard_map/ppermute | solution.py:52
  41.0 4.7 %collective-permute-start.19 = (f32[1,5248]{1,0:T(1,128)S(1)}, f32[1,5248]{1,0:T(1,128)S(1)}, u32[]{:S(2)}, u32[]{:S(2)}) collective-permute-start(f32[1,5248]{1,0:T(1,128)S(1)} %add.2.refs_6_.refs_0_), channel_id=1, source_target_pairs={{0,6},{2,4},{4,2},{6,0},{8,14},{10,12},{12,10},{14,8},{1,7},{3,5},... | collective-permute-start | bytes 62984 | tf_op jit(solution)/shard_map/ppermute | solution.py:52
  42.8 3.8 %collective-permute-start.18 = (f32[1,5248]{1,0:T(1,128)S(1)}, f32[1,5248]{1,0:T(1,128)S(1)}, u32[]{:S(2)}, u32[]{:S(2)}) collective-permute-start(f32[1,5248]{1,0:T(1,128)S(1)} %add.2.refs_6_.refs_0_), channel_id=1, source_target_pairs={{0,4},{2,6},{4,0},{6,2},{8,12},{10,14},{12,8},{14,10},{1,5},{3,7},... | collective-permute-start | bytes 62984 | tf_op jit(solution)/shard_map/ppermute | solution.py:52
  46.6 4.8 %collective-permute-start.21 = (f32[1,5248]{1,0:T(1,128)S(1)}, f32[1,5248]{1,0:T(1,128)S(1)}, u32[]{:S(2)}, u32[]{:S(2)}) collective-permute-start(f32[1,5248]{1,0:T(1,128)S(1)} %add.3.refs_2_.terms_ref), channel_id=1, source_target_pairs={{0,8},{2,10},{4,12},{6,14},{8,0},{10,2},{12,4},{14,6},{1,9},{3,11}... | collective-permute-start | bytes 62984 | tf_op jit(solution)/shard_map/ppermute | solution.py:52

commit v7 on v6

--- a/solution.py
+++ b/solution.py
@@ -52,7 +52,7 @@
     return lax.ppermute(values, "lat", [(i, i ^ mask) for i in range(lax.axis_size("lat"))])
 
 
-ROWS_ORDER, SUM_ORDER, RESID_ORDER, TERMS_ORDER = (2, 3, 1), (1, 3, 2), (2, 1, 3), (2, 3, 1)
+ROWS_ORDER, SUM_ORDER, RESID_ORDER, TERMS_ORDER = (2, 3, 1), (2, 1, 3), (2, 3, 1), (2, 3, 1)
 
 
 def plan(lat):
@@ -119,8 +119,8 @@
     return run(kernel, "add_parts", [((size, width), jnp.float32)] * count, [first, *others], after)
 
 
-def halve(parts, steps, dec_weight):
-    dec_turned = turn(dec_weight, [parts[0]])
+def halve(parts, steps, dec_weights):
+    dec_turned = turn(dec_weights, 1, [parts[0]])
     for step, masks in enumerate(steps):
         others = [swap(part, mask) for part, mask in zip(parts[1:], masks)]
         if len(masks) > 1:
@@ -210,32 +210,41 @@
     )
 
 
-def turn(weight, after):
-    rows, columns = weight.shape
-
-    def kernel(weight_ref, turned_ref):
-        turned_ref[...] = weight_ref[...].T
-
-    return run(kernel, "turn", [((columns, rows), weight.dtype)], [weight], after, moved=4 * rows * columns)[0]
-
-
-def backward(half_a, half_b, dec_weight, active_a, active_b, row_count):
-    half, width = half_a.shape
-    latents = dec_weight.shape[1]
-
-    def kernel(a_ref, b_ref, dec_ref, active_a_ref, active_b_ref, code_grad_ref, total_ref):
-        resid = jnp.concatenate([a_ref[...], b_ref[...]], axis=0)
-        back = jnp.dot(resid, dec_ref[...], preferred_element_type=jnp.float32)
-        active = jnp.concatenate([active_a_ref[...], active_b_ref[...]], axis=0)
+def turn(weights, axis, after):
+    rows, columns = weights[0].shape
+    count = len(weights)
+
+    def kernel(*refs):
+        turned_ref = refs[-1]
+        for i in range(count):
+            if axis == 0:
+                turned_ref[i * columns : (i + 1) * columns] = refs[i][...].T
+            else:
+                turned_ref[:, i * rows : (i + 1) * rows] = refs[i][...].T
+
+    shape = (count * columns, rows) if axis == 0 else (columns, count * rows)
+    return run(
+        kernel, "turn", [(shape, weights[0].dtype)], weights, after, moved=4 * count * rows * columns
+    )[0]
+
+
+def backward(resid, dec_turned, active_own, active_sibling, row_count):
+    height = resid.shape[0]
+    latents = active_own.shape[1]
+
+    def kernel(resid_ref, dec_ref, own_ref, sibling_ref, own_grad_ref, sibling_grad_ref, total_ref):
+        back = jnp.dot(resid_ref[...], dec_ref[...], preferred_element_type=jnp.float32)
+        active = jnp.concatenate([own_ref[...], sibling_ref[...]], axis=1)
         code_grad = 2.0 * active * (back + PENALTY / row_count)
-        code_grad_ref[...] = code_grad.astype(jnp.bfloat16)
+        own_grad_ref[...] = code_grad[:, :latents].astype(jnp.bfloat16)
+        sibling_grad_ref[...] = code_grad[:, latents:]
         total_ref[...] = jnp.sum(code_grad, axis=0, keepdims=True)
 
     return run(
         kernel,
         "backward",
-        [((2 * half, latents), jnp.bfloat16), ((1, latents), jnp.float32)],
-        [half_a, half_b, dec_weight, active_a, active_b],
+        [((height, latents), jnp.bfloat16), ((height, latents), jnp.float32), ((1, 2 * latents), jnp.float32)],
+        [resid, dec_turned, active_own, active_sibling],
     )
 
 
@@ -261,57 +270,61 @@
     )[0]
 
 
-def enc_gradient(centered_a, centered_b, code_grad, after):
-    half, width = centered_a.shape
-    latents = code_grad.shape[1]
-
-    def kernel(a_ref, b_ref, code_grad_ref, grad_ref):
-        centered = jnp.concatenate([a_ref[...], b_ref[...]], axis=0)
-        grad_ref[...] = lax.dot_general(
-            centered, code_grad_ref[...], CONTRACT_FIRST, preferred_element_type=jnp.float32
-        ).astype(jnp.bfloat16)
-
-    return run(
-        kernel,
-        "enc_gradient",
-        [((width, latents), jnp.bfloat16)],
-        [centered_a, centered_b, code_grad],
-        after,
-        flops=4 * half * width * latents,
-    )[0]
-
-
-def dec_gradient(active_a, active_b, resid_a, resid_b, stored, after):
+def dec_gradient(active_a, active_b, resid_a, resid_b, after):
     half, latents = active_a.shape
     width = resid_a.shape[1]
-    count = len(stored)
-
-    def kernel(*refs):
-        active_a_ref, active_b_ref, a_ref, b_ref = refs[:4]
-        outs, grad_ref, sems = refs[5 + count : 5 + 2 * count], refs[-2], refs[-1]
-        copies = [pltpu.make_async_copy(refs[4 + i], outs[i], sems.at[i]) for i in range(count)]
-        for copy in copies:
-            copy.start()
+
+    def kernel(active_a_ref, active_b_ref, a_ref, b_ref, grad_ref):
         active = jnp.concatenate([active_a_ref[...], active_b_ref[...]], axis=0)
         codes = (active * active).astype(jnp.bfloat16)
         resid = jnp.concatenate([a_ref[...], b_ref[...]], axis=0)
         grad_ref[...] = lax.dot_general(
             codes, resid, CONTRACT_FIRST, preferred_element_type=jnp.float32
         ).astype(jnp.bfloat16)
+
+    return run(
+        kernel,
+        "dec_gradient",
+        [((latents, width), jnp.bfloat16)],
+        [active_a, active_b, resid_a, resid_b],
+        after,
+        flops=4 * half * width * latents,
+    )[0]
+
+
+def enc_gradient(centered_a, centered_b, code_grad_a, code_grad_b, total, stored, after):
+    half, width = centered_a.shape
+    latents = code_grad_a.shape[1]
+    count = len(stored)
+
+    def kernel(*refs):
+        a_ref, b_ref, code_grad_a_ref, code_grad_b_ref, total_ref = refs[:5]
+        outs, (grad_ref, bias_ref, sems) = refs[6 + count : 6 + 2 * count], refs[-3:]
+        copies = [pltpu.make_async_copy(refs[5 + i], outs[i], sems.at[i]) for i in range(count)]
+        for copy in copies:
+            copy.start()
+        grad_b = code_grad_b_ref[...]
+        bias_ref[...] = total_ref[:, :latents] + jnp.sum(grad_b, axis=0, keepdims=True)
+        centered = jnp.concatenate([a_ref[...], b_ref[...]], axis=0)
+        code_grad = jnp.concatenate([code_grad_a_ref[...], grad_b.astype(jnp.bfloat16)], axis=0)
+        grad_ref[...] = lax.dot_general(
+            centered, code_grad, CONTRACT_FIRST, preferred_element_type=jnp.float32
+        ).astype(jnp.bfloat16)
         for copy in copies:
             copy.wait()
 
-    *outs, grad = pl.pallas_call(
-        kernel,
-        out_shape=[jax.ShapeDtypeStruct(a.shape, a.dtype) for a in stored] + [vmem((latents, width), jnp.bfloat16)],
-        in_specs=[VMEM] * (5 + count),
-        out_specs=[HBM] * count + [VMEM],
+    *outs, grad, bias = pl.pallas_call(
+        kernel,
+        out_shape=[jax.ShapeDtypeStruct(a.shape, a.dtype) for a in stored]
+        + [vmem((width, latents), jnp.bfloat16), vmem((1, latents), jnp.float32)],
+        in_specs=[VMEM] * (6 + count),
+        out_specs=[HBM] * count + [VMEM] * 2,
         scratch_shapes=[pltpu.SemaphoreType.DMA((count,))],
         compiler_params=pltpu.CompilerParams(vmem_limit_bytes=LIMIT),
         cost_estimate=pl.CostEstimate(flops=4 * half * latents * width, bytes_accessed=4 * latents * width, transcendentals=0),
-        name="dec_gradient",
-    )(*[in_vmem(a) for a in (active_a, active_b, resid_a, resid_b, *stored, after)])
-    return outs, grad
+        name="enc_gradient",
+    )(*[in_vmem(a) for a in (centered_a, centered_b, code_grad_a, code_grad_b, total, *stored, after)])
+    return outs, grad, bias
 
 
 def store(arrays, after):
@@ -385,32 +398,36 @@
         rows, [(enc_vmem, enc_bias_row, dec_vmem), siblings], dec_bias_row, len(steps[-1]) + 1
     )
 
-    summed, dec_turned = halve(parts, steps[::-1], dec_vmem)
+    summed, dec_turned = halve(parts, steps[::-1], [dec_vmem, siblings[2]])
     active_b = swap(active_sibling, CORES)
     centered_b = swap(centered_a, CORES)
-    enc_turned = turn(enc_vmem, [summed])
+    enc_turned = turn([enc_vmem, siblings[0]], 0, [summed])
     error_args = summed, swap(summed, far), paired, dec_bias_row, row_count
     resid_bf = residual_gradient(*error_args, [enc_turned, active_b, centered_b])
 
-    resid_a = gather(resid_bf, steps, RESID_ORDER)
+    recon, own_bias, square = own_terms(*error_args, [resid_bf])
+    code_total = code_sum(active_a, active_b)
+    resid_a = gather(resid_bf, steps, RESID_ORDER, after=[square, code_total])
     resid_b = swap(resid_a, CORES)
-    recon, own_bias, square = own_terms(*error_args, [resid_bf])
-    code_grad_bf, total = backward(resid_a, resid_b, dec_turned, active_a, active_b, row_count)
-    terms = bias_product(total, enc_turned, own_bias, square, code_sum(active_a, active_b), row_count)
-
-    grad_enc = enc_gradient(centered_a, centered_b, code_grad_bf, [terms])
-    terms = add(terms, swap(terms, CORES), after=[grad_enc])
-    (grad_enc, total), grad_dec = dec_gradient(active_a, active_b, resid_a, resid_b, [grad_enc, total], terms)
+    code_grad_a, code_grad_sibling, total = backward(resid_a, dec_turned, active_a, active_sibling, row_count)
+    terms = bias_product(total, enc_turned, own_bias, square, code_total, row_count)
+    code_grad_b = swap(code_grad_sibling, CORES)
+
+    grad_dec = dec_gradient(active_a, active_b, resid_a, resid_b, [terms])
+    terms = add(terms, swap(terms, CORES), after=[grad_dec])
+    (grad_dec, recon), grad_enc, grad_enc_bias = enc_gradient(
+        centered_a, centered_b, code_grad_a, code_grad_b, total, [grad_dec, recon], terms
+    )
     for masks in steps:
         terms = add(
             terms,
             *[swap(terms, mask) for mask in masks],
-            after=[grad_dec],
+            after=[grad_enc],
             order=[0, *TERMS_ORDER] if len(masks) > 1 else None,
         )
-    grad_dec, recon, stored = store([grad_dec, recon], terms)
+    grad_enc, grad_enc_bias, stored = store([grad_enc, grad_enc_bias], terms)
     grad_dec_bias, loss_value = finish(terms, swap(terms, far), width, stored)
-    return recon, loss_value[0], grad_enc, total[0], grad_dec, grad_dec_bias[0]
+    return recon, loss_value[0], grad_enc, grad_enc_bias[0], grad_dec, grad_dec_bias[0]
 
 
 def solution(mesh):

time: 52.1 us -> 51.4 us (0.987)
  waiting for transfers between devices: 13.7 us -> 9.97 us
  Pallas kernels: 12.8 us -> 14.7 us
  starting transfers between devices: 24.7 us -> 25.7 us
    ppermute x15, waiting for transfers between devices: 12.1 us -> 9.95 us  [swap(): lax.ppermute(values, 'lat', [(i, i ^ mask) for i in range(lax.axis_size('...]
    pallas_call x15, Pallas kernels: 5.61 us -> 7.56 us  [run(): pl.pallas_call(body, out_shape=[vmem(*out) for out in outs], in_specs=[VM...]
    ppermute x7 -> x8, waiting for transfers between devices: 1.55 us -> 0.02 us  [swap(): return lax.ppermute(values, 'sub', [(i, i ^ 1) for i in range(2)])]
    ppermute x15, starting transfers between devices: 23.8 us -> 24.4 us  [swap(): lax.ppermute(values, 'lat', [(i, i ^ mask) for i in range(lax.axis_size('...]
    ppermute x7 -> x8, starting transfers between devices: 0.88 us -> 1.29 us  [swap(): return lax.ppermute(values, 'sub', [(i, i ^ 1) for i in range(2)])]
  transfers between devices with their start and end apart: 22 -> 23, of which waited for: 16 -> 13; matrix products, arithmetic and copies ran while one was open for 0% -> 0% of each run, Pallas kernels for 18% -> 24%
where the time goes in v7:
time: 51.4 us; the launch traced here: 51.2 us
  starting transfers between devices  25.7 us (50%)
  Pallas kernels  14.7 us (29%)
  waiting for transfers between devices  9.97 us (19%)
  between operations  0.81 us (2%)
    ppermute x15, starting transfers between devices, swap(): lax.ppermute(values, 'lat', [(i, i ^ mask) for i in range(lax.axis_size('...  24.4 us
    ppermute x15, waiting for transfers between devices, swap(): lax.ppermute(values, 'lat', [(i, i ^ mask) for i in range(lax.axis_size('...  9.95 us
    pallas_call x15, Pallas kernels, run(): pl.pallas_call(body, out_shape=[vmem(*out) for out in outs], in_specs=[VM...  7.56 us
    pallas_call x2, Pallas kernels, load(): pl.pallas_call(kernel, out_shape=[vmem(array.shape, array.dtype) for arra...  3.54 us
    pallas_call x1, Pallas kernels, enc_gradient(): pl.pallas_call(kernel, out_shape=[jax.ShapeDtypeStruct(a.shape, a.dtype)...  1.51 us
    pallas_call x1, Pallas kernels, store(): pl.pallas_call(kernel, out_shape=[jax.ShapeDtypeStruct(a.shape, a.dtype)...  1.51 us
    ppermute x8, starting transfers between devices, swap(): return lax.ppermute(values, 'sub', [(i, i ^ 1) for i in range(2)])  1.29 us
  transfers between devices with their start and end apart: 23, of which 13 were waited for; matrix products, arithmetic and copies ran while one was open for 0% of the time, Pallas kernels for 24%

profile of v7, /device:TPU:0, one launch (start us, length us, event | category | flops | bytes accessed | tf_op | source)
XLA Modules:
  0.0 51.2 jit_solution(6598229564058256198)
XLA Ops:
  1.2 4.0 %collective-permute-start = (bf16[2,5120]{1,0:T(2,128)(2,1)}, bf16[2,5120]{1,0:T(2,128)(2,1)S(1)}, u32[]{:S(2)}, u32[]{:S(2)}) collective-permute-start(bf16[2,5120]{1,0:T(2,128)(2,1)} %refs_1_.1), channel_id=1, source_target_pairs={{0,8},{2,10},{4,12},{6,14},{8,0},{10,2},{12,4},{14,6},{1,9},{3,11}... | collective-permute-start | bytes 61448 | tf_op jit(solution)/shard_map/ppermute | solution.py:52
  5.2 1.8 %load.2 = (bf16[5120,256]{1,0:T(8,128)(2,1)S(1)}, bf16[2,5120]{1,0:T(2,128)(2,1)S(1)}, f32[1,5120]{1,0:T(1,128)S(1)}, f32[1,256]{1,0:T(1,128)S(1)}) custom-call(bf16[5120,256]{1,0:T(8,128)(2,1)} %refs_0_.2, bf16[2,5120]{1,0:T(2,128)(2,1)} %refs_1_.1, f32[1,5120]{1,0:T(1,128)} %bitcast.5, f32[1,256]{1,0:T(1,128)} %bitcast.6), custom_call_target="tpu_custom_call" | custom-call | bytes 5326848 | tf_op jit(solution)/shard_map/load/pallas_call | solution.py:77
  7.3 1.9 %collective-permute-start.3 = (bf16[4,5120]{1,0:T(4,128)(2,1)S(1)}, bf16[4,5120]{1,0:T(4,128)(2,1)S(1)}, u32[]{:S(2)}, u32[]{:S(2)}) collective-permute-start(bf16[4,5120]{1,0:T(4,128)(2,1)S(1)} %stack.3.refs_1_.refs_0_.refs_2_), channel_id=1, source_target_pairs={{0,2},{2,0},{4,6},{6,4},{8,10},{10,8},{12,14},{14,12},{1,3},{3,1},... | collective-permute-start | bytes 122888 | tf_op jit(solution)/shard_map/ppermute | solution.py:52
  9.2 1.5 %collective-permute-start.2 = (bf16[4,5120]{1,0:T(4,128)(2,1)S(1)}, bf16[4,5120]{1,0:T(4,128)(2,1)S(1)}, u32[]{:S(2)}, u32[]{:S(2)}) collective-permute-start(bf16[4,5120]{1,0:T(4,128)(2,1)S(1)} %stack.3.refs_1_.refs_0_.refs_2_), channel_id=1, source_target_pairs={{0,6},{2,4},{4,2},{6,0},{8,14},{10,12},{12,10},{14,8},{1,7},{3,5},... | collective-permute-start | bytes 122888 | tf_op jit(solution)/shard_map/ppermute | solution.py:52
  11.3 1.7 %load.3.refs_4_.refs_0_ = bf16[256,5120]{1,0:T(8,128)(2,1)S(1)} custom-call(bf16[256,5120]{1,0:T(8,128)(2,1)} %refs_0_.3, bf16[4,5120]{1,0:T(4,128)(2,1)S(1)} %stack.3.refs_1_.refs_0_.refs_2_), custom_call_target="tpu_custom_call" | custom-call | bytes 5242880 | tf_op jit(solution)/shard_map/load/pallas_call | solution.py:77
  13.1 1.0 %collective-permute-done.2.refs_2_ = bf16[4,5120]{1,0:T(4,128)(2,1)S(1)} collective-permute-done((bf16[4,5120]{1,0:T(4,128)(2,1)S(1)}, bf16[4,5120]{1,0:T(4,128)(2,1)S(1)}, u32[]{:S(2)}, u32[]{:S(2)}) %collective-permute-start.2) | collective-permute-done | bytes 40992 | tf_op jit(solution)/shard_map/ppermute | solution.py:52
  14.1 0.6 %collective-permute-done.1.refs_1_ = bf16[4,5120]{1,0:T(4,128)(2,1)S(1)} collective-permute-done((bf16[4,5120]{1,0:T(4,128)(2,1)S(1)}, bf16[4,5120]{1,0:T(4,128)(2,1)S(1)}, u32[]{:S(2)}, u32[]{:S(2)}) %collective-permute-start.1) | collective-permute-done | bytes 40992 | tf_op jit(solution)/shard_map/ppermute | solution.py:52
  14.8 1.6 %encode_decode.1 = (bf16[16,5120]{1,0:T(8,128)(2,1)S(1)}, f32[16,256]{1,0:T(8,128)S(1)}, f32[16,256]{1,0:T(8,128)S(1)}, f32[4,5120]{1,0:T(4,128)S(1)}, f32[4,512...) custom-call(bf16[16,5120]{1,0:T(8,128)(2,1)S(1)} %stack.4.refs_0_, ...), custom_call_target="tpu_custom_call" | custom-call | flops 167772160 | tf_op jit(solution)/shard_map/encode_decode/pallas_call | solution.py:38
  16.3 1.0 %collective-permute-start.8 = (f32[4,5120]{1,0:T(4,128)S(1)}, f32[4,5120]{1,0:T(4,128)S(1)}, u32[]{:S(2)}, u32[]{:S(2)}) collective-permute-start(f32[4,5120]{1,0:T(4,128)S(1)} %get-tuple-element.38), channel_id=1, source_target_pairs={{0,4},{2,6},{4,0},{6,2},{8,12},{10,14},{12,8},{14,10},{1,5},{3,7},... | collective-permute-start | bytes 245768 | tf_op jit(solution)/shard_map/ppermute | solution.py:52
  17.3 1.0 %collective-permute-start.9 = (f32[4,5120]{1,0:T(4,128)S(1)}, f32[4,5120]{1,0:T(4,128)S(1)}, u32[]{:S(2)}, u32[]{:S(2)}) collective-permute-start(f32[4,5120]{1,0:T(4,128)S(1)} %get-tuple-element.39), channel_id=1, source_target_pairs={{0,2},{2,0},{4,6},{6,4},{8,10},{10,8},{12,14},{14,12},{1,3},{3,1},... | collective-permute-start | bytes 245768 | tf_op jit(solution)/shard_map/ppermute | solution.py:52
  18.3 1.5 %collective-permute-start.10 = (f32[4,5120]{1,0:T(4,128)S(1)}, f32[4,5120]{1,0:T(4,128)S(1)}, u32[]{:S(2)}, u32[]{:S(2)}) collective-permute-start(f32[4,5120]{1,0:T(4,128)S(1)} %get-tuple-element.40), channel_id=1, source_target_pairs={{0,6},{2,4},{4,2},{6,0},{8,14},{10,12},{12,10},{14,8},{1,7},{3,5},... | collective-permute-start | bytes 245768 | tf_op jit(solution)/shard_map/ppermute | solution.py:52
  19.9 1.4 %turn.2.refs_4_.refs_1_ = bf16[5120,512]{1,0:T(8,128)(2,1)S(1)} custom-call(bf16[256,5120]{1,0:T(8,128)(2,1)S(1)} %load.3.refs_4_.refs_0_, bf16[256,5120]{1,0:T(8,128)(2,1)S(1)} %collective-permute-done.6.refs_7_.refs_1_, f32[4,5120]{1,0:T(4,128)S(1)} %get-tuple-element.37.refs_2_.refs_0_), custom_call_target="tpu_custom_call" | custom-call | bytes 10485760 | tf_op jit(solution)/shard_map/turn/pallas_call | solution.py:38
  21.3 0.6 %collective-permute-done.9.refs_2_ = f32[4,5120]{1,0:T(4,128)S(1)} collective-permute-done((f32[4,5120]{1,0:T(4,128)S(1)}, f32[4,5120]{1,0:T(4,128)S(1)}, u32[]{:S(2)}, u32[]{:S(2)}) %collective-permute-start.9) | collective-permute-done | bytes 81952 | tf_op jit(solution)/shard_map/ppermute | solution.py:52
  21.9 1.8 %collective-permute-done.10.refs_3_ = f32[4,5120]{1,0:T(4,128)S(1)} collective-permute-done((f32[4,5120]{1,0:T(4,128)S(1)}, f32[4,5120]{1,0:T(4,128)S(1)}, u32[]{:S(2)}, u32[]{:S(2)}) %collective-permute-start.10) | collective-permute-done | bytes 81952 | tf_op jit(solution)/shard_map/ppermute | solution.py:52
  23.7 2.8 %collective-permute-start.11 = (f32[4,5120]{1,0:T(4,128)S(1)}, f32[4,5120]{1,0:T(4,128)S(1)}, u32[]{:S(2)}, u32[]{:S(2)}) collective-permute-start(f32[4,5120]{1,0:T(4,128)S(1)} %add_parts.1.refs_2_.refs_0_), channel_id=1, source_target_pairs={{0,8},{2,10},{4,12},{6,14},{8,0},{10,2},{12,4},{14,6},{1,9},{3,11}... | collective-permute-start | bytes 245768 | tf_op jit(solution)/shard_map/ppermute | solution.py:52
  26.5 1.5 %turn.3.refs_4_.refs_1_ = bf16[512,5120]{1,0:T(8,128)(2,1)S(1)} custom-call(bf16[5120,256]{1,0:T(8,128)(2,1)S(1)} %get-tuple-element.33.refs_2_.refs_0_, bf16[5120,256]{1,0:T(8,128)(2,1)S(1)} %collective-permute-done.4.refs_5_.refs_1_, f32[4,5120]{1,0:T(4,128)S(1)} %add_parts.1.refs_2_.refs_0_), custom_call_target="tpu_custom_call" | custom-call | bytes 10485760 | tf_op jit(solution)/shard_map/turn/pallas_call | solution.py:38
  28.0 1.1 %collective-permute-done.11.refs_1_ = f32[4,5120]{1,0:T(4,128)S(1)} collective-permute-done((f32[4,5120]{1,0:T(4,128)S(1)}, f32[4,5120]{1,0:T(4,128)S(1)}, u32[]{:S(2)}, u32[]{:S(2)}) %collective-permute-start.11) | collective-permute-done | bytes 81952 | tf_op jit(solution)/shard_map/ppermute | solution.py:52
  29.2 1.9 %collective-permute-start.15 = (bf16[4,5120]{1,0:T(4,128)(2,1)S(1)}, bf16[4,5120]{1,0:T(4,128)(2,1)S(1)}, u32[]{:S(2)}, u32[]{:S(2)}) collective-permute-start(bf16[4,5120]{1,0:T(4,128)(2,1)S(1)} %residual_gradient.1.refs_4_.refs_0_), channel_id=1, source_target_pairs={{0,2},{2,0},{4,6},{6,4},{8,10},{10,8},{12,14},{14,12},{1,3},{3,1},... | collective-permute-start | bytes 122888 | tf_op jit(solution)/shard_map/ppermute | solution.py:52
  31.1 1.2 %collective-permute-start.14 = (bf16[4,5120]{1,0:T(4,128)(2,1)S(1)}, bf16[4,5120]{1,0:T(4,128)(2,1)S(1)}, u32[]{:S(2)}, u32[]{:S(2)}) collective-permute-start(bf16[4,5120]{1,0:T(4,128)(2,1)S(1)} %residual_gradient.1.refs_4_.refs_0_), channel_id=1, source_target_pairs={{0,6},{2,4},{4,2},{6,0},{8,14},{10,12},{12,10},{14,8},{1,7},{3,5},... | collective-permute-start | bytes 122888 | tf_op jit(solution)/shard_map/ppermute | solution.py:52
  33.1 0.5 %collective-permute-done.15.refs_3_ = bf16[4,5120]{1,0:T(4,128)(2,1)S(1)} collective-permute-done((bf16[4,5120]{1,0:T(4,128)(2,1)S(1)}, bf16[4,5120]{1,0:T(4,128)(2,1)S(1)}, u32[]{:S(2)}, u32[]{:S(2)}) %collective-permute-start.15) | collective-permute-done | bytes 40992 | tf_op jit(solution)/shard_map/ppermute | solution.py:52
  33.7 2.3 %collective-permute-done.14.refs_2_ = bf16[4,5120]{1,0:T(4,128)(2,1)S(1)} collective-permute-done((bf16[4,5120]{1,0:T(4,128)(2,1)S(1)}, bf16[4,5120]{1,0:T(4,128)(2,1)S(1)}, u32[]{:S(2)}, u32[]{:S(2)}) %collective-permute-start.14) | collective-permute-done | bytes 40992 | tf_op jit(solution)/shard_map/ppermute | solution.py:52
  36.5 0.8 %backward.1 = (bf16[16,256]{1,0:T(8,128)(2,1)S(1)}, f32[16,256]{1,0:T(8,128)S(1)}, f32[1,512]{1,0:T(1,128)S(1)}) custom-call(bf16[16,5120]{1,0:T(8,128)(2,1)S(1)} %stack.5.refs_0_.refs_2_, bf16[5120,512]{1,0:T(8,128)(2,1)S(1)} %turn.2.refs_4_.refs_1_, f32[16,256]{1,0:T(8,128)S(1)} %get-tuple-element.43.refs_0_.refs_2_, f32[16,256]{1,0:T(8,128)S(1)} %get-tuple-element.41.refs_3_), custom_call_target="tpu_custom_call" | custom-call | tf_op jit(solution)/shard_map/backward/pallas_call | solution.py:38
  37.3 0.8 %bias_product.1.refs_4_.refs_0_ = f32[1,5248]{1,0:T(1,128)S(1)} custom-call(f32[1,512]{1,0:T(1,128)S(1)} %get-tuple-element.46.refs_0_.refs_4_, bf16[512,5120]{1,0:T(8,128)(2,1)S(1)} %turn.3.refs_4_.refs_1_, f32[1,5120]{1,0:T(1,128)S(1)} %get-tuple-element.47.refs_2_, f32[1,128]{1,0:T(1,128)S(1)} %get-tuple-element.42.refs_4_.refs_3_, ...), custom_call_target="tpu_custom_call" | custom-call | tf_op jit(solution)/shard_map/bias_product/pallas_call | solution.py:38
  38.1 0.5 %collective-permute-start.18 = (f32[1,5248]{1,0:T(1,128)S(1)}, f32[1,5248]{1,0:T(1,128)S(1)}, u32[]{:S(2)}, u32[]{:S(2)}) collective-permute-start(f32[1,5248]{1,0:T(1,128)S(1)} %bias_product.1.refs_4_.refs_0_), channel_id=1, source_target_pairs={{0,1},{1,0},{2,3},{3,2},{4,5},{5,4},{6,7},{7,6},{8,9},{9,8},{10,11... | collective-permute-start | bytes 62984 | tf_op jit(solution)/shard_map/ppermute | solution.py:51
  38.7 0.9 %dec_gradient.1.refs_2_.refs_5_ = bf16[256,5120]{1,0:T(8,128)(2,1)S(1)} custom-call(f32[16,256]{1,0:T(8,128)S(1)} %get-tuple-element.43.refs_0_.refs_2_, f32[16,256]{1,0:T(8,128)S(1)} %collective-permute-done.12.refs_5_.refs_1_, bf16[16,5120]{1,0:T(8,128)(2,1)S(1)} %stack.5.refs_0_.refs_2_, bf16[16,5120]{1,0:T(8,128)(2,1)S(1)} %collective-permute-done.17.refs_3_, ...), custom_call_target="tpu_custom_call" | custom-call | flops 83886080 | tf_op jit(solution)/shard_map/dec_gradient/pallas_call | solution.py:38
  39.6 0.8 %collective-permute-start.21 = (f32[1,5248]{1,0:T(1,128)S(1)}, f32[1,5248]{1,0:T(1,128)S(1)}, u32[]{:S(2)}, u32[]{:S(2)}) collective-permute-start(f32[1,5248]{1,0:T(1,128)S(1)} %add.2.refs_7_.refs_0_), channel_id=1, source_target_pairs={{0,2},{2,0},{4,6},{6,4},{8,10},{10,8},{12,14},{14,12},{1,3},{3,1},... | collective-permute-start | bytes 62984 | tf_op jit(solution)/shard_map/ppermute | solution.py:52
  40.4 1.2 %collective-permute-start.20 = (f32[1,5248]{1,0:T(1,128)S(1)}, f32[1,5248]{1,0:T(1,128)S(1)}, u32[]{:S(2)}, u32[]{:S(2)}) collective-permute-start(f32[1,5248]{1,0:T(1,128)S(1)} %add.2.refs_7_.refs_0_), channel_id=1, source_target_pairs={{0,6},{2,4},{4,2},{6,0},{8,14},{10,12},{12,10},{14,8},{1,7},{3,5},... | collective-permute-start | bytes 62984 | tf_op jit(solution)/shard_map/ppermute | solution.py:52
  41.6 1.6 %collective-permute-start.19 = (f32[1,5248]{1,0:T(1,128)S(1)}, f32[1,5248]{1,0:T(1,128)S(1)}, u32[]{:S(2)}, u32[]{:S(2)}) collective-permute-start(f32[1,5248]{1,0:T(1,128)S(1)} %add.2.refs_7_.refs_0_), channel_id=1, source_target_pairs={{0,4},{2,6},{4,0},{6,2},{8,12},{10,14},{12,8},{14,10},{1,5},{3,7},... | collective-permute-start | bytes 62984 | tf_op jit(solution)/shard_map/ppermute | solution.py:52
  43.2 1.5 %enc_gradient.1 = (bf16[256,5120]{1,0:T(8,128)(2,1)}, bf16[2,5120]{1,0:T(2,128)(2,1)}, bf16[5120,256]{1,0:T(8,128)(2,1)S(1)}, f32[1,256]{1,0:T(1,128)S(1)}) custom-call(bf16[16,5120]{1,0:T(8,128)(2,1)S(1)} %get-tuple-element.36.refs_0_, bf16[16,5120]{1,0:T(8,128)(2,1)S(1)} %collective-permute-done.7.refs_6_.refs_1_, ...), custom_call_target="tpu_custom_call" | custom-call | flops 83886080 | bytes 5242880 | tf_op jit(solution)/shard_map/enc_gradient/pallas_call | solution.py:316
  45.4 3.4 %collective-permute-start.22 = (f32[1,5248]{1,0:T(1,128)S(1)}, f32[1,5248]{1,0:T(1,128)S(1)}, u32[]{:S(2)}, u32[]{:S(2)}) collective-permute-start(f32[1,5248]{1,0:T(1,128)S(1)} %add.3.refs_2_.terms_ref), channel_id=1, source_target_pairs={{0,8},{2,10},{4,12},{6,14},{8,0},{10,2},{12,4},{14,6},{1,9},{3,11}... | collective-permute-start | bytes 62984 | tf_op jit(solution)/shard_map/ppermute | solution.py:52
  48.8 1.5 %store.1 = (bf16[5120,256]{1,0:T(8,128)(2,1)}, f32[1,256]{1,0:T(1,128)}, f32[8,128]{1,0:T(8,128)S(1)}) custom-call(bf16[5120,256]{1,0:T(8,128)(2,1)S(1)} %get-tuple-element.50.refs_4_.refs_0_, f32[1,256]{1,0:T(1,128)S(1)} %get-tuple-element.51.refs_1_, f32[1,5248]{1,0:T(1,128)S(1)} %add.3.refs_2_.terms_ref), custom_call_target="tpu_custom_call" | custom-call | bytes 5244928 | tf_op jit(solution)/shard_map/store/pallas_call | solution.py:342
  50.6 0.6 %finish.1 = (f32[1,5120]{1,0:T(1,128)}, f32[1,1]{1,0:T(1,128)}) custom-call(f32[1,5248]{1,0:T(1,128)S(1)} %add.3.refs_2_.terms_ref, f32[1,5248]{1,0:T(1,128)S(1)} %collective-permute-done.22.other_ref, f32[8,128]{1,0:T(8,128)S(1)} %get-tuple-element.52.after_ref), custom_call_target="tpu_custom_call" | custom-call | tf_op jit(solution)/shard_map/finish/pallas_call | solution.py:374
  (36 shorter events, 3.8 us)
Async XLA Ops:
  0.6 14.1 %collective-permute-start.4 = (bf16[5120,256]{1,0:T(8,128)(2,1)}, bf16[5120,256]{1,0:T(8,128)(2,1)S(1)}, u32[]{:S(2)}, u32[]{:S(2)}) collective-permute-start(bf16[5120,256]{1,0:T(8,128)(2,1)} %refs_0_.2), channel_id=1, source_target_pairs={{0,1},{1,0},{2,3},{3,2},{4,5},{5,4},{6,7},{7,6},{8,9},{9,8},{10,11... | collective-permute-start | bytes 7864328 | tf_op jit(solution)/shard_map/ppermute | solution.py:51
  1.2 13.6 %collective-permute-start.6 = (bf16[256,5120]{1,0:T(8,128)(2,1)}, bf16[256,5120]{1,0:T(8,128)(2,1)S(1)}, u32[]{:S(2)}, u32[]{:S(2)}) collective-permute-start(bf16[256,5120]{1,0:T(8,128)(2,1)} %refs_0_.3), channel_id=1, source_target_pairs={{0,1},{1,0},{2,3},{3,2},{4,5},{5,4},{6,7},{7,6},{8,9},{9,8},{10,11... | collective-permute-start | bytes 7864328 | tf_op jit(solution)/shard_map/ppermute | solution.py:51
  1.2 6.0 %collective-permute-start = (bf16[2,5120]{1,0:T(2,128)(2,1)}, bf16[2,5120]{1,0:T(2,128)(2,1)S(1)}, u32[]{:S(2)}, u32[]{:S(2)}) collective-permute-start(bf16[2,5120]{1,0:T(2,128)(2,1)} %refs_1_.1), channel_id=1, source_target_pairs={{0,8},{2,10},{4,12},{6,14},{8,0},{10,2},{12,4},{14,6},{1,9},{3,11}... | collective-permute-start | bytes 61448 | tf_op jit(solution)/shard_map/ppermute | solution.py:52
  5.2 6.1 %copy-start = (f32[256]{0:T(256)S(1)}, f32[256]{0:T(256)}, u32[]{:S(2)}) copy-start(f32[256]{0:T(256)} %param.7) | copy-start | bytes 3076
  7.3 4.1 %collective-permute-start.3 = (bf16[4,5120]{1,0:T(4,128)(2,1)S(1)}, bf16[4,5120]{1,0:T(4,128)(2,1)S(1)}, u32[]{:S(2)}, u32[]{:S(2)}) collective-permute-start(bf16[4,5120]{1,0:T(4,128)(2,1)S(1)} %stack.3.refs_1_.refs_0_.refs_2_), channel_id=1, source_target_pairs={{0,2},{2,0},{4,6},{6,4},{8,10},{10,8},{12,14},{14,12},{1,3},{3,1},... | collective-permute-start | bytes 122888 | tf_op jit(solution)/shard_map/ppermute | solution.py:52
  9.2 4.9 %collective-permute-start.2 = (bf16[4,5120]{1,0:T(4,128)(2,1)S(1)}, bf16[4,5120]{1,0:T(4,128)(2,1)S(1)}, u32[]{:S(2)}, u32[]{:S(2)}) collective-permute-start(bf16[4,5120]{1,0:T(4,128)(2,1)S(1)} %stack.3.refs_1_.refs_0_.refs_2_), channel_id=1, source_target_pairs={{0,6},{2,4},{4,2},{6,0},{8,14},{10,12},{12,10},{14,8},{1,7},{3,5},... | collective-permute-start | bytes 122888 | tf_op jit(solution)/shard_map/ppermute | solution.py:52
  10.7 4.0 %collective-permute-start.1 = (bf16[4,5120]{1,0:T(4,128)(2,1)S(1)}, bf16[4,5120]{1,0:T(4,128)(2,1)S(1)}, u32[]{:S(2)}, u32[]{:S(2)}) collective-permute-start(bf16[4,5120]{1,0:T(4,128)(2,1)S(1)} %stack.3.refs_1_.refs_0_.refs_2_), channel_id=1, source_target_pairs={{0,4},{2,6},{4,0},{6,2},{8,12},{10,14},{12,8},{14,10},{1,5},{3,7},... | collective-permute-start | bytes 122888 | tf_op jit(solution)/shard_map/ppermute | solution.py:52
  11.3 3.4 %collective-permute-start.5 = (f32[1,256]{1,0:T(1,128)S(1)}, f32[1,256]{1,0:T(1,128)S(1)}, u32[]{:S(2)}, u32[]{:S(2)}) collective-permute-start(f32[1,256]{1,0:T(1,128)S(1)} %bitcast.7), channel_id=1, source_target_pairs={{0,1},{1,0},{2,3},{3,2},{4,5},{5,4},{6,7},{7,6},{8,9},{9,8},{10,11... | collective-permute-start | bytes 3080 | tf_op jit(solution)/shard_map/ppermute | solution.py:51
  16.3 4.9 %collective-permute-start.8 = (f32[4,5120]{1,0:T(4,128)S(1)}, f32[4,5120]{1,0:T(4,128)S(1)}, u32[]{:S(2)}, u32[]{:S(2)}) collective-permute-start(f32[4,5120]{1,0:T(4,128)S(1)} %get-tuple-element.38), channel_id=1, source_target_pairs={{0,4},{2,6},{4,0},{6,2},{8,12},{10,14},{12,8},{14,10},{1,5},{3,7},... | collective-permute-start | bytes 245768 | tf_op jit(solution)/shard_map/ppermute | solution.py:52
  17.3 4.6 %collective-permute-start.9 = (f32[4,5120]{1,0:T(4,128)S(1)}, f32[4,5120]{1,0:T(4,128)S(1)}, u32[]{:S(2)}, u32[]{:S(2)}) collective-permute-start(f32[4,5120]{1,0:T(4,128)S(1)} %get-tuple-element.39), channel_id=1, source_target_pairs={{0,2},{2,0},{4,6},{6,4},{8,10},{10,8},{12,14},{14,12},{1,3},{3,1},... | collective-permute-start | bytes 245768 | tf_op jit(solution)/shard_map/ppermute | solution.py:52
  18.3 5.3 %collective-permute-start.10 = (f32[4,5120]{1,0:T(4,128)S(1)}, f32[4,5120]{1,0:T(4,128)S(1)}, u32[]{:S(2)}, u32[]{:S(2)}) collective-permute-start(f32[4,5120]{1,0:T(4,128)S(1)} %get-tuple-element.40), channel_id=1, source_target_pairs={{0,6},{2,4},{4,2},{6,0},{8,14},{10,12},{12,10},{14,8},{1,7},{3,5},... | collective-permute-start | bytes 245768 | tf_op jit(solution)/shard_map/ppermute | solution.py:52
  19.9 9.2 %collective-permute-start.7 = (bf16[16,5120]{1,0:T(8,128)(2,1)S(1)}, bf16[16,5120]{1,0:T(8,128)(2,1)S(1)}, u32[]{:S(2)}, u32[]{:S(2)}) collective-permute-start(bf16[16,5120]{1,0:T(8,128)(2,1)S(1)} %get-tuple-element.36.refs_0_), channel_id=1, source_target_pairs={{0,1},{1,0},{2,3},{3,2},{4,5},{5,4},{6,7},{7,6},{8,9},{9,8},{10,11... | collective-permute-start | bytes 491528 | tf_op jit(solution)/shard_map/ppermute | solution.py:51
  23.7 5.4 %collective-permute-start.11 = (f32[4,5120]{1,0:T(4,128)S(1)}, f32[4,5120]{1,0:T(4,128)S(1)}, u32[]{:S(2)}, u32[]{:S(2)}) collective-permute-start(f32[4,5120]{1,0:T(4,128)S(1)} %add_parts.1.refs_2_.refs_0_), channel_id=1, source_target_pairs={{0,8},{2,10},{4,12},{6,14},{8,0},{10,2},{12,4},{14,6},{1,9},{3,11}... | collective-permute-start | bytes 245768 | tf_op jit(solution)/shard_map/ppermute | solution.py:52
  26.5 1.5 %collective-permute-start.12 = (f32[16,256]{1,0:T(8,128)S(1)}, f32[16,256]{1,0:T(8,128)S(1)}, u32[]{:S(2)}, u32[]{:S(2)}) collective-permute-start(f32[16,256]{1,0:T(8,128)S(1)} %get-tuple-element.41.refs_3_), channel_id=1, source_target_pairs={{0,1},{1,0},{2,3},{3,2},{4,5},{5,4},{6,7},{7,6},{8,9},{9,8},{10,11... | collective-permute-start | bytes 49160 | tf_op jit(solution)/shard_map/ppermute | solution.py:51
  29.2 4.5 %collective-permute-start.15 = (bf16[4,5120]{1,0:T(4,128)(2,1)S(1)}, bf16[4,5120]{1,0:T(4,128)(2,1)S(1)}, u32[]{:S(2)}, u32[]{:S(2)}) collective-permute-start(bf16[4,5120]{1,0:T(4,128)(2,1)S(1)} %residual_gradient.1.refs_4_.refs_0_), channel_id=1, source_target_pairs={{0,2},{2,0},{4,6},{6,4},{8,10},{10,8},{12,14},{14,12},{1,3},{3,1},... | collective-permute-start | bytes 122888 | tf_op jit(solution)/shard_map/ppermute | solution.py:52
  31.1 4.9 %collective-permute-start.14 = (bf16[4,5120]{1,0:T(4,128)(2,1)S(1)}, bf16[4,5120]{1,0:T(4,128)(2,1)S(1)}, u32[]{:S(2)}, u32[]{:S(2)}) collective-permute-start(bf16[4,5120]{1,0:T(4,128)(2,1)S(1)} %residual_gradient.1.refs_4_.refs_0_), channel_id=1, source_target_pairs={{0,6},{2,4},{4,2},{6,0},{8,14},{10,12},{12,10},{14,8},{1,7},{3,5},... | collective-permute-start | bytes 122888 | tf_op jit(solution)/shard_map/ppermute | solution.py:52
  32.4 4.0 %collective-permute-start.13 = (bf16[4,5120]{1,0:T(4,128)(2,1)S(1)}, bf16[4,5120]{1,0:T(4,128)(2,1)S(1)}, u32[]{:S(2)}, u32[]{:S(2)}) collective-permute-start(bf16[4,5120]{1,0:T(4,128)(2,1)S(1)} %residual_gradient.1.refs_4_.refs_0_), channel_id=1, source_target_pairs={{0,4},{2,6},{4,0},{6,2},{8,12},{10,14},{12,8},{14,10},{1,5},{3,7},... | collective-permute-start | bytes 122888 | tf_op jit(solution)/shard_map/ppermute | solution.py:52
  36.4 2.3 %collective-permute-start.17 = (bf16[16,5120]{1,0:T(8,128)(2,1)S(1)}, bf16[16,5120]{1,0:T(8,128)(2,1)S(1)}, u32[]{:S(2)}, u32[]{:S(2)}) collective-permute-start(bf16[16,5120]{1,0:T(8,128)(2,1)S(1)} %stack.5.refs_0_.refs_2_), channel_id=1, source_target_pairs={{0,1},{1,0},{2,3},{3,2},{4,5},{5,4},{6,7},{7,6},{8,9},{9,8},{10,11... | collective-permute-start | bytes 491528 | tf_op jit(solution)/shard_map/ppermute | solution.py:51
  38.1 1.5 %collective-permute-start.18 = (f32[1,5248]{1,0:T(1,128)S(1)}, f32[1,5248]{1,0:T(1,128)S(1)}, u32[]{:S(2)}, u32[]{:S(2)}) collective-permute-start(f32[1,5248]{1,0:T(1,128)S(1)} %bias_product.1.refs_4_.refs_0_), channel_id=1, source_target_pairs={{0,1},{1,0},{2,3},{3,2},{4,5},{5,4},{6,7},{7,6},{8,9},{9,8},{10,11... | collective-permute-start | bytes 62984 | tf_op jit(solution)/shard_map/ppermute | solution.py:51
  38.6 4.5 %collective-permute-start.16 = (f32[16,256]{1,0:T(8,128)S(1)}, f32[16,256]{1,0:T(8,128)S(1)}, u32[]{:S(2)}, u32[]{:S(2)}) collective-permute-start(f32[16,256]{1,0:T(8,128)S(1)} %get-tuple-element.45), channel_id=1, source_target_pairs={{0,1},{1,0},{2,3},{3,2},{4,5},{5,4},{6,7},{7,6},{8,9},{9,8},{10,11... | collective-permute-start | bytes 49160 | tf_op jit(solution)/shard_map/ppermute | solution.py:51
  39.6 5.1 %collective-permute-start.21 = (f32[1,5248]{1,0:T(1,128)S(1)}, f32[1,5248]{1,0:T(1,128)S(1)}, u32[]{:S(2)}, u32[]{:S(2)}) collective-permute-start(f32[1,5248]{1,0:T(1,128)S(1)} %add.2.refs_7_.refs_0_), channel_id=1, source_target_pairs={{0,2},{2,0},{4,6},{6,4},{8,10},{10,8},{12,14},{14,12},{1,3},{3,1},... | collective-permute-start | bytes 62984 | tf_op jit(solution)/shard_map/ppermute | solution.py:52
  40.4 4.7 %collective-permute-start.20 = (f32[1,5248]{1,0:T(1,128)S(1)}, f32[1,5248]{1,0:T(1,128)S(1)}, u32[]{:S(2)}, u32[]{:S(2)}) collective-permute-start(f32[1,5248]{1,0:T(1,128)S(1)} %add.2.refs_7_.refs_0_), channel_id=1, source_target_pairs={{0,6},{2,4},{4,2},{6,0},{8,14},{10,12},{12,10},{14,8},{1,7},{3,5},... | collective-permute-start | bytes 62984 | tf_op jit(solution)/shard_map/ppermute | solution.py:52
  41.6 3.8 %collective-permute-start.19 = (f32[1,5248]{1,0:T(1,128)S(1)}, f32[1,5248]{1,0:T(1,128)S(1)}, u32[]{:S(2)}, u32[]{:S(2)}) collective-permute-start(f32[1,5248]{1,0:T(1,128)S(1)} %add.2.refs_7_.refs_0_), channel_id=1, source_target_pairs={{0,4},{2,6},{4,0},{6,2},{8,12},{10,14},{12,8},{14,10},{1,5},{3,7},... | collective-permute-start | bytes 62984 | tf_op jit(solution)/shard_map/ppermute | solution.py:52
  45.4 5.2 %collective-permute-start.22 = (f32[1,5248]{1,0:T(1,128)S(1)}, f32[1,5248]{1,0:T(1,128)S(1)}, u32[]{:S(2)}, u32[]{:S(2)}) collective-permute-start(f32[1,5248]{1,0:T(1,128)S(1)} %add.3.refs_2_.terms_ref), channel_id=1, source_target_pairs={{0,8},{2,10},{4,12},{6,14},{8,0},{10,2},{12,4},{14,6},{1,9},{3,11}... | collective-permute-start | bytes 62984 | tf_op jit(solution)/shard_map/ppermute | solution.py:52

commit v8 on v7

--- a/solution.py
+++ b/solution.py
@@ -232,18 +232,17 @@
     height = resid.shape[0]
     latents = active_own.shape[1]
 
-    def kernel(resid_ref, dec_ref, own_ref, sibling_ref, own_grad_ref, sibling_grad_ref, total_ref):
+    def kernel(resid_ref, dec_ref, own_ref, sibling_ref, own_grad_ref, total_ref):
         back = jnp.dot(resid_ref[...], dec_ref[...], preferred_element_type=jnp.float32)
         active = jnp.concatenate([own_ref[...], sibling_ref[...]], axis=1)
         code_grad = 2.0 * active * (back + PENALTY / row_count)
         own_grad_ref[...] = code_grad[:, :latents].astype(jnp.bfloat16)
-        sibling_grad_ref[...] = code_grad[:, latents:]
         total_ref[...] = jnp.sum(code_grad, axis=0, keepdims=True)
 
     return run(
         kernel,
         "backward",
-        [((height, latents), jnp.bfloat16), ((height, latents), jnp.float32), ((1, 2 * latents), jnp.float32)],
+        [((height, latents), jnp.bfloat16), ((1, 2 * latents), jnp.float32)],
         [resid, dec_turned, active_own, active_sibling],
     )
 
@@ -292,18 +291,19 @@
     )[0]
 
 
-def enc_gradient(centered_a, centered_b, code_grad_a, code_grad_b, total, stored, after):
+def enc_gradient(centered_a, centered_b, code_grad_a, resid_b, dec_turned, active_b, total, row_count, stored, after):
     half, width = centered_a.shape
     latents = code_grad_a.shape[1]
     count = len(stored)
 
     def kernel(*refs):
-        a_ref, b_ref, code_grad_a_ref, code_grad_b_ref, total_ref = refs[:5]
-        outs, (grad_ref, bias_ref, sems) = refs[6 + count : 6 + 2 * count], refs[-3:]
-        copies = [pltpu.make_async_copy(refs[5 + i], outs[i], sems.at[i]) for i in range(count)]
+        a_ref, b_ref, code_grad_a_ref, resid_ref, dec_ref, active_ref, total_ref = refs[:7]
+        outs, (grad_ref, bias_ref, sems) = refs[8 + count : 8 + 2 * count], refs[-3:]
+        copies = [pltpu.make_async_copy(refs[7 + i], outs[i], sems.at[i]) for i in range(count)]
         for copy in copies:
             copy.start()
-        grad_b = code_grad_b_ref[...]
+        back = jnp.dot(resid_ref[...], dec_ref[:, :latents], preferred_element_type=jnp.float32)
+        grad_b = 2.0 * active_ref[...] * (back + PENALTY / row_count)
         bias_ref[...] = total_ref[:, :latents] + jnp.sum(grad_b, axis=0, keepdims=True)
         centered = jnp.concatenate([a_ref[...], b_ref[...]], axis=0)
         code_grad = jnp.concatenate([code_grad_a_ref[...], grad_b.astype(jnp.bfloat16)], axis=0)
@@ -317,13 +317,13 @@
         kernel,
         out_shape=[jax.ShapeDtypeStruct(a.shape, a.dtype) for a in stored]
         + [vmem((width, latents), jnp.bfloat16), vmem((1, latents), jnp.float32)],
-        in_specs=[VMEM] * (6 + count),
+        in_specs=[VMEM] * (8 + count),
         out_specs=[HBM] * count + [VMEM] * 2,
         scratch_shapes=[pltpu.SemaphoreType.DMA((count,))],
         compiler_params=pltpu.CompilerParams(vmem_limit_bytes=LIMIT),
         cost_estimate=pl.CostEstimate(flops=4 * half * latents * width, bytes_accessed=4 * latents * width, transcendentals=0),
         name="enc_gradient",
-    )(*[in_vmem(a) for a in (centered_a, centered_b, code_grad_a, code_grad_b, total, *stored, after)])
+    )(*[in_vmem(a) for a in (centered_a, centered_b, code_grad_a, resid_b, dec_turned, active_b, total, *stored, after)])
     return outs, grad, bias
 
 
@@ -409,14 +409,13 @@
     code_total = code_sum(active_a, active_b)
     resid_a = gather(resid_bf, steps, RESID_ORDER, after=[square, code_total])
     resid_b = swap(resid_a, CORES)
-    code_grad_a, code_grad_sibling, total = backward(resid_a, dec_turned, active_a, active_sibling, row_count)
+    code_grad_a, total = backward(resid_a, dec_turned, active_a, active_sibling, row_count)
     terms = bias_product(total, enc_turned, own_bias, square, code_total, row_count)
-    code_grad_b = swap(code_grad_sibling, CORES)
 
     grad_dec = dec_gradient(active_a, active_b, resid_a, resid_b, [terms])
     terms = add(terms, swap(terms, CORES), after=[grad_dec])
     (grad_dec, recon), grad_enc, grad_enc_bias = enc_gradient(
-        centered_a, centered_b, code_grad_a, code_grad_b, total, [grad_dec, recon], terms
+        centered_a, centered_b, code_grad_a, resid_b, dec_turned, active_b, total, row_count, [grad_dec, recon], terms
     )
     for masks in steps:
         terms = add(

time: 51.4 us -> 51.3 us (level)
    ppermute x8 -> x7, starting transfers between devices: 1.29 us -> 1.21 us  [swap(): return lax.ppermute(values, 'sub', [(i, i ^ 1) for i in range(2)])]
  transfers between devices with their start and end apart: 23 -> 22, of which waited for: 13 -> 12; matrix products, arithmetic and copies ran while one was open for 0% -> 0% of each run, Pallas kernels for 24% -> 25%
where the time goes in v8:
time: 51.3 us; the launch traced here: 51.1 us
  starting transfers between devices  25.6 us (50%)
  Pallas kernels  15.2 us (30%)
  waiting for transfers between devices  9.49 us (18%)
  between operations  0.82 us (2%)
    ppermute x15, starting transfers between devices, swap(): lax.ppermute(values, 'lat', [(i, i ^ mask) for i in range(lax.axis_size('...  24.4 us
    ppermute x15, waiting for transfers between devices, swap(): lax.ppermute(values, 'lat', [(i, i ^ mask) for i in range(lax.axis_size('...  9.48 us
    pallas_call x15, Pallas kernels, run(): pl.pallas_call(body, out_shape=[vmem(*out) for out in outs], in_specs=[VM...  7.57 us
    pallas_call x2, Pallas kernels, load(): pl.pallas_call(kernel, out_shape=[vmem(array.shape, array.dtype) for arra...  3.54 us
    pallas_call x1, Pallas kernels, enc_gradient(): pl.pallas_call(kernel, out_shape=[jax.ShapeDtypeStruct(a.shape, a.dtype)...  1.96 us
    pallas_call x1, Pallas kernels, store(): pl.pallas_call(kernel, out_shape=[jax.ShapeDtypeStruct(a.shape, a.dtype)...  1.51 us
    ppermute x7, starting transfers between devices, swap(): return lax.ppermute(values, 'sub', [(i, i ^ 1) for i in range(2)])  1.21 us
  transfers between devices with their start and end apart: 22, of which 12 were waited for; matrix products, arithmetic and copies ran while one was open for 0% of the time, Pallas kernels for 25%

profile of v8, /device:TPU:0, one launch (start us, length us, event | category | flops | bytes accessed | tf_op | source)
XLA Modules:
  0.0 51.1 jit_solution(9626465819084597389)
XLA Ops:
  1.2 4.0 %collective-permute-start = (bf16[2,5120]{1,0:T(2,128)(2,1)}, bf16[2,5120]{1,0:T(2,128)(2,1)S(1)}, u32[]{:S(2)}, u32[]{:S(2)}) collective-permute-start(bf16[2,5120]{1,0:T(2,128)(2,1)} %refs_1_.1), channel_id=1, source_target_pairs={{0,8},{2,10},{4,12},{6,14},{8,0},{10,2},{12,4},{14,6},{1,9},{3,11}... | collective-permute-start | bytes 61448 | tf_op jit(solution)/shard_map/ppermute | solution.py:52
  5.2 1.8 %load.2 = (bf16[5120,256]{1,0:T(8,128)(2,1)S(1)}, bf16[2,5120]{1,0:T(2,128)(2,1)S(1)}, f32[1,5120]{1,0:T(1,128)S(1)}, f32[1,256]{1,0:T(1,128)S(1)}) custom-call(bf16[5120,256]{1,0:T(8,128)(2,1)} %refs_0_.2, bf16[2,5120]{1,0:T(2,128)(2,1)} %refs_1_.1, f32[1,5120]{1,0:T(1,128)} %bitcast.5, f32[1,256]{1,0:T(1,128)} %bitcast.6), custom_call_target="tpu_custom_call" | custom-call | bytes 5326848 | tf_op jit(solution)/shard_map/load/pallas_call | solution.py:77
  7.3 1.9 %collective-permute-start.3 = (bf16[4,5120]{1,0:T(4,128)(2,1)S(1)}, bf16[4,5120]{1,0:T(4,128)(2,1)S(1)}, u32[]{:S(2)}, u32[]{:S(2)}) collective-permute-start(bf16[4,5120]{1,0:T(4,128)(2,1)S(1)} %stack.3.refs_1_.refs_0_.refs_2_), channel_id=1, source_target_pairs={{0,2},{2,0},{4,6},{6,4},{8,10},{10,8},{12,14},{14,12},{1,3},{3,1},... | collective-permute-start | bytes 122888 | tf_op jit(solution)/shard_map/ppermute | solution.py:52
  9.2 1.5 %collective-permute-start.2 = (bf16[4,5120]{1,0:T(4,128)(2,1)S(1)}, bf16[4,5120]{1,0:T(4,128)(2,1)S(1)}, u32[]{:S(2)}, u32[]{:S(2)}) collective-permute-start(bf16[4,5120]{1,0:T(4,128)(2,1)S(1)} %stack.3.refs_1_.refs_0_.refs_2_), channel_id=1, source_target_pairs={{0,6},{2,4},{4,2},{6,0},{8,14},{10,12},{12,10},{14,8},{1,7},{3,5},... | collective-permute-start | bytes 122888 | tf_op jit(solution)/shard_map/ppermute | solution.py:52
  11.3 1.7 %load.3.refs_4_.refs_0_ = bf16[256,5120]{1,0:T(8,128)(2,1)S(1)} custom-call(bf16[256,5120]{1,0:T(8,128)(2,1)} %refs_0_.3, bf16[4,5120]{1,0:T(4,128)(2,1)S(1)} %stack.3.refs_1_.refs_0_.refs_2_), custom_call_target="tpu_custom_call" | custom-call | bytes 5242880 | tf_op jit(solution)/shard_map/load/pallas_call | solution.py:77
  13.1 1.0 %collective-permute-done.2.refs_2_ = bf16[4,5120]{1,0:T(4,128)(2,1)S(1)} collective-permute-done((bf16[4,5120]{1,0:T(4,128)(2,1)S(1)}, bf16[4,5120]{1,0:T(4,128)(2,1)S(1)}, u32[]{:S(2)}, u32[]{:S(2)}) %collective-permute-start.2) | collective-permute-done | bytes 40992 | tf_op jit(solution)/shard_map/ppermute | solution.py:52
  14.1 0.6 %collective-permute-done.1.refs_1_ = bf16[4,5120]{1,0:T(4,128)(2,1)S(1)} collective-permute-done((bf16[4,5120]{1,0:T(4,128)(2,1)S(1)}, bf16[4,5120]{1,0:T(4,128)(2,1)S(1)}, u32[]{:S(2)}, u32[]{:S(2)}) %collective-permute-start.1) | collective-permute-done | bytes 40992 | tf_op jit(solution)/shard_map/ppermute | solution.py:52
  14.8 1.6 %encode_decode.1 = (bf16[16,5120]{1,0:T(8,128)(2,1)S(1)}, f32[16,256]{1,0:T(8,128)S(1)}, f32[16,256]{1,0:T(8,128)S(1)}, f32[4,5120]{1,0:T(4,128)S(1)}, f32[4,512...) custom-call(bf16[16,5120]{1,0:T(8,128)(2,1)S(1)} %stack.4.refs_0_, ...), custom_call_target="tpu_custom_call" | custom-call | flops 167772160 | tf_op jit(solution)/shard_map/encode_decode/pallas_call | solution.py:38
  16.3 1.0 %collective-permute-start.8 = (f32[4,5120]{1,0:T(4,128)S(1)}, f32[4,5120]{1,0:T(4,128)S(1)}, u32[]{:S(2)}, u32[]{:S(2)}) collective-permute-start(f32[4,5120]{1,0:T(4,128)S(1)} %get-tuple-element.37), channel_id=1, source_target_pairs={{0,4},{2,6},{4,0},{6,2},{8,12},{10,14},{12,8},{14,10},{1,5},{3,7},... | collective-permute-start | bytes 245768 | tf_op jit(solution)/shard_map/ppermute | solution.py:52
  17.3 1.0 %collective-permute-start.9 = (f32[4,5120]{1,0:T(4,128)S(1)}, f32[4,5120]{1,0:T(4,128)S(1)}, u32[]{:S(2)}, u32[]{:S(2)}) collective-permute-start(f32[4,5120]{1,0:T(4,128)S(1)} %get-tuple-element.38), channel_id=1, source_target_pairs={{0,2},{2,0},{4,6},{6,4},{8,10},{10,8},{12,14},{14,12},{1,3},{3,1},... | collective-permute-start | bytes 245768 | tf_op jit(solution)/shard_map/ppermute | solution.py:52
  18.3 1.5 %collective-permute-start.10 = (f32[4,5120]{1,0:T(4,128)S(1)}, f32[4,5120]{1,0:T(4,128)S(1)}, u32[]{:S(2)}, u32[]{:S(2)}) collective-permute-start(f32[4,5120]{1,0:T(4,128)S(1)} %get-tuple-element.39), channel_id=1, source_target_pairs={{0,6},{2,4},{4,2},{6,0},{8,14},{10,12},{12,10},{14,8},{1,7},{3,5},... | collective-permute-start | bytes 245768 | tf_op jit(solution)/shard_map/ppermute | solution.py:52
  19.9 1.4 %turn.2.refs_4_.refs_1_ = bf16[5120,512]{1,0:T(8,128)(2,1)S(1)} custom-call(bf16[256,5120]{1,0:T(8,128)(2,1)S(1)} %load.3.refs_4_.refs_0_, bf16[256,5120]{1,0:T(8,128)(2,1)S(1)} %collective-permute-done.6.refs_7_.refs_1_, f32[4,5120]{1,0:T(4,128)S(1)} %get-tuple-element.36.refs_2_.refs_0_), custom_call_target="tpu_custom_call" | custom-call | bytes 10485760 | tf_op jit(solution)/shard_map/turn/pallas_call | solution.py:38
  21.3 0.6 %collective-permute-done.9.refs_2_ = f32[4,5120]{1,0:T(4,128)S(1)} collective-permute-done((f32[4,5120]{1,0:T(4,128)S(1)}, f32[4,5120]{1,0:T(4,128)S(1)}, u32[]{:S(2)}, u32[]{:S(2)}) %collective-permute-start.9) | collective-permute-done | bytes 81952 | tf_op jit(solution)/shard_map/ppermute | solution.py:52
  21.9 1.8 %collective-permute-done.10.refs_3_ = f32[4,5120]{1,0:T(4,128)S(1)} collective-permute-done((f32[4,5120]{1,0:T(4,128)S(1)}, f32[4,5120]{1,0:T(4,128)S(1)}, u32[]{:S(2)}, u32[]{:S(2)}) %collective-permute-start.10) | collective-permute-done | bytes 81952 | tf_op jit(solution)/shard_map/ppermute | solution.py:52
  23.7 2.8 %collective-permute-start.11 = (f32[4,5120]{1,0:T(4,128)S(1)}, f32[4,5120]{1,0:T(4,128)S(1)}, u32[]{:S(2)}, u32[]{:S(2)}) collective-permute-start(f32[4,5120]{1,0:T(4,128)S(1)} %add_parts.1.refs_2_.refs_0_), channel_id=1, source_target_pairs={{0,8},{2,10},{4,12},{6,14},{8,0},{10,2},{12,4},{14,6},{1,9},{3,11}... | collective-permute-start | bytes 245768 | tf_op jit(solution)/shard_map/ppermute | solution.py:52
  26.5 1.5 %turn.3.refs_4_.refs_1_ = bf16[512,5120]{1,0:T(8,128)(2,1)S(1)} custom-call(bf16[5120,256]{1,0:T(8,128)(2,1)S(1)} %get-tuple-element.32.refs_2_.refs_0_, bf16[5120,256]{1,0:T(8,128)(2,1)S(1)} %collective-permute-done.4.refs_5_.refs_1_, f32[4,5120]{1,0:T(4,128)S(1)} %add_parts.1.refs_2_.refs_0_), custom_call_target="tpu_custom_call" | custom-call | bytes 10485760 | tf_op jit(solution)/shard_map/turn/pallas_call | solution.py:38
  28.0 1.1 %collective-permute-done.11.refs_1_ = f32[4,5120]{1,0:T(4,128)S(1)} collective-permute-done((f32[4,5120]{1,0:T(4,128)S(1)}, f32[4,5120]{1,0:T(4,128)S(1)}, u32[]{:S(2)}, u32[]{:S(2)}) %collective-permute-start.11) | collective-permute-done | bytes 81952 | tf_op jit(solution)/shard_map/ppermute | solution.py:52
  29.2 1.9 %collective-permute-start.15 = (bf16[4,5120]{1,0:T(4,128)(2,1)S(1)}, bf16[4,5120]{1,0:T(4,128)(2,1)S(1)}, u32[]{:S(2)}, u32[]{:S(2)}) collective-permute-start(bf16[4,5120]{1,0:T(4,128)(2,1)S(1)} %residual_gradient.1.refs_4_.refs_0_), channel_id=1, source_target_pairs={{0,2},{2,0},{4,6},{6,4},{8,10},{10,8},{12,14},{14,12},{1,3},{3,1},... | collective-permute-start | bytes 122888 | tf_op jit(solution)/shard_map/ppermute | solution.py:52
  31.1 1.2 %collective-permute-start.14 = (bf16[4,5120]{1,0:T(4,128)(2,1)S(1)}, bf16[4,5120]{1,0:T(4,128)(2,1)S(1)}, u32[]{:S(2)}, u32[]{:S(2)}) collective-permute-start(bf16[4,5120]{1,0:T(4,128)(2,1)S(1)} %residual_gradient.1.refs_4_.refs_0_), channel_id=1, source_target_pairs={{0,6},{2,4},{4,2},{6,0},{8,14},{10,12},{12,10},{14,8},{1,7},{3,5},... | collective-permute-start | bytes 122888 | tf_op jit(solution)/shard_map/ppermute | solution.py:52
  33.1 0.5 %collective-permute-done.15.refs_3_ = bf16[4,5120]{1,0:T(4,128)(2,1)S(1)} collective-permute-done((bf16[4,5120]{1,0:T(4,128)(2,1)S(1)}, bf16[4,5120]{1,0:T(4,128)(2,1)S(1)}, u32[]{:S(2)}, u32[]{:S(2)}) %collective-permute-start.15) | collective-permute-done | bytes 40992 | tf_op jit(solution)/shard_map/ppermute | solution.py:52
  33.7 2.3 %collective-permute-done.14.refs_2_ = bf16[4,5120]{1,0:T(4,128)(2,1)S(1)} collective-permute-done((bf16[4,5120]{1,0:T(4,128)(2,1)S(1)}, bf16[4,5120]{1,0:T(4,128)(2,1)S(1)}, u32[]{:S(2)}, u32[]{:S(2)}) %collective-permute-start.14) | collective-permute-done | bytes 40992 | tf_op jit(solution)/shard_map/ppermute | solution.py:52
  36.5 0.8 %backward.1 = (bf16[16,256]{1,0:T(8,128)(2,1)S(1)}, f32[1,512]{1,0:T(1,128)S(1)}) custom-call(bf16[16,5120]{1,0:T(8,128)(2,1)S(1)} %stack.5.refs_0_.refs_2_, bf16[5120,512]{1,0:T(8,128)(2,1)S(1)} %turn.2.refs_4_.refs_1_, f32[16,256]{1,0:T(8,128)S(1)} %get-tuple-element.42.refs_0_.refs_2_, f32[16,256]{1,0:T(8,128)S(1)} %get-tuple-element.40.refs_3_), custom_call_target="tpu_custom_call" | custom-call | tf_op jit(solution)/shard_map/backward/pallas_call | solution.py:38
  37.3 0.8 %bias_product.1.refs_4_.refs_0_ = f32[1,5248]{1,0:T(1,128)S(1)} custom-call(f32[1,512]{1,0:T(1,128)S(1)} %get-tuple-element.44.refs_0_.refs_6_, bf16[512,5120]{1,0:T(8,128)(2,1)S(1)} %turn.3.refs_4_.refs_1_, f32[1,5120]{1,0:T(1,128)S(1)} %get-tuple-element.45.refs_2_, f32[1,128]{1,0:T(1,128)S(1)} %get-tuple-element.41.refs_4_.refs_3_, ...), custom_call_target="tpu_custom_call" | custom-call | tf_op jit(solution)/shard_map/bias_product/pallas_call | solution.py:38
  38.1 0.5 %collective-permute-start.17 = (f32[1,5248]{1,0:T(1,128)S(1)}, f32[1,5248]{1,0:T(1,128)S(1)}, u32[]{:S(2)}, u32[]{:S(2)}) collective-permute-start(f32[1,5248]{1,0:T(1,128)S(1)} %bias_product.1.refs_4_.refs_0_), channel_id=1, source_target_pairs={{0,1},{1,0},{2,3},{3,2},{4,5},{5,4},{6,7},{7,6},{8,9},{9,8},{10,11... | collective-permute-start | bytes 62984 | tf_op jit(solution)/shard_map/ppermute | solution.py:51
  38.6 0.9 %dec_gradient.1.refs_2_.refs_7_ = bf16[256,5120]{1,0:T(8,128)(2,1)S(1)} custom-call(f32[16,256]{1,0:T(8,128)S(1)} %get-tuple-element.42.refs_0_.refs_2_, f32[16,256]{1,0:T(8,128)S(1)} %collective-permute-done.12.refs_5_.refs_1_, bf16[16,5120]{1,0:T(8,128)(2,1)S(1)} %stack.5.refs_0_.refs_2_, bf16[16,5120]{1,0:T(8,128)(2,1)S(1)} %collective-permute-done.16.refs_3_, ...), custom_call_target="tpu_custom_call" | custom-call | flops 83886080 | tf_op jit(solution)/shard_map/dec_gradient/pallas_call | solution.py:38
  39.5 0.8 %collective-permute-start.20 = (f32[1,5248]{1,0:T(1,128)S(1)}, f32[1,5248]{1,0:T(1,128)S(1)}, u32[]{:S(2)}, u32[]{:S(2)}) collective-permute-start(f32[1,5248]{1,0:T(1,128)S(1)} %add.2.refs_9_.refs_0_), channel_id=1, source_target_pairs={{0,2},{2,0},{4,6},{6,4},{8,10},{10,8},{12,14},{14,12},{1,3},{3,1},... | collective-permute-start | bytes 62984 | tf_op jit(solution)/shard_map/ppermute | solution.py:52
  40.3 1.2 %collective-permute-start.19 = (f32[1,5248]{1,0:T(1,128)S(1)}, f32[1,5248]{1,0:T(1,128)S(1)}, u32[]{:S(2)}, u32[]{:S(2)}) collective-permute-start(f32[1,5248]{1,0:T(1,128)S(1)} %add.2.refs_9_.refs_0_), channel_id=1, source_target_pairs={{0,6},{2,4},{4,2},{6,0},{8,14},{10,12},{12,10},{14,8},{1,7},{3,5},... | collective-permute-start | bytes 62984 | tf_op jit(solution)/shard_map/ppermute | solution.py:52
  41.5 1.6 %collective-permute-start.18 = (f32[1,5248]{1,0:T(1,128)S(1)}, f32[1,5248]{1,0:T(1,128)S(1)}, u32[]{:S(2)}, u32[]{:S(2)}) collective-permute-start(f32[1,5248]{1,0:T(1,128)S(1)} %add.2.refs_9_.refs_0_), channel_id=1, source_target_pairs={{0,4},{2,6},{4,0},{6,2},{8,12},{10,14},{12,8},{14,10},{1,5},{3,7},... | collective-permute-start | bytes 62984 | tf_op jit(solution)/shard_map/ppermute | solution.py:52
  43.1 2.0 %enc_gradient.1 = (bf16[256,5120]{1,0:T(8,128)(2,1)}, bf16[2,5120]{1,0:T(2,128)(2,1)}, bf16[5120,256]{1,0:T(8,128)(2,1)S(1)}, f32[1,256]{1,0:T(1,128)S(1)}) custom-call(bf16[16,5120]{1,0:T(8,128)(2,1)S(1)} %get-tuple-element.35.refs_0_, bf16[16,5120]{1,0:T(8,128)(2,1)S(1)} %collective-permute-done.7.refs_6_.refs_1_, ...), custom_call_target="tpu_custom_call" | custom-call | flops 83886080 | bytes 5242880 | tf_op jit(solution)/shard_map/enc_gradient/pallas_call | solution.py:316
  45.3 3.4 %collective-permute-start.21 = (f32[1,5248]{1,0:T(1,128)S(1)}, f32[1,5248]{1,0:T(1,128)S(1)}, u32[]{:S(2)}, u32[]{:S(2)}) collective-permute-start(f32[1,5248]{1,0:T(1,128)S(1)} %add.3.refs_2_.terms_ref), channel_id=1, source_target_pairs={{0,8},{2,10},{4,12},{6,14},{8,0},{10,2},{12,4},{14,6},{1,9},{3,11}... | collective-permute-start | bytes 62984 | tf_op jit(solution)/shard_map/ppermute | solution.py:52
  48.7 1.5 %store.1 = (bf16[5120,256]{1,0:T(8,128)(2,1)}, f32[1,256]{1,0:T(1,128)}, f32[8,128]{1,0:T(8,128)S(1)}) custom-call(bf16[5120,256]{1,0:T(8,128)(2,1)S(1)} %get-tuple-element.48.refs_4_.refs_0_, f32[1,256]{1,0:T(1,128)S(1)} %get-tuple-element.49.refs_1_, f32[1,5248]{1,0:T(1,128)S(1)} %add.3.refs_2_.terms_ref), custom_call_target="tpu_custom_call" | custom-call | bytes 5244928 | tf_op jit(solution)/shard_map/store/pallas_call | solution.py:342
  50.5 0.6 %finish.1 = (f32[1,5120]{1,0:T(1,128)}, f32[1,1]{1,0:T(1,128)}) custom-call(f32[1,5248]{1,0:T(1,128)S(1)} %add.3.refs_2_.terms_ref, f32[1,5248]{1,0:T(1,128)S(1)} %collective-permute-done.21.other_ref, f32[8,128]{1,0:T(8,128)S(1)} %get-tuple-element.50.after_ref), custom_call_target="tpu_custom_call" | custom-call | tf_op jit(solution)/shard_map/finish/pallas_call | solution.py:374
  (34 shorter events, 3.3 us)
Async XLA Ops:
  0.6 14.1 %collective-permute-start.4 = (bf16[5120,256]{1,0:T(8,128)(2,1)}, bf16[5120,256]{1,0:T(8,128)(2,1)S(1)}, u32[]{:S(2)}, u32[]{:S(2)}) collective-permute-start(bf16[5120,256]{1,0:T(8,128)(2,1)} %refs_0_.2), channel_id=1, source_target_pairs={{0,1},{1,0},{2,3},{3,2},{4,5},{5,4},{6,7},{7,6},{8,9},{9,8},{10,11... | collective-permute-start | bytes 7864328 | tf_op jit(solution)/shard_map/ppermute | solution.py:51
  1.2 13.6 %collective-permute-start.6 = (bf16[256,5120]{1,0:T(8,128)(2,1)}, bf16[256,5120]{1,0:T(8,128)(2,1)S(1)}, u32[]{:S(2)}, u32[]{:S(2)}) collective-permute-start(bf16[256,5120]{1,0:T(8,128)(2,1)} %refs_0_.3), channel_id=1, source_target_pairs={{0,1},{1,0},{2,3},{3,2},{4,5},{5,4},{6,7},{7,6},{8,9},{9,8},{10,11... | collective-permute-start | bytes 7864328 | tf_op jit(solution)/shard_map/ppermute | solution.py:51
  1.2 6.0 %collective-permute-start = (bf16[2,5120]{1,0:T(2,128)(2,1)}, bf16[2,5120]{1,0:T(2,128)(2,1)S(1)}, u32[]{:S(2)}, u32[]{:S(2)}) collective-permute-start(bf16[2,5120]{1,0:T(2,128)(2,1)} %refs_1_.1), channel_id=1, source_target_pairs={{0,8},{2,10},{4,12},{6,14},{8,0},{10,2},{12,4},{14,6},{1,9},{3,11}... | collective-permute-start | bytes 61448 | tf_op jit(solution)/shard_map/ppermute | solution.py:52
  5.2 6.1 %copy-start = (f32[256]{0:T(256)S(1)}, f32[256]{0:T(256)}, u32[]{:S(2)}) copy-start(f32[256]{0:T(256)} %param.7) | copy-start | bytes 3076
  7.3 4.1 %collective-permute-start.3 = (bf16[4,5120]{1,0:T(4,128)(2,1)S(1)}, bf16[4,5120]{1,0:T(4,128)(2,1)S(1)}, u32[]{:S(2)}, u32[]{:S(2)}) collective-permute-start(bf16[4,5120]{1,0:T(4,128)(2,1)S(1)} %stack.3.refs_1_.refs_0_.refs_2_), channel_id=1, source_target_pairs={{0,2},{2,0},{4,6},{6,4},{8,10},{10,8},{12,14},{14,12},{1,3},{3,1},... | collective-permute-start | bytes 122888 | tf_op jit(solution)/shard_map/ppermute | solution.py:52
  9.2 4.9 %collective-permute-start.2 = (bf16[4,5120]{1,0:T(4,128)(2,1)S(1)}, bf16[4,5120]{1,0:T(4,128)(2,1)S(1)}, u32[]{:S(2)}, u32[]{:S(2)}) collective-permute-start(bf16[4,5120]{1,0:T(4,128)(2,1)S(1)} %stack.3.refs_1_.refs_0_.refs_2_), channel_id=1, source_target_pairs={{0,6},{2,4},{4,2},{6,0},{8,14},{10,12},{12,10},{14,8},{1,7},{3,5},... | collective-permute-start | bytes 122888 | tf_op jit(solution)/shard_map/ppermute | solution.py:52
  10.7 4.0 %collective-permute-start.1 = (bf16[4,5120]{1,0:T(4,128)(2,1)S(1)}, bf16[4,5120]{1,0:T(4,128)(2,1)S(1)}, u32[]{:S(2)}, u32[]{:S(2)}) collective-permute-start(bf16[4,5120]{1,0:T(4,128)(2,1)S(1)} %stack.3.refs_1_.refs_0_.refs_2_), channel_id=1, source_target_pairs={{0,4},{2,6},{4,0},{6,2},{8,12},{10,14},{12,8},{14,10},{1,5},{3,7},... | collective-permute-start | bytes 122888 | tf_op jit(solution)/shard_map/ppermute | solution.py:52
  11.3 3.4 %collective-permute-start.5 = (f32[1,256]{1,0:T(1,128)S(1)}, f32[1,256]{1,0:T(1,128)S(1)}, u32[]{:S(2)}, u32[]{:S(2)}) collective-permute-start(f32[1,256]{1,0:T(1,128)S(1)} %bitcast.7), channel_id=1, source_target_pairs={{0,1},{1,0},{2,3},{3,2},{4,5},{5,4},{6,7},{7,6},{8,9},{9,8},{10,11... | collective-permute-start | bytes 3080 | tf_op jit(solution)/shard_map/ppermute | solution.py:51
  16.3 5.0 %collective-permute-start.8 = (f32[4,5120]{1,0:T(4,128)S(1)}, f32[4,5120]{1,0:T(4,128)S(1)}, u32[]{:S(2)}, u32[]{:S(2)}) collective-permute-start(f32[4,5120]{1,0:T(4,128)S(1)} %get-tuple-element.37), channel_id=1, source_target_pairs={{0,4},{2,6},{4,0},{6,2},{8,12},{10,14},{12,8},{14,10},{1,5},{3,7},... | collective-permute-start | bytes 245768 | tf_op jit(solution)/shard_map/ppermute | solution.py:52
  17.3 4.6 %collective-permute-start.9 = (f32[4,5120]{1,0:T(4,128)S(1)}, f32[4,5120]{1,0:T(4,128)S(1)}, u32[]{:S(2)}, u32[]{:S(2)}) collective-permute-start(f32[4,5120]{1,0:T(4,128)S(1)} %get-tuple-element.38), channel_id=1, source_target_pairs={{0,2},{2,0},{4,6},{6,4},{8,10},{10,8},{12,14},{14,12},{1,3},{3,1},... | collective-permute-start | bytes 245768 | tf_op jit(solution)/shard_map/ppermute | solution.py:52
  18.3 5.3 %collective-permute-start.10 = (f32[4,5120]{1,0:T(4,128)S(1)}, f32[4,5120]{1,0:T(4,128)S(1)}, u32[]{:S(2)}, u32[]{:S(2)}) collective-permute-start(f32[4,5120]{1,0:T(4,128)S(1)} %get-tuple-element.39), channel_id=1, source_target_pairs={{0,6},{2,4},{4,2},{6,0},{8,14},{10,12},{12,10},{14,8},{1,7},{3,5},... | collective-permute-start | bytes 245768 | tf_op jit(solution)/shard_map/ppermute | solution.py:52
  19.9 9.2 %collective-permute-start.7 = (bf16[16,5120]{1,0:T(8,128)(2,1)S(1)}, bf16[16,5120]{1,0:T(8,128)(2,1)S(1)}, u32[]{:S(2)}, u32[]{:S(2)}) collective-permute-start(bf16[16,5120]{1,0:T(8,128)(2,1)S(1)} %get-tuple-element.35.refs_0_), channel_id=1, source_target_pairs={{0,1},{1,0},{2,3},{3,2},{4,5},{5,4},{6,7},{7,6},{8,9},{9,8},{10,11... | collective-permute-start | bytes 491528 | tf_op jit(solution)/shard_map/ppermute | solution.py:51
  23.7 5.4 %collective-permute-start.11 = (f32[4,5120]{1,0:T(4,128)S(1)}, f32[4,5120]{1,0:T(4,128)S(1)}, u32[]{:S(2)}, u32[]{:S(2)}) collective-permute-start(f32[4,5120]{1,0:T(4,128)S(1)} %add_parts.1.refs_2_.refs_0_), channel_id=1, source_target_pairs={{0,8},{2,10},{4,12},{6,14},{8,0},{10,2},{12,4},{14,6},{1,9},{3,11}... | collective-permute-start | bytes 245768 | tf_op jit(solution)/shard_map/ppermute | solution.py:52
  26.5 1.5 %collective-permute-start.12 = (f32[16,256]{1,0:T(8,128)S(1)}, f32[16,256]{1,0:T(8,128)S(1)}, u32[]{:S(2)}, u32[]{:S(2)}) collective-permute-start(f32[16,256]{1,0:T(8,128)S(1)} %get-tuple-element.40.refs_3_), channel_id=1, source_target_pairs={{0,1},{1,0},{2,3},{3,2},{4,5},{5,4},{6,7},{7,6},{8,9},{9,8},{10,11... | collective-permute-start | bytes 49160 | tf_op jit(solution)/shard_map/ppermute | solution.py:51
  29.2 4.5 %collective-permute-start.15 = (bf16[4,5120]{1,0:T(4,128)(2,1)S(1)}, bf16[4,5120]{1,0:T(4,128)(2,1)S(1)}, u32[]{:S(2)}, u32[]{:S(2)}) collective-permute-start(bf16[4,5120]{1,0:T(4,128)(2,1)S(1)} %residual_gradient.1.refs_4_.refs_0_), channel_id=1, source_target_pairs={{0,2},{2,0},{4,6},{6,4},{8,10},{10,8},{12,14},{14,12},{1,3},{3,1},... | collective-permute-start | bytes 122888 | tf_op jit(solution)/shard_map/ppermute | solution.py:52
  31.1 4.9 %collective-permute-start.14 = (bf16[4,5120]{1,0:T(4,128)(2,1)S(1)}, bf16[4,5120]{1,0:T(4,128)(2,1)S(1)}, u32[]{:S(2)}, u32[]{:S(2)}) collective-permute-start(bf16[4,5120]{1,0:T(4,128)(2,1)S(1)} %residual_gradient.1.refs_4_.refs_0_), channel_id=1, source_target_pairs={{0,6},{2,4},{4,2},{6,0},{8,14},{10,12},{12,10},{14,8},{1,7},{3,5},... | collective-permute-start | bytes 122888 | tf_op jit(solution)/shard_map/ppermute | solution.py:52
  32.3 4.0 %collective-permute-start.13 = (bf16[4,5120]{1,0:T(4,128)(2,1)S(1)}, bf16[4,5120]{1,0:T(4,128)(2,1)S(1)}, u32[]{:S(2)}, u32[]{:S(2)}) collective-permute-start(bf16[4,5120]{1,0:T(4,128)(2,1)S(1)} %residual_gradient.1.refs_4_.refs_0_), channel_id=1, source_target_pairs={{0,4},{2,6},{4,0},{6,2},{8,12},{10,14},{12,8},{14,10},{1,5},{3,7},... | collective-permute-start | bytes 122888 | tf_op jit(solution)/shard_map/ppermute | solution.py:52
  36.4 2.2 %collective-permute-start.16 = (bf16[16,5120]{1,0:T(8,128)(2,1)S(1)}, bf16[16,5120]{1,0:T(8,128)(2,1)S(1)}, u32[]{:S(2)}, u32[]{:S(2)}) collective-permute-start(bf16[16,5120]{1,0:T(8,128)(2,1)S(1)} %stack.5.refs_0_.refs_2_), channel_id=1, source_target_pairs={{0,1},{1,0},{2,3},{3,2},{4,5},{5,4},{6,7},{7,6},{8,9},{9,8},{10,11... | collective-permute-start | bytes 491528 | tf_op jit(solution)/shard_map/ppermute | solution.py:51
  38.1 1.4 %collective-permute-start.17 = (f32[1,5248]{1,0:T(1,128)S(1)}, f32[1,5248]{1,0:T(1,128)S(1)}, u32[]{:S(2)}, u32[]{:S(2)}) collective-permute-start(f32[1,5248]{1,0:T(1,128)S(1)} %bias_product.1.refs_4_.refs_0_), channel_id=1, source_target_pairs={{0,1},{1,0},{2,3},{3,2},{4,5},{5,4},{6,7},{7,6},{8,9},{9,8},{10,11... | collective-permute-start | bytes 62984 | tf_op jit(solution)/shard_map/ppermute | solution.py:51
  39.5 5.5 %collective-permute-start.20 = (f32[1,5248]{1,0:T(1,128)S(1)}, f32[1,5248]{1,0:T(1,128)S(1)}, u32[]{:S(2)}, u32[]{:S(2)}) collective-permute-start(f32[1,5248]{1,0:T(1,128)S(1)} %add.2.refs_9_.refs_0_), channel_id=1, source_target_pairs={{0,2},{2,0},{4,6},{6,4},{8,10},{10,8},{12,14},{14,12},{1,3},{3,1},... | collective-permute-start | bytes 62984 | tf_op jit(solution)/shard_map/ppermute | solution.py:52
  40.3 4.8 %collective-permute-start.19 = (f32[1,5248]{1,0:T(1,128)S(1)}, f32[1,5248]{1,0:T(1,128)S(1)}, u32[]{:S(2)}, u32[]{:S(2)}) collective-permute-start(f32[1,5248]{1,0:T(1,128)S(1)} %add.2.refs_9_.refs_0_), channel_id=1, source_target_pairs={{0,6},{2,4},{4,2},{6,0},{8,14},{10,12},{12,10},{14,8},{1,7},{3,5},... | collective-permute-start | bytes 62984 | tf_op jit(solution)/shard_map/ppermute | solution.py:52
  41.5 3.8 %collective-permute-start.18 = (f32[1,5248]{1,0:T(1,128)S(1)}, f32[1,5248]{1,0:T(1,128)S(1)}, u32[]{:S(2)}, u32[]{:S(2)}) collective-permute-start(f32[1,5248]{1,0:T(1,128)S(1)} %add.2.refs_9_.refs_0_), channel_id=1, source_target_pairs={{0,4},{2,6},{4,0},{6,2},{8,12},{10,14},{12,8},{14,10},{1,5},{3,7},... | collective-permute-start | bytes 62984 | tf_op jit(solution)/shard_map/ppermute | solution.py:52
  45.3 5.2 %collective-permute-start.21 = (f32[1,5248]{1,0:T(1,128)S(1)}, f32[1,5248]{1,0:T(1,128)S(1)}, u32[]{:S(2)}, u32[]{:S(2)}) collective-permute-start(f32[1,5248]{1,0:T(1,128)S(1)} %add.3.refs_2_.terms_ref), channel_id=1, source_target_pairs={{0,8},{2,10},{4,12},{6,14},{8,0},{10,2},{12,4},{14,6},{1,9},{3,11}... | collective-permute-start | bytes 62984 | tf_op jit(solution)/shard_map/ppermute | solution.py:52

commit v9 on v8

--- a/solution.py
+++ b/solution.py
@@ -389,10 +389,11 @@
 
     enc_bias = enc_bias.reshape(1, -1)
     other = swap(residuals, far)
-    siblings = swap(enc_weight, CORES), swap(enc_bias, CORES), swap(dec_weight, CORES)
-    enc_vmem, own, dec_bias_row, enc_bias_row = load([enc_weight, residuals, dec_bias.reshape(1, width), enc_bias])
+    enc_sibling, dec_sibling = swap(enc_weight, CORES), swap(dec_weight, CORES)
+    enc_vmem, own, dec_bias_row = load([enc_weight, residuals, dec_bias.reshape(1, width)])
     paired = stack([own, other], after=[enc_vmem])
-    (dec_vmem,) = load([dec_weight], after=[paired])
+    dec_vmem, enc_bias_row = load([dec_weight, enc_bias], after=[paired])
+    siblings = enc_sibling, swap(enc_bias_row, CORES), dec_sibling
     rows = gather(paired, steps, ROWS_ORDER, after=[dec_vmem])
     centered_a, active_a, active_sibling, *parts = encode_decode(
         rows, [(enc_vmem, enc_bias_row, dec_vmem), siblings], dec_bias_row, len(steps[-1]) + 1

time: 51.3 us -> 52.1 us (1.016)
  waiting for transfers between devices: 9.49 us -> 11.4 us
  starting transfers between devices: 25.6 us -> 24.5 us
    ppermute x15, waiting for transfers between devices: 9.48 us -> 11.4 us  [swap(): lax.ppermute(values, 'lat', [(i, i ^ mask) for i in range(lax.axis_size('...]
    ppermute x15, starting transfers between devices: 24.4 us -> 23.2 us  [swap(): lax.ppermute(values, 'lat', [(i, i ^ mask) for i in range(lax.axis_size('...]
where the time goes in v9:
time: 52.1 us; the launch traced here: 51.9 us
  starting transfers between devices  24.5 us (47%)
  Pallas kernels  15.2 us (29%)
  waiting for transfers between devices  11.4 us (22%)
  between operations  0.83 us (2%)
    ppermute x15, starting transfers between devices, swap(): lax.ppermute(values, 'lat', [(i, i ^ mask) for i in range(lax.axis_size('...  23.2 us
    ppermute x15, waiting for transfers between devices, swap(): lax.ppermute(values, 'lat', [(i, i ^ mask) for i in range(lax.axis_size('...  11.4 us
    pallas_call x15, Pallas kernels, run(): pl.pallas_call(body, out_shape=[vmem(*out) for out in outs], in_specs=[VM...  7.57 us
    pallas_call x2, Pallas kernels, load(): pl.pallas_call(kernel, out_shape=[vmem(array.shape, array.dtype) for arra...  3.53 us
    pallas_call x1, Pallas kernels, enc_gradient(): pl.pallas_call(kernel, out_shape=[jax.ShapeDtypeStruct(a.shape, a.dtype)...  1.96 us
    pallas_call x1, Pallas kernels, store(): pl.pallas_call(kernel, out_shape=[jax.ShapeDtypeStruct(a.shape, a.dtype)...  1.51 us
    ppermute x7, starting transfers between devices, swap(): return lax.ppermute(values, 'sub', [(i, i ^ 1) for i in range(2)])  1.28 us
  transfers between devices with their start and end apart: 22, of which 12 were waited for; matrix products, arithmetic and copies ran while one was open for 0% of the time, Pallas kernels for 25%

profile of v9, /device:TPU:0, one launch (start us, length us, event | category | flops | bytes accessed | tf_op | source)
XLA Modules:
  0.0 51.9 jit_solution(14270192147598430400)
XLA Ops:
  1.2 4.0 %collective-permute-start = (bf16[2,5120]{1,0:T(2,128)(2,1)}, bf16[2,5120]{1,0:T(2,128)(2,1)S(1)}, u32[]{:S(2)}, u32[]{:S(2)}) collective-permute-start(bf16[2,5120]{1,0:T(2,128)(2,1)} %refs_1_.1), channel_id=1, source_target_pairs={{0,8},{2,10},{4,12},{6,14},{8,0},{10,2},{12,4},{14,6},{1,9},{3,11}... | collective-permute-start | bytes 61448 | tf_op jit(solution)/shard_map/ppermute | solution.py:52
  5.2 1.8 %load.2 = (bf16[5120,256]{1,0:T(8,128)(2,1)S(1)}, bf16[2,5120]{1,0:T(2,128)(2,1)S(1)}, f32[1,5120]{1,0:T(1,128)S(1)}) custom-call(bf16[5120,256]{1,0:T(8,128)(2,1)} %refs_0_.2, bf16[2,5120]{1,0:T(2,128)(2,1)} %refs_1_.1, f32[1,5120]{1,0:T(1,128)} %bitcast.5), custom_call_target="tpu_custom_call" | custom-call | bytes 5324800 | tf_op jit(solution)/shard_map/load/pallas_call | solution.py:77
  7.3 1.9 %collective-permute-start.3 = (bf16[4,5120]{1,0:T(4,128)(2,1)S(1)}, bf16[4,5120]{1,0:T(4,128)(2,1)S(1)}, u32[]{:S(2)}, u32[]{:S(2)}) collective-permute-start(bf16[4,5120]{1,0:T(4,128)(2,1)S(1)} %stack.3.refs_2_.refs_0_), channel_id=1, source_target_pairs={{0,2},{2,0},{4,6},{6,4},{8,10},{10,8},{12,14},{14,12},{1,3},{3,1},... | collective-permute-start | bytes 122888 | tf_op jit(solution)/shard_map/ppermute | solution.py:52
  9.2 1.5 %collective-permute-start.2 = (bf16[4,5120]{1,0:T(4,128)(2,1)S(1)}, bf16[4,5120]{1,0:T(4,128)(2,1)S(1)}, u32[]{:S(2)}, u32[]{:S(2)}) collective-permute-start(bf16[4,5120]{1,0:T(4,128)(2,1)S(1)} %stack.3.refs_2_.refs_0_), channel_id=1, source_target_pairs={{0,6},{2,4},{4,2},{6,0},{8,14},{10,12},{12,10},{14,8},{1,7},{3,5},... | collective-permute-start | bytes 122888 | tf_op jit(solution)/shard_map/ppermute | solution.py:52
  10.8 1.8 %load.3 = (bf16[256,5120]{1,0:T(8,128)(2,1)S(1)}, f32[1,256]{1,0:T(1,128)S(1)}) custom-call(bf16[256,5120]{1,0:T(8,128)(2,1)} %refs_0_.3, f32[1,256]{1,0:T(1,128)} %bitcast.6, bf16[4,5120]{1,0:T(4,128)(2,1)S(1)} %stack.3.refs_2_.refs_0_), custom_call_target="tpu_custom_call" | custom-call | bytes 5244928 | tf_op jit(solution)/shard_map/load/pallas_call | solution.py:77
  12.7 1.4 %collective-permute-done.2.refs_2_ = bf16[4,5120]{1,0:T(4,128)(2,1)S(1)} collective-permute-done((bf16[4,5120]{1,0:T(4,128)(2,1)S(1)}, bf16[4,5120]{1,0:T(4,128)(2,1)S(1)}, u32[]{:S(2)}, u32[]{:S(2)}) %collective-permute-start.2) | collective-permute-done | bytes 40992 | tf_op jit(solution)/shard_map/ppermute | solution.py:52
  14.1 0.6 %collective-permute-done.1.refs_1_ = bf16[4,5120]{1,0:T(4,128)(2,1)S(1)} collective-permute-done((bf16[4,5120]{1,0:T(4,128)(2,1)S(1)}, bf16[4,5120]{1,0:T(4,128)(2,1)S(1)}, u32[]{:S(2)}, u32[]{:S(2)}) %collective-permute-start.1) | collective-permute-done | bytes 40992 | tf_op jit(solution)/shard_map/ppermute | solution.py:52
  14.8 1.6 %encode_decode.1 = (bf16[16,5120]{1,0:T(8,128)(2,1)S(1)}, f32[16,256]{1,0:T(8,128)S(1)}, f32[16,256]{1,0:T(8,128)S(1)}, f32[4,5120]{1,0:T(4,128)S(1)}, f32[4,512...) custom-call(bf16[16,5120]{1,0:T(8,128)(2,1)S(1)} %stack.4.refs_0_, ...), custom_call_target="tpu_custom_call" | custom-call | flops 167772160 | tf_op jit(solution)/shard_map/encode_decode/pallas_call | solution.py:38
  16.3 1.0 %collective-permute-start.8 = (f32[4,5120]{1,0:T(4,128)S(1)}, f32[4,5120]{1,0:T(4,128)S(1)}, u32[]{:S(2)}, u32[]{:S(2)}) collective-permute-start(f32[4,5120]{1,0:T(4,128)S(1)} %get-tuple-element.39), channel_id=1, source_target_pairs={{0,4},{2,6},{4,0},{6,2},{8,12},{10,14},{12,8},{14,10},{1,5},{3,7},... | collective-permute-start | bytes 245768 | tf_op jit(solution)/shard_map/ppermute | solution.py:52
  17.3 1.5 %collective-permute-start.9 = (f32[4,5120]{1,0:T(4,128)S(1)}, f32[4,5120]{1,0:T(4,128)S(1)}, u32[]{:S(2)}, u32[]{:S(2)}) collective-permute-start(f32[4,5120]{1,0:T(4,128)S(1)} %get-tuple-element.40), channel_id=1, source_target_pairs={{0,2},{2,0},{4,6},{6,4},{8,10},{10,8},{12,14},{14,12},{1,3},{3,1},... | collective-permute-start | bytes 245768 | tf_op jit(solution)/shard_map/ppermute | solution.py:52
  18.8 1.1 %collective-permute-start.10 = (f32[4,5120]{1,0:T(4,128)S(1)}, f32[4,5120]{1,0:T(4,128)S(1)}, u32[]{:S(2)}, u32[]{:S(2)}) collective-permute-start(f32[4,5120]{1,0:T(4,128)S(1)} %get-tuple-element.41), channel_id=1, source_target_pairs={{0,6},{2,4},{4,2},{6,0},{8,14},{10,12},{12,10},{14,8},{1,7},{3,5},... | collective-permute-start | bytes 245768 | tf_op jit(solution)/shard_map/ppermute | solution.py:52
  19.9 1.4 %turn.2.refs_4_.refs_1_ = bf16[5120,512]{1,0:T(8,128)(2,1)S(1)} custom-call(bf16[256,5120]{1,0:T(8,128)(2,1)S(1)} %get-tuple-element.34.refs_4_.refs_0_, bf16[256,5120]{1,0:T(8,128)(2,1)S(1)} %collective-permute-done.6.refs_7_.refs_1_, f32[4,5120]{1,0:T(4,128)S(1)} %get-tuple-element.38.refs_2_.refs_0_), custom_call_target="tpu_custom_call" | custom-call | bytes 10485760 | tf_op jit(solution)/shard_map/turn/pallas_call | solution.py:38
  21.3 1.2 %collective-permute-done.9.refs_2_ = f32[4,5120]{1,0:T(4,128)S(1)} collective-permute-done((f32[4,5120]{1,0:T(4,128)S(1)}, f32[4,5120]{1,0:T(4,128)S(1)}, u32[]{:S(2)}, u32[]{:S(2)}) %collective-permute-start.9) | collective-permute-done | bytes 81952 | tf_op jit(solution)/shard_map/ppermute | solution.py:52
  22.5 1.6 %collective-permute-done.10.refs_3_ = f32[4,5120]{1,0:T(4,128)S(1)} collective-permute-done((f32[4,5120]{1,0:T(4,128)S(1)}, f32[4,5120]{1,0:T(4,128)S(1)}, u32[]{:S(2)}, u32[]{:S(2)}) %collective-permute-start.10) | collective-permute-done | bytes 81952 | tf_op jit(solution)/shard_map/ppermute | solution.py:52
  24.1 2.8 %collective-permute-start.11 = (f32[4,5120]{1,0:T(4,128)S(1)}, f32[4,5120]{1,0:T(4,128)S(1)}, u32[]{:S(2)}, u32[]{:S(2)}) collective-permute-start(f32[4,5120]{1,0:T(4,128)S(1)} %add_parts.1.refs_2_.refs_0_), channel_id=1, source_target_pairs={{0,8},{2,10},{4,12},{6,14},{8,0},{10,2},{12,4},{14,6},{1,9},{3,11}... | collective-permute-start | bytes 245768 | tf_op jit(solution)/shard_map/ppermute | solution.py:52
  26.9 1.5 %turn.3.refs_4_.refs_1_ = bf16[512,5120]{1,0:T(8,128)(2,1)S(1)} custom-call(bf16[5120,256]{1,0:T(8,128)(2,1)S(1)} %get-tuple-element.33.refs_2_.refs_0_, bf16[5120,256]{1,0:T(8,128)(2,1)S(1)} %collective-permute-done.4.refs_5_.refs_1_, f32[4,5120]{1,0:T(4,128)S(1)} %add_parts.1.refs_2_.refs_0_), custom_call_target="tpu_custom_call" | custom-call | bytes 10485760 | tf_op jit(solution)/shard_map/turn/pallas_call | solution.py:38
  28.4 2.0 %collective-permute-done.11.refs_1_ = f32[4,5120]{1,0:T(4,128)S(1)} collective-permute-done((f32[4,5120]{1,0:T(4,128)S(1)}, f32[4,5120]{1,0:T(4,128)S(1)}, u32[]{:S(2)}, u32[]{:S(2)}) %collective-permute-start.11) | collective-permute-done | bytes 81952 | tf_op jit(solution)/shard_map/ppermute | solution.py:52
  30.5 0.9 %collective-permute-start.15 = (bf16[4,5120]{1,0:T(4,128)(2,1)S(1)}, bf16[4,5120]{1,0:T(4,128)(2,1)S(1)}, u32[]{:S(2)}, u32[]{:S(2)}) collective-permute-start(bf16[4,5120]{1,0:T(4,128)(2,1)S(1)} %residual_gradient.1.refs_4_.refs_0_), channel_id=1, source_target_pairs={{0,2},{2,0},{4,6},{6,4},{8,10},{10,8},{12,14},{14,12},{1,3},{3,1},... | collective-permute-start | bytes 122888 | tf_op jit(solution)/shard_map/ppermute | solution.py:52
  31.4 1.1 %collective-permute-start.14 = (bf16[4,5120]{1,0:T(4,128)(2,1)S(1)}, bf16[4,5120]{1,0:T(4,128)(2,1)S(1)}, u32[]{:S(2)}, u32[]{:S(2)}) collective-permute-start(bf16[4,5120]{1,0:T(4,128)(2,1)S(1)} %residual_gradient.1.refs_4_.refs_0_), channel_id=1, source_target_pairs={{0,6},{2,4},{4,2},{6,0},{8,14},{10,12},{12,10},{14,8},{1,7},{3,5},... | collective-permute-start | bytes 122888 | tf_op jit(solution)/shard_map/ppermute | solution.py:52
  32.5 1.6 %collective-permute-start.13 = (bf16[4,5120]{1,0:T(4,128)(2,1)S(1)}, bf16[4,5120]{1,0:T(4,128)(2,1)S(1)}, u32[]{:S(2)}, u32[]{:S(2)}) collective-permute-start(bf16[4,5120]{1,0:T(4,128)(2,1)S(1)} %residual_gradient.1.refs_4_.refs_0_), channel_id=1, source_target_pairs={{0,4},{2,6},{4,0},{6,2},{8,12},{10,14},{12,8},{14,10},{1,5},{3,7},... | collective-permute-start | bytes 122888 | tf_op jit(solution)/shard_map/ppermute | solution.py:52
  34.6 1.8 %collective-permute-done.14.refs_2_ = bf16[4,5120]{1,0:T(4,128)(2,1)S(1)} collective-permute-done((bf16[4,5120]{1,0:T(4,128)(2,1)S(1)}, bf16[4,5120]{1,0:T(4,128)(2,1)S(1)}, u32[]{:S(2)}, u32[]{:S(2)}) %collective-permute-start.14) | collective-permute-done | bytes 40992 | tf_op jit(solution)/shard_map/ppermute | solution.py:52
  36.6 0.8 %backward.1 = (bf16[16,256]{1,0:T(8,128)(2,1)S(1)}, f32[1,512]{1,0:T(1,128)S(1)}) custom-call(bf16[16,5120]{1,0:T(8,128)(2,1)S(1)} %stack.5.refs_0_.refs_2_, bf16[5120,512]{1,0:T(8,128)(2,1)S(1)} %turn.2.refs_4_.refs_1_, f32[16,256]{1,0:T(8,128)S(1)} %get-tuple-element.44.refs_0_.refs_2_, f32[16,256]{1,0:T(8,128)S(1)} %get-tuple-element.42.refs_3_), custom_call_target="tpu_custom_call" | custom-call | tf_op jit(solution)/shard_map/backward/pallas_call | solution.py:38
  37.4 0.8 %bias_product.1.refs_4_.refs_0_ = f32[1,5248]{1,0:T(1,128)S(1)} custom-call(f32[1,512]{1,0:T(1,128)S(1)} %get-tuple-element.46.refs_0_.refs_6_, bf16[512,5120]{1,0:T(8,128)(2,1)S(1)} %turn.3.refs_4_.refs_1_, f32[1,5120]{1,0:T(1,128)S(1)} %get-tuple-element.47.refs_2_, f32[1,128]{1,0:T(1,128)S(1)} %get-tuple-element.43.refs_4_.refs_3_, ...), custom_call_target="tpu_custom_call" | custom-call | tf_op jit(solution)/shard_map/bias_product/pallas_call | solution.py:38
  38.8 0.9 %dec_gradient.1.refs_2_.refs_7_ = bf16[256,5120]{1,0:T(8,128)(2,1)S(1)} custom-call(f32[16,256]{1,0:T(8,128)S(1)} %get-tuple-element.44.refs_0_.refs_2_, f32[16,256]{1,0:T(8,128)S(1)} %collective-permute-done.12.refs_5_.refs_1_, bf16[16,5120]{1,0:T(8,128)(2,1)S(1)} %stack.5.refs_0_.refs_2_, bf16[16,5120]{1,0:T(8,128)(2,1)S(1)} %collective-permute-done.16.refs_3_, ...), custom_call_target="tpu_custom_call" | custom-call | flops 83886080 | tf_op jit(solution)/shard_map/dec_gradient/pallas_call | solution.py:38
  39.7 1.1 %collective-permute-start.20 = (f32[1,5248]{1,0:T(1,128)S(1)}, f32[1,5248]{1,0:T(1,128)S(1)}, u32[]{:S(2)}, u32[]{:S(2)}) collective-permute-start(f32[1,5248]{1,0:T(1,128)S(1)} %add.2.refs_9_.refs_0_), channel_id=1, source_target_pairs={{0,2},{2,0},{4,6},{6,4},{8,10},{10,8},{12,14},{14,12},{1,3},{3,1},... | collective-permute-start | bytes 62984 | tf_op jit(solution)/shard_map/ppermute | solution.py:52
  40.7 2.0 %collective-permute-start.19 = (f32[1,5248]{1,0:T(1,128)S(1)}, f32[1,5248]{1,0:T(1,128)S(1)}, u32[]{:S(2)}, u32[]{:S(2)}) collective-permute-start(f32[1,5248]{1,0:T(1,128)S(1)} %add.2.refs_9_.refs_0_), channel_id=1, source_target_pairs={{0,6},{2,4},{4,2},{6,0},{8,14},{10,12},{12,10},{14,8},{1,7},{3,5},... | collective-permute-start | bytes 62984 | tf_op jit(solution)/shard_map/ppermute | solution.py:52
  43.2 2.0 %enc_gradient.1 = (bf16[256,5120]{1,0:T(8,128)(2,1)}, bf16[2,5120]{1,0:T(2,128)(2,1)}, bf16[5120,256]{1,0:T(8,128)(2,1)S(1)}, f32[1,256]{1,0:T(1,128)S(1)}) custom-call(bf16[16,5120]{1,0:T(8,128)(2,1)S(1)} %get-tuple-element.37.refs_0_, bf16[16,5120]{1,0:T(8,128)(2,1)S(1)} %collective-permute-done.7.refs_6_.refs_1_, ...), custom_call_target="tpu_custom_call" | custom-call | flops 83886080 | bytes 5242880 | tf_op jit(solution)/shard_map/enc_gradient/pallas_call | solution.py:316
  45.5 1.0 %collective-permute-done.18.refs_1_ = f32[1,5248]{1,0:T(1,128)S(1)} collective-permute-done((f32[1,5248]{1,0:T(1,128)S(1)}, f32[1,5248]{1,0:T(1,128)S(1)}, u32[]{:S(2)}, u32[]{:S(2)}) %collective-permute-start.18) | collective-permute-done | bytes 21024 | tf_op jit(solution)/shard_map/ppermute | solution.py:52
  46.6 2.3 %collective-permute-start.21 = (f32[1,5248]{1,0:T(1,128)S(1)}, f32[1,5248]{1,0:T(1,128)S(1)}, u32[]{:S(2)}, u32[]{:S(2)}) collective-permute-start(f32[1,5248]{1,0:T(1,128)S(1)} %add.3.refs_2_.terms_ref), channel_id=1, source_target_pairs={{0,8},{2,10},{4,12},{6,14},{8,0},{10,2},{12,4},{14,6},{1,9},{3,11}... | collective-permute-start | bytes 62984 | tf_op jit(solution)/shard_map/ppermute | solution.py:52
  48.8 1.5 %store.1 = (bf16[5120,256]{1,0:T(8,128)(2,1)}, f32[1,256]{1,0:T(1,128)}, f32[8,128]{1,0:T(8,128)S(1)}) custom-call(bf16[5120,256]{1,0:T(8,128)(2,1)S(1)} %get-tuple-element.50.refs_4_.refs_0_, f32[1,256]{1,0:T(1,128)S(1)} %get-tuple-element.51.refs_1_, f32[1,5248]{1,0:T(1,128)S(1)} %add.3.refs_2_.terms_ref), custom_call_target="tpu_custom_call" | custom-call | bytes 5244928 | tf_op jit(solution)/shard_map/store/pallas_call | solution.py:342
  50.4 1.0 %collective-permute-done.21.other_ref = f32[1,5248]{1,0:T(1,128)S(1)} collective-permute-done((f32[1,5248]{1,0:T(1,128)S(1)}, f32[1,5248]{1,0:T(1,128)S(1)}, u32[]{:S(2)}, u32[]{:S(2)}) %collective-permute-start.21) | collective-permute-done | bytes 21024 | tf_op jit(solution)/shard_map/ppermute | solution.py:52
  51.3 0.6 %finish.1 = (f32[1,5120]{1,0:T(1,128)}, f32[1,1]{1,0:T(1,128)}) custom-call(f32[1,5248]{1,0:T(1,128)S(1)} %add.3.refs_2_.terms_ref, f32[1,5248]{1,0:T(1,128)S(1)} %collective-permute-done.21.other_ref, f32[8,128]{1,0:T(8,128)S(1)} %get-tuple-element.52.after_ref), custom_call_target="tpu_custom_call" | custom-call | tf_op jit(solution)/shard_map/finish/pallas_call | solution.py:374
  (32 shorter events, 3.3 us)
Async XLA Ops:
  0.6 14.1 %collective-permute-start.4 = (bf16[5120,256]{1,0:T(8,128)(2,1)}, bf16[5120,256]{1,0:T(8,128)(2,1)S(1)}, u32[]{:S(2)}, u32[]{:S(2)}) collective-permute-start(bf16[5120,256]{1,0:T(8,128)(2,1)} %refs_0_.2), channel_id=1, source_target_pairs={{0,1},{1,0},{2,3},{3,2},{4,5},{5,4},{6,7},{7,6},{8,9},{9,8},{10,11... | collective-permute-start | bytes 7864328 | tf_op jit(solution)/shard_map/ppermute | solution.py:51
  1.1 13.6 %collective-permute-start.6 = (bf16[256,5120]{1,0:T(8,128)(2,1)}, bf16[256,5120]{1,0:T(8,128)(2,1)S(1)}, u32[]{:S(2)}, u32[]{:S(2)}) collective-permute-start(bf16[256,5120]{1,0:T(8,128)(2,1)} %refs_0_.3), channel_id=1, source_target_pairs={{0,1},{1,0},{2,3},{3,2},{4,5},{5,4},{6,7},{7,6},{8,9},{9,8},{10,11... | collective-permute-start | bytes 7864328 | tf_op jit(solution)/shard_map/ppermute | solution.py:51
  1.2 6.0 %collective-permute-start = (bf16[2,5120]{1,0:T(2,128)(2,1)}, bf16[2,5120]{1,0:T(2,128)(2,1)S(1)}, u32[]{:S(2)}, u32[]{:S(2)}) collective-permute-start(bf16[2,5120]{1,0:T(2,128)(2,1)} %refs_1_.1), channel_id=1, source_target_pairs={{0,8},{2,10},{4,12},{6,14},{8,0},{10,2},{12,4},{14,6},{1,9},{3,11}... | collective-permute-start | bytes 61448 | tf_op jit(solution)/shard_map/ppermute | solution.py:52
  7.3 5.3 %collective-permute-start.3 = (bf16[4,5120]{1,0:T(4,128)(2,1)S(1)}, bf16[4,5120]{1,0:T(4,128)(2,1)S(1)}, u32[]{:S(2)}, u32[]{:S(2)}) collective-permute-start(bf16[4,5120]{1,0:T(4,128)(2,1)S(1)} %stack.3.refs_2_.refs_0_), channel_id=1, source_target_pairs={{0,2},{2,0},{4,6},{6,4},{8,10},{10,8},{12,14},{14,12},{1,3},{3,1},... | collective-permute-start | bytes 122888 | tf_op jit(solution)/shard_map/ppermute | solution.py:52
  9.2 4.9 %collective-permute-start.2 = (bf16[4,5120]{1,0:T(4,128)(2,1)S(1)}, bf16[4,5120]{1,0:T(4,128)(2,1)S(1)}, u32[]{:S(2)}, u32[]{:S(2)}) collective-permute-start(bf16[4,5120]{1,0:T(4,128)(2,1)S(1)} %stack.3.refs_2_.refs_0_), channel_id=1, source_target_pairs={{0,6},{2,4},{4,2},{6,0},{8,14},{10,12},{12,10},{14,8},{1,7},{3,5},... | collective-permute-start | bytes 122888 | tf_op jit(solution)/shard_map/ppermute | solution.py:52
  10.7 4.0 %collective-permute-start.1 = (bf16[4,5120]{1,0:T(4,128)(2,1)S(1)}, bf16[4,5120]{1,0:T(4,128)(2,1)S(1)}, u32[]{:S(2)}, u32[]{:S(2)}) collective-permute-start(bf16[4,5120]{1,0:T(4,128)(2,1)S(1)} %stack.3.refs_2_.refs_0_), channel_id=1, source_target_pairs={{0,4},{2,6},{4,0},{6,2},{8,12},{10,14},{12,8},{14,10},{1,5},{3,7},... | collective-permute-start | bytes 122888 | tf_op jit(solution)/shard_map/ppermute | solution.py:52
  12.6 2.2 %collective-permute-start.5 = (f32[1,256]{1,0:T(1,128)S(1)}, f32[1,256]{1,0:T(1,128)S(1)}, u32[]{:S(2)}, u32[]{:S(2)}) collective-permute-start(f32[1,256]{1,0:T(1,128)S(1)} %get-tuple-element.36.refs_3_), channel_id=1, source_target_pairs={{0,1},{1,0},{2,3},{3,2},{4,5},{5,4},{6,7},{7,6},{8,9},{9,8},{10,11... | collective-permute-start | bytes 3080 | tf_op jit(solution)/shard_map/ppermute | solution.py:51
  16.3 5.0 %collective-permute-start.8 = (f32[4,5120]{1,0:T(4,128)S(1)}, f32[4,5120]{1,0:T(4,128)S(1)}, u32[]{:S(2)}, u32[]{:S(2)}) collective-permute-start(f32[4,5120]{1,0:T(4,128)S(1)} %get-tuple-element.39), channel_id=1, source_target_pairs={{0,4},{2,6},{4,0},{6,2},{8,12},{10,14},{12,8},{14,10},{1,5},{3,7},... | collective-permute-start | bytes 245768 | tf_op jit(solution)/shard_map/ppermute | solution.py:52
  17.3 5.2 %collective-permute-start.9 = (f32[4,5120]{1,0:T(4,128)S(1)}, f32[4,5120]{1,0:T(4,128)S(1)}, u32[]{:S(2)}, u32[]{:S(2)}) collective-permute-start(f32[4,5120]{1,0:T(4,128)S(1)} %get-tuple-element.40), channel_id=1, source_target_pairs={{0,2},{2,0},{4,6},{6,4},{8,10},{10,8},{12,14},{14,12},{1,3},{3,1},... | collective-permute-start | bytes 245768 | tf_op jit(solution)/shard_map/ppermute | solution.py:52
  18.8 5.3 %collective-permute-start.10 = (f32[4,5120]{1,0:T(4,128)S(1)}, f32[4,5120]{1,0:T(4,128)S(1)}, u32[]{:S(2)}, u32[]{:S(2)}) collective-permute-start(f32[4,5120]{1,0:T(4,128)S(1)} %get-tuple-element.41), channel_id=1, source_target_pairs={{0,6},{2,4},{4,2},{6,0},{8,14},{10,12},{12,10},{14,8},{1,7},{3,5},... | collective-permute-start | bytes 245768 | tf_op jit(solution)/shard_map/ppermute | solution.py:52
  19.9 10.6 %collective-permute-start.7 = (bf16[16,5120]{1,0:T(8,128)(2,1)S(1)}, bf16[16,5120]{1,0:T(8,128)(2,1)S(1)}, u32[]{:S(2)}, u32[]{:S(2)}) collective-permute-start(bf16[16,5120]{1,0:T(8,128)(2,1)S(1)} %get-tuple-element.37.refs_0_), channel_id=1, source_target_pairs={{0,1},{1,0},{2,3},{3,2},{4,5},{5,4},{6,7},{7,6},{8,9},{9,8},{10,11... | collective-permute-start | bytes 491528 | tf_op jit(solution)/shard_map/ppermute | solution.py:51
  24.1 6.3 %collective-permute-start.11 = (f32[4,5120]{1,0:T(4,128)S(1)}, f32[4,5120]{1,0:T(4,128)S(1)}, u32[]{:S(2)}, u32[]{:S(2)}) collective-permute-start(f32[4,5120]{1,0:T(4,128)S(1)} %add_parts.1.refs_2_.refs_0_), channel_id=1, source_target_pairs={{0,8},{2,10},{4,12},{6,14},{8,0},{10,2},{12,4},{14,6},{1,9},{3,11}... | collective-permute-start | bytes 245768 | tf_op jit(solution)/shard_map/ppermute | solution.py:52
  26.9 1.5 %collective-permute-start.12 = (f32[16,256]{1,0:T(8,128)S(1)}, f32[16,256]{1,0:T(8,128)S(1)}, u32[]{:S(2)}, u32[]{:S(2)}) collective-permute-start(f32[16,256]{1,0:T(8,128)S(1)} %get-tuple-element.42.refs_3_), channel_id=1, source_target_pairs={{0,1},{1,0},{2,3},{3,2},{4,5},{5,4},{6,7},{7,6},{8,9},{9,8},{10,11... | collective-permute-start | bytes 49160 | tf_op jit(solution)/shard_map/ppermute | solution.py:51
  30.5 4.1 %collective-permute-start.15 = (bf16[4,5120]{1,0:T(4,128)(2,1)S(1)}, bf16[4,5120]{1,0:T(4,128)(2,1)S(1)}, u32[]{:S(2)}, u32[]{:S(2)}) collective-permute-start(bf16[4,5120]{1,0:T(4,128)(2,1)S(1)} %residual_gradient.1.refs_4_.refs_0_), channel_id=1, source_target_pairs={{0,2},{2,0},{4,6},{6,4},{8,10},{10,8},{12,14},{14,12},{1,3},{3,1},... | collective-permute-start | bytes 122888 | tf_op jit(solution)/shard_map/ppermute | solution.py:52
  31.4 4.9 %collective-permute-start.14 = (bf16[4,5120]{1,0:T(4,128)(2,1)S(1)}, bf16[4,5120]{1,0:T(4,128)(2,1)S(1)}, u32[]{:S(2)}, u32[]{:S(2)}) collective-permute-start(bf16[4,5120]{1,0:T(4,128)(2,1)S(1)} %residual_gradient.1.refs_4_.refs_0_), channel_id=1, source_target_pairs={{0,6},{2,4},{4,2},{6,0},{8,14},{10,12},{12,10},{14,8},{1,7},{3,5},... | collective-permute-start | bytes 122888 | tf_op jit(solution)/shard_map/ppermute | solution.py:52
  32.5 4.0 %collective-permute-start.13 = (bf16[4,5120]{1,0:T(4,128)(2,1)S(1)}, bf16[4,5120]{1,0:T(4,128)(2,1)S(1)}, u32[]{:S(2)}, u32[]{:S(2)}) collective-permute-start(bf16[4,5120]{1,0:T(4,128)(2,1)S(1)} %residual_gradient.1.refs_4_.refs_0_), channel_id=1, source_target_pairs={{0,4},{2,6},{4,0},{6,2},{8,12},{10,14},{12,8},{14,10},{1,5},{3,7},... | collective-permute-start | bytes 122888 | tf_op jit(solution)/shard_map/ppermute | solution.py:52
  36.5 2.2 %collective-permute-start.16 = (bf16[16,5120]{1,0:T(8,128)(2,1)S(1)}, bf16[16,5120]{1,0:T(8,128)(2,1)S(1)}, u32[]{:S(2)}, u32[]{:S(2)}) collective-permute-start(bf16[16,5120]{1,0:T(8,128)(2,1)S(1)} %stack.5.refs_0_.refs_2_), channel_id=1, source_target_pairs={{0,1},{1,0},{2,3},{3,2},{4,5},{5,4},{6,7},{7,6},{8,9},{9,8},{10,11... | collective-permute-start | bytes 491528 | tf_op jit(solution)/shard_map/ppermute | solution.py:51
  38.2 1.4 %collective-permute-start.17 = (f32[1,5248]{1,0:T(1,128)S(1)}, f32[1,5248]{1,0:T(1,128)S(1)}, u32[]{:S(2)}, u32[]{:S(2)}) collective-permute-start(f32[1,5248]{1,0:T(1,128)S(1)} %bias_product.1.refs_4_.refs_0_), channel_id=1, source_target_pairs={{0,1},{1,0},{2,3},{3,2},{4,5},{5,4},{6,7},{7,6},{8,9},{9,8},{10,11... | collective-permute-start | bytes 62984 | tf_op jit(solution)/shard_map/ppermute | solution.py:51
  39.7 5.5 %collective-permute-start.20 = (f32[1,5248]{1,0:T(1,128)S(1)}, f32[1,5248]{1,0:T(1,128)S(1)}, u32[]{:S(2)}, u32[]{:S(2)}) collective-permute-start(f32[1,5248]{1,0:T(1,128)S(1)} %add.2.refs_9_.refs_0_), channel_id=1, source_target_pairs={{0,2},{2,0},{4,6},{6,4},{8,10},{10,8},{12,14},{14,12},{1,3},{3,1},... | collective-permute-start | bytes 62984 | tf_op jit(solution)/shard_map/ppermute | solution.py:52
  40.7 4.8 %collective-permute-start.19 = (f32[1,5248]{1,0:T(1,128)S(1)}, f32[1,5248]{1,0:T(1,128)S(1)}, u32[]{:S(2)}, u32[]{:S(2)}) collective-permute-start(f32[1,5248]{1,0:T(1,128)S(1)} %add.2.refs_9_.refs_0_), channel_id=1, source_target_pairs={{0,6},{2,4},{4,2},{6,0},{8,14},{10,12},{12,10},{14,8},{1,7},{3,5},... | collective-permute-start | bytes 62984 | tf_op jit(solution)/shard_map/ppermute | solution.py:52
  42.8 3.8 %collective-permute-start.18 = (f32[1,5248]{1,0:T(1,128)S(1)}, f32[1,5248]{1,0:T(1,128)S(1)}, u32[]{:S(2)}, u32[]{:S(2)}) collective-permute-start(f32[1,5248]{1,0:T(1,128)S(1)} %add.2.refs_9_.refs_0_), channel_id=1, source_target_pairs={{0,4},{2,6},{4,0},{6,2},{8,12},{10,14},{12,8},{14,10},{1,5},{3,7},... | collective-permute-start | bytes 62984 | tf_op jit(solution)/shard_map/ppermute | solution.py:52
  46.6 4.8 %collective-permute-start.21 = (f32[1,5248]{1,0:T(1,128)S(1)}, f32[1,5248]{1,0:T(1,128)S(1)}, u32[]{:S(2)}, u32[]{:S(2)}) collective-permute-start(f32[1,5248]{1,0:T(1,128)S(1)} %add.3.refs_2_.terms_ref), channel_id=1, source_target_pairs={{0,8},{2,10},{4,12},{6,14},{8,0},{10,2},{12,4},{14,6},{1,9},{3,11}... | collective-permute-start | bytes 62984 | tf_op jit(solution)/shard_map/ppermute | solution.py:52
